TPU v7x, 128 devices: a whole 4x4x4 slice. The times are simulated.
128 devices in a mesh: enc: 16 (over z, y), dom: 8 (over x, core).
Axes of the slice: x: 4, y: 4, z: 4, core: 2. Of those that a mesh axis runs over, the one named last changes fastest.
Arguments:
- token_states: bfloat16 [131072, 1024], P(('enc', 'dom')), may hold values from -6 to 6
- token_nodes: int32 [128, 1024], P(('enc', 'dom')), may hold values from 0 to 191, never falling along the last dimension, each value on 1 to 21 neighbouring positions
- expand_weight: bfloat16 [1024, 4096], replicated, may hold values from -0.1875 to 0.1875
- contract_weight: bfloat16 [4096, 1024], replicated, may hold values from -0.09375 to 0.09375
- node_owner: int32 [24576, 1], P(('enc', 'dom')), may hold values from 0 to 127; in each aligned block of 192 rows (0 to 191, 192 to 383, ...) at most 2 rows name the same one
- tile_columns: int32 [128, 2, 3], P(('enc', 'dom')), may hold values from 0 to 3, as said below
- tile_count: int32 [128, 2], P(('enc', 'dom')), may hold values from 1 to 3
- tile_values: bfloat16 [128, 2, 3, 128, 128], P(('enc', 'dom')), may hold values from -1.5 to 1.5
- first_weight: bfloat16 [1024, 1024], replicated, may hold values from -0.1875 to 0.1875
- second_weight: bfloat16 [1024, 1024], replicated, may hold values from -0.1875 to 0.1875
- output_cotangent: bfloat16 [32768, 1024], P(('enc', 'dom')), may hold values from -1.1953125 to 1.1953125
Outputs:
- graph_output: bfloat16 [32768, 1024], P(('enc', 'dom'))
- node_grads: bfloat16 [24576, 1024], P(('enc', 'dom'))
Inputs may be any that keep to these rules, and one draw needn't show every extreme that they name: `token_nodes`: each row lists one device's 1024 tokens by node, in order: node numbers never fall and each of the 192 nodes has 1 to 21 tokens. `node_owner`: among the nodes of one device, at most 2 have the same owner. `tile_columns`: the entries of row tile r are distinct and lie among r, r + 1 and r + 2; column tile 0 is the left owner's last 128 slots, the tiles after it are the owner's own, and the last column tile, one past the owner's own, is the right owner's first 128 slots. Only the first tile_count entries are used.
All inputs are finite; a program needn't handle non-finite values.
Results may differ from a plain program's by a relative error of at most 0.014.
Values may be sent and summed in bfloat16 or wider, within the bound.
No kernel may reach another device: no remote copies, remote signals or barrier semaphores. Data moves between devices by JAX's collectives and lax.ppermute only.
A program may use at most 128 MiB of HBM per device.

v0:
```python
import jax
import jax.numpy as jnp
from jax import lax
from jax.sharding import PartitionSpec as P

NODE_DEV = 192
SLOTS = 256
TILE = 128


norm_eps = 1e-07


def extended_2(x, sides, width):
    for axis, dim in sides:
        devices, length = (lax.axis_size(axis), x.shape[dim])
        up = [(i, (i + 1) % devices) for i in range(devices - 1)]
        down = [(j, i) for i, j in up]
        last = lax.slice_in_dim(x, length - width, length, axis=dim)
        initial = lax.slice_in_dim(x, 0, width, axis=dim)
        before = lax.ppermute(last, axis, up)
        after = lax.ppermute(initial, axis, down)
        x = jnp.concatenate([before, x, after], axis=dim)
    return x


def activate(values):
    return jax.nn.gelu(values, approximate=False)


def transposed_product(left_rows, right_matrix):
    return lax.dot_general(
        left_rows, right_matrix, (((1,), (1,)), ((), ())), preferred_element_type=jnp.float32
    )


def encode(states_rows, node_ids, expand_weight, contract_weight):
    hidden = jnp.dot(states_rows, expand_weight, preferred_element_type=jnp.float32)
    hidden = activate(hidden).astype(jnp.bfloat16)
    mixed = states_rows.astype(jnp.float32) + jnp.dot(
        hidden, contract_weight, preferred_element_type=jnp.float32
    )
    average = jnp.mean(mixed, axis=1, keepdims=True)
    centred = mixed - average
    variance = jnp.mean(centred * centred, axis=1, keepdims=True)
    normed = (centred * lax.rsqrt(variance + norm_eps)).astype(jnp.bfloat16)
    member = node_ids[None, :] == jnp.arange(NODE_DEV, dtype=jnp.int32)[:, None]
    summed = jnp.dot(member.astype(jnp.bfloat16), normed, preferred_element_type=jnp.float32)
    counts = jnp.sum(member.astype(jnp.float32), axis=1, keepdims=True)
    return (summed / counts).astype(jnp.bfloat16)


def placement(owners, capacity):
    order = jnp.arange(owners.shape[0], dtype=jnp.int32)
    earlier = (owners[:, None] == owners[None, :]) & (order[None, :] < order[:, None])
    ranking = jnp.sum(earlier.astype(jnp.int32), axis=1)
    position = owners * capacity + ranking
    return (jnp.arange(SLOTS, dtype=jnp.int32)[:, None] == position[None, :]).astype(jnp.bfloat16)


def aggregate(extended, columns, counts, values):
    tile_rows = values.shape[2]
    outputs = []
    for row_tile in range(values.shape[0]):
        running = jnp.zeros((tile_rows, extended.shape[1]), jnp.float32)
        for slot_index in range(values.shape[1]):
            start = columns[row_tile, slot_index] * tile_rows
            column_block = lax.dynamic_slice_in_dim(extended, start, tile_rows, 0)
            active = (slot_index < counts[row_tile]).astype(jnp.float32)
            running = running + active * jnp.dot(
                values[row_tile, slot_index], column_block, preferred_element_type=jnp.float32
            )
        outputs.append(running)
    return jnp.concatenate(outputs, axis=0)


def spread_back(grad_rows, columns, counts, values):
    tile_rows = values.shape[2]
    row_tiles = values.shape[0]
    extended = jnp.zeros(((row_tiles + 2) * tile_rows, grad_rows.shape[1]), jnp.float32)
    for row_tile in range(row_tiles):
        grad_block = grad_rows[row_tile * tile_rows : (row_tile + 1) * tile_rows]
        for slot_index in range(values.shape[1]):
            start = columns[row_tile, slot_index] * tile_rows
            active = (slot_index < counts[row_tile]).astype(jnp.float32)
            contrib = active * lax.dot_general(
                values[row_tile, slot_index],
                grad_block,
                (((0,), (0,)), ((), ())),
                preferred_element_type=jnp.float32,
            )
            current = lax.dynamic_slice_in_dim(extended, start, tile_rows, 0)
            extended = lax.dynamic_update_slice_in_dim(extended, current + contrib, start, 0)
    return extended


def widen(vertex_rows):
    return extended_2(vertex_rows, (("dom", 0),), TILE)


def collect(extended):
    slot_total = extended.shape[0] - 2 * TILE
    rims = jnp.concatenate([extended[:TILE], extended[TILE + slot_total :]], axis=0).astype(
        jnp.bfloat16
    )
    arrived = extended_2(rims, (("dom", 0),), TILE)
    interior = extended[TILE : TILE + slot_total]
    interior = interior.at[:TILE].add(arrived[:TILE].astype(jnp.float32))
    interior = interior.at[slot_total - TILE :].add(arrived[3 * TILE :].astype(jnp.float32))
    return interior


def local(
    token_states,
    token_nodes,
    expand_weight,
    contract_weight,
    node_owner,
    tile_columns,
    tile_count,
    tile_values,
    first_weight,
    second_weight,
    output_cotangent,
):
    enc_count = lax.axis_size("enc")
    dom_count = lax.axis_size("dom")
    devices = enc_count * dom_count
    capacity = SLOTS // devices
    features = token_states.shape[1]
    columns = tile_columns[0]
    counts = tile_count[0]
    values = tile_values[0]
    embeds = encode(token_states, token_nodes[0], expand_weight, contract_weight)
    onehot = placement(node_owner[:, 0], capacity)
    outgoing = jnp.dot(onehot, embeds, preferred_element_type=jnp.float32).astype(jnp.bfloat16)
    arrived = lax.all_to_all(
        outgoing.reshape(devices, capacity, features),
        ("enc", "dom"),
        split_axis=0,
        concat_axis=0,
        tiled=True,
    )
    vertex_rows = arrived.reshape(SLOTS, features)
    first_mix = aggregate(widen(vertex_rows), columns, counts, values).astype(jnp.bfloat16)
    first_pre = jnp.dot(first_mix, first_weight, preferred_element_type=jnp.float32)
    first_act = activate(first_pre).astype(jnp.bfloat16)
    second_mix = aggregate(widen(first_act), columns, counts, values).astype(jnp.bfloat16)
    graph_output = jnp.dot(second_mix, second_weight, preferred_element_type=jnp.float32).astype(
        jnp.bfloat16
    )
    grad_second_mix = transposed_product(output_cotangent, second_weight).astype(jnp.bfloat16)
    grad_first_act = collect(spread_back(grad_second_mix, columns, counts, values))
    derivative = jax.vjp(activate, first_pre)[1]
    grad_first_pre = derivative(grad_first_act)[0].astype(jnp.bfloat16)
    grad_first_mix = transposed_product(grad_first_pre, first_weight).astype(jnp.bfloat16)
    grad_vertex = collect(spread_back(grad_first_mix, columns, counts, values)).astype(jnp.bfloat16)
    returned = lax.all_to_all(
        grad_vertex.reshape(devices, capacity, features),
        ("enc", "dom"),
        split_axis=0,
        concat_axis=0,
        tiled=True,
    )
    returned = returned.reshape(SLOTS, features)
    node_grads = lax.dot_general(
        onehot, returned, (((0,), (0,)), ((), ())), preferred_element_type=jnp.float32
    ).astype(jnp.bfloat16)
    return (graph_output, node_grads)


def solution(mesh):
    placed = (
        P(("enc", "dom"), None),
        P(("enc", "dom"), None),
        P(),
        P(),
        P(("enc", "dom"), None),
        P(("enc", "dom"), None, None),
        P(("enc", "dom"), None),
        P(("enc", "dom"), None, None, None, None),
        P(),
        P(),
        P(("enc", "dom"), None),
    )
    return jax.shard_map(
        local,
        mesh=mesh,
        in_specs=placed,
        out_specs=(P(("enc", "dom"), None), P(("enc", "dom"), None)),
        check_vma=False,
    )
```

profile of v0, /device:TPU:1, one launch (start us, length us, event | category | flops | bytes accessed | tf_op | source)
XLA Modules:
  0.0 187.5 jit_solution(12748780001091704142)
XLA Ops:
  0.6 4.1 %copy.20 = bf16[1024,1024]{0,1:T(8,128)(2,1)} copy(bf16[1024,1024]{1,0:T(8,128)(2,1)} %param.19) | data formatting | bytes 4194304 | tf_op args[0]
  4.8 47.0 %fusion.13.clone.4 = bf16[1024,4096]{1,0:T(8,128)(2,1)} fusion(bf16[1024,1024]{1,0:T(8,128)(2,1)} %param.19, bf16[1024,4096]{1,0:T(8,128)(2,1)} %param.21), kind=kOutput, calls=%fused_computation.3.clone.clone.clone.clone.clone.clone.1 | convolution fusion | flops 8862564352 | bytes 18874368 | tf_op jit(solution)/shard_map/dot_general | solution.py:38
  51.8 14.1 %fusion.173 = (f32[1024]{0:T(1024)S(1)}, f32[1024,1024]{0,1:T(8,128)S(1)}) fusion(bf16[4096,1024]{1,0:T(8,128)(2,1)} %param.22, bf16[1024,1024]{0,1:T(8,128)(2,1)} %copy.20, bf16[1024,4096]{1,0:T(8,128)(2,1)} %fusion.13.clone.4), kind=kOutput, calls=%fused_computation.242 | convolution fusion | flops 8593079296 | bytes 23072768 | tf_op jit(solution)/shard_map/dot_general | solution.py:40
  68.8 3.3 %convolution_convert_fusion.3 = bf16[256,1024]{1,0:T(8,128)(2,1)S(1)} fusion(f32[1024,1024]{0,1:T(8,128)} %copy-done.1, f32[1024]{0:T(1024)S(1)} %add_rsqrt_fusion, f32[1024]{0:T(1024)S(1)} %broadcast_multiply_fusion, f32[192]{0:T(256)S(1)} %convert_reduce_fusion, s32[1024]{0:T(1024)S(1)} %bitcast.173, s32[192]{0:T(256)S(1)} %multiply_add_fusion), kind=kOutput, calls=%fused_computation.30 | convolution fusion | flops 507363328 | bytes 4732416 | tf_op jit(solution)/shard_map/dot_general | solution.py:136
  73.1 11.5 %all-to-all-start = ((bf16[128,2,1024]{2,1,0:T(2,128)(2,1)}), bf16[128,2,1024]{2,1,0:T(2,128)(2,1)S(1)}, u32[]{:S(2)}, u32[]{:S(2)}) async-start(bf16[128,2,1024]{2,1,0:T(2,128)(2,1)} %reshape.175), calls=%async_computation | async-start | bytes 1048576 | tf_op jit(solution)/shard_map/all_to_all | solution.py:137
  92.4 2.5 %convolution_convert_fusion.1 = bf16[256,1024]{1,0:T(8,128)(2,1)S(1)} fusion(bf16[256,1024]{1,0:T(8,128)(2,1)} %param.29, bf16[1024,1024]{1,0:T(8,128)(2,1)} %param.28), kind=kOutput, calls=%fused_computation.28 | convolution fusion | flops 537133056 | bytes 3145728 | tf_op jit(solution)/shard_map/dot_general | solution.py:32
  97.6 2.1 %fusion.32 = f32[512,1024]{1,0:T(8,128)} fusion(f32[512,1024]{1,0:T(8,128)} %fusion.30, s32[]{:T(128)S(6)} %select_n.13, f32[]{:T(128)} %bitcast.7, bf16[256,1024]{1,0:T(8,128)(2,1)S(1)} %convolution_convert_fusion.1, bf16[2,3,128,128]{3,2,1,0:T(8,128)(2,1)S(1)} %bitcast.146), kind=kOutput, calls=%fused_computation.71 | convolution fusion | flops 33816576 | bytes 1344004 | tf_op jit(solution)/shard_map/dot_general | solution.py:86
  99.7 2.1 %fusion.34 = f32[512,1024]{1,0:T(8,128)} fusion(f32[512,1024]{1,0:T(8,128)} %fusion.32, s32[]{:T(128)S(6)} %select_n.14, f32[]{:T(128)} %bitcast.10, bf16[256,1024]{1,0:T(8,128)(2,1)S(1)} %convolution_convert_fusion.1, bf16[2,3,128,128]{3,2,1,0:T(8,128)(2,1)S(1)} %bitcast.147), kind=kOutput, calls=%fused_computation.73 | convolution fusion | flops 33816576 | bytes 1344004 | tf_op jit(solution)/shard_map/dot_general | solution.py:86
  101.8 2.1 %fusion.36 = f32[512,1024]{1,0:T(8,128)} fusion(f32[512,1024]{1,0:T(8,128)} %fusion.34, s32[]{:T(128)S(6)} %select_n.15, f32[]{:T(128)} %bitcast.14, bf16[256,1024]{1,0:T(8,128)(2,1)S(1)} %convolution_convert_fusion.1, bf16[2,3,128,128]{3,2,1,0:T(8,128)(2,1)S(1)} %bitcast.148), kind=kOutput, calls=%fused_computation.75 | convolution fusion | flops 33816576 | bytes 1344004 | tf_op jit(solution)/shard_map/dot_general | solution.py:86
  103.9 2.1 %fusion.38 = f32[512,1024]{1,0:T(8,128)} fusion(f32[512,1024]{1,0:T(8,128)} %fusion.36, s32[]{:T(128)S(6)} %select_n.16, f32[]{:T(128)} %bitcast.17, bf16[256,1024]{1,0:T(8,128)(2,1)S(1)} %convolution_convert_fusion.1, bf16[2,3,128,128]{3,2,1,0:T(8,128)(2,1)S(1)} %bitcast.149), kind=kOutput, calls=%fused_computation.77 | convolution fusion | flops 33816576 | bytes 1344004 | tf_op jit(solution)/shard_map/dot_general | solution.py:86
  107.4 2.1 %fusion.40 = f32[512,1024]{1,0:T(8,128)} fusion(f32[512,1024]{1,0:T(8,128)} %fusion.38, s32[]{:T(128)S(6)} %select_n.17, f32[]{:T(128)} %bitcast.20, bf16[256,1024]{1,0:T(8,128)(2,1)S(1)} %convolution_convert_fusion.1, bf16[2,3,128,128]{3,2,1,0:T(8,128)(2,1)S(1)} %bitcast.150), kind=kOutput, calls=%fused_computation.79 | convolution fusion | flops 33816576 | bytes 1344004 | tf_op jit(solution)/shard_map/dot_general | solution.py:86
  112.1 3.5 %collective-permute-start.4 = (bf16[128,1024]{1,0:T(8,128)(2,1)}, bf16[128,1024]{1,0:T(8,128)(2,1)}, u32[]{:S(2)}, u32[]{:S(2)}) collective-permute-start(bf16[128,1024]{1,0:T(8,128)(2,1)} %get-tuple-element.55), channel_id=1, source_target_pairs={{0,1},{1,2},{2,3},{3,4},{4,5},{5,6},{6,7},{8,9},{9,10},{10,11},{11... | collective-permute-start | bytes 786440 | tf_op jit(solution)/shard_map/ppermute | solution.py:21
  117.6 2.3 %slice.282 = f32[256,1024]{1,0:T(8,128)} slice(f32[512,1024]{1,0:T(8,128)} %fusion.40), slice={[128:384], [0:1024]} | slice | bytes 2097152 | tf_op jit(solution)/shard_map/slice | solution.py:107
  121.1 3.6 %collective-permute-start = (bf16[128,1024]{1,0:T(8,128)(2,1)}, bf16[128,1024]{1,0:T(8,128)(2,1)}, u32[]{:S(2)}, u32[]{:S(2)}) collective-permute-start(bf16[128,1024]{1,0:T(8,128)(2,1)} %slice.238), channel_id=1, source_target_pairs={{0,1},{1,2},{2,3},{3,4},{4,5},{5,6},{6,7},{8,9},{9,10},{10,11},{11... | collective-permute-start | bytes 786440 | tf_op jit(solution)/shard_map/ppermute | solution.py:21
  124.7 2.0 %fusion.78 = f32[256,1024]{1,0:T(8,128)} fusion(f32[256,1024]{1,0:T(8,128)} %slice.282, f32[512,1024]{1,0:T(8,128)} %fusion.40, bf16[128,1024]{1,0:T(8,128)(2,1)} %collective-permute-done.4), kind=kLoop, calls=%fused_computation.134 | loop fusion | flops 262144 | bytes 1310720 | tf_op jit(solution)/shard_map/scatter-add | solution.py:108
  129.4 2.0 %fusion.77 = f32[256,1024]{1,0:T(8,128)} fusion(f32[256,1024]{1,0:T(8,128)} %fusion.78, bf16[128,1024]{1,0:T(8,128)(2,1)} %collective-permute-done.5), kind=kLoop, calls=%fused_computation.132 | loop fusion | flops 262144 | bytes 1310720 | tf_op jit(solution)/shard_map/scatter-add | solution.py:109
  132.6 2.9 %collective-permute-done.1 = bf16[128,1024]{1,0:T(8,128)(2,1)} collective-permute-done((bf16[128,1024]{1,0:T(8,128)(2,1)}, bf16[128,1024]{1,0:T(8,128)(2,1)}, u32[]{:S(2)}, u32[]{:S(2)}) %collective-permute-start.1) | collective-permute-done | bytes 262176 | tf_op jit(solution)/shard_map/ppermute | solution.py:22
  137.9 2.8 %multiply_convert_fusion.8 = (bf16[256,1024]{1,0:T(8,128)(2,1)S(1)}, f32[256,1024]{1,0:T(8,128)S(1)}, f32[256,1024]{1,0:T(8,128)S(1)}) fusion(bf16[1024,1024]{1,0:T(8,128)(2,1)S(1)} %copy-done, bf16[128,1024]{1,0:T(8,128)(2,1)S(1)} %fusion.66, bf16[128,1024]{1,0:T(8,128)(2,1)S(1)} %fusion.65), kind=kOutput, calls=%fused_computation.111 | convolution fusion | flops 554958848 | bytes 5242880 | tf_op jit(solution)/shard_map/dot_general | solution.py:146
  142.7 3.6 %collective-permute-start.2 = (bf16[128,1024]{1,0:T(8,128)(2,1)S(1)}, bf16[128,1024]{1,0:T(8,128)(2,1)S(1)}, u32[]{:S(2)}, u32[]{:S(2)}) collective-permute-start(bf16[128,1024]{1,0:T(8,128)(2,1)S(1)} %get-tuple-element.56), channel_id=1, source_target_pairs={{0,1},{1,2},{2,3},{3,4},{4,5},{5,6},{6,7},{8,9},{9,10},{10,11},{11... | collective-permute-start | bytes 786440 | tf_op jit(solution)/shard_map/ppermute | solution.py:21
  151.6 2.4 %collective-permute-start.7 = (bf16[128,1024]{1,0:T(8,128)(2,1)S(1)}, bf16[128,1024]{1,0:T(8,128)(2,1)S(1)}, u32[]{:S(2)}, u32[]{:S(2)}) collective-permute-start(bf16[128,1024]{1,0:T(8,128)(2,1)S(1)} %get-tuple-element.52), channel_id=1, source_target_pairs={{1,0},{2,1},{3,2},{4,3},{5,4},{6,5},{7,6},{9,8},{10,9},{11,10},{12... | collective-permute-start | bytes 786440 | tf_op jit(solution)/shard_map/ppermute | solution.py:22
  160.3 2.1 %reshape.177 = bf16[128,2,1024]{2,1,0:T(2,128)(2,1)} reshape(bf16[256,1024]{1,0:T(8,128)(2,1)} %convert_element_type.142) | data formatting | bytes 1048576 | tf_op jit(solution)/shard_map/reshape | solution.py:159
  162.3 9.5 %all-to-all-start.1 = ((bf16[128,2,1024]{2,1,0:T(2,128)(2,1)}), bf16[128,2,1024]{2,1,0:T(2,128)(2,1)}, u32[]{:S(2)}, u32[]{:S(2)}) async-start(bf16[128,2,1024]{2,1,0:T(2,128)(2,1)} %reshape.177), calls=%async_computation.1 | async-start | bytes 1048576 | tf_op jit(solution)/shard_map/all_to_all | solution.py:158
  174.7 3.1 %convolution_convert_fusion.2 = bf16[256,1024]{1,0:T(8,128)(2,1)} fusion(bf16[1024,1024]{1,0:T(8,128)(2,1)} %param.28, bf16[128,1024]{1,0:T(8,128)(2,1)S(1)} %fusion.68, bf16[128,1024]{1,0:T(8,128)(2,1)S(1)} %fusion.67), kind=kOutput, calls=%fused_computation.29 | convolution fusion | flops 538181632 | bytes 3145728 | tf_op jit(solution)/shard_map/dot_general | solution.py:149
  177.8 7.4 %all-to-all-done.1 = bf16[128,2,1024]{2,1,0:T(2,128)(2,1)} async-done(((bf16[128,2,1024]{2,1,0:T(2,128)(2,1)}), bf16[128,2,1024]{2,1,0:T(2,128)(2,1)}, u32[]{:S(2)}, u32[]{:S(2)}) %all-to-all-start.1) | async-done | bytes 524320 | tf_op jit(solution)/shard_map/all_to_all | solution.py:158
  (78 shorter events, 38.2 us)
Async XLA Ops:
  0.6 137.3 %copy-start = (bf16[1024,1024]{1,0:T(8,128)(2,1)S(1)}, bf16[1024,1024]{1,0:T(8,128)(2,1)}, u32[]{:S(2)}) copy-start(bf16[1024,1024]{1,0:T(8,128)(2,1)} %param.27) | copy-start | bytes 6291460
  51.8 16.6 %copy-start.6 = (s32[1,1024]{1,0:T(1,128)S(1)}, s32[1,1024]{1,0:T(1,128)}, u32[]{:S(2)}) copy-start(s32[1,1024]{1,0:T(1,128)} %param.20) | copy-start | bytes 12292
  51.8 16.8 %copy-start.4 = (s32[192,1]{0,1:T(1,128)S(1)}, s32[192,1]{0,1:T(1,128)}, u32[]{:S(2)}) copy-start(s32[192,1]{0,1:T(1,128)} %param.23) | copy-start | bytes 2308
  66.0 2.0 %copy-start.1 = (f32[1024,1024]{0,1:T(8,128)}, f32[1024,1024]{0,1:T(8,128)S(1)}, u32[]{:S(2)}) copy-start(f32[1024,1024]{0,1:T(8,128)S(1)} %get-tuple-element.69) | copy-start | bytes 12582916
  66.0 18.6 %copy-start.5 = (s32[1,2,3]{2,1,0:T(2,128)S(1)}, s32[1,2,3]{2,1,0:T(2,128)}, u32[]{:S(2)}) copy-start(s32[1,2,3]{2,1,0:T(2,128)} %param.24) | copy-start | bytes 76
  66.0 22.4 %copy-start.7 = (s32[1,2]{1,0:T(1,128)S(1)}, s32[1,2]{1,0:T(1,128)}, u32[]{:S(2)}) copy-start(s32[1,2]{1,0:T(1,128)} %param.25) | copy-start | bytes 28
  67.9 28.6 %copy-start.2 = (bf16[1,2,3,128,128]{4,3,2,1,0:T(8,128)(2,1)S(1)}, bf16[1,2,3,128,128]{4,3,2,1,0:T(8,128)(2,1)}, u32[]{:S(2)}) copy-start(bf16[1,2,3,128,128]{4,3,2,1,0:T(8,128)(2,1)} %param.26) | copy-start | bytes 589828
  73.1 46.9 %all-to-all-start = ((bf16[128,2,1024]{2,1,0:T(2,128)(2,1)}), bf16[128,2,1024]{2,1,0:T(2,128)(2,1)S(1)}, u32[]{:S(2)}, u32[]{:S(2)}) async-start(bf16[128,2,1024]{2,1,0:T(2,128)(2,1)} %reshape.175), calls=%async_computation | async-start | bytes 1048576 | tf_op jit(solution)/shard_map/all_to_all | solution.py:137
  112.1 12.6 %collective-permute-start.4 = (bf16[128,1024]{1,0:T(8,128)(2,1)}, bf16[128,1024]{1,0:T(8,128)(2,1)}, u32[]{:S(2)}, u32[]{:S(2)}) collective-permute-start(bf16[128,1024]{1,0:T(8,128)(2,1)} %get-tuple-element.55), channel_id=1, source_target_pairs={{0,1},{1,2},{2,3},{3,4},{4,5},{5,6},{6,7},{8,9},{9,10},{10,11},{11... | collective-permute-start | bytes 786440 | tf_op jit(solution)/shard_map/ppermute | solution.py:21
  115.7 13.8 %collective-permute-start.5 = (bf16[128,1024]{1,0:T(8,128)(2,1)}, bf16[128,1024]{1,0:T(8,128)(2,1)}, u32[]{:S(2)}, u32[]{:S(2)}) collective-permute-start(bf16[128,1024]{1,0:T(8,128)(2,1)} %get-tuple-element.54), channel_id=1, source_target_pairs={{1,0},{2,1},{3,2},{4,3},{5,4},{6,5},{7,6},{9,8},{10,9},{11,10},{12... | collective-permute-start | bytes 786440 | tf_op jit(solution)/shard_map/ppermute | solution.py:22
  121.1 10.6 %collective-permute-start = (bf16[128,1024]{1,0:T(8,128)(2,1)}, bf16[128,1024]{1,0:T(8,128)(2,1)}, u32[]{:S(2)}, u32[]{:S(2)}) collective-permute-start(bf16[128,1024]{1,0:T(8,128)(2,1)} %slice.238), channel_id=1, source_target_pairs={{0,1},{1,2},{2,3},{3,4},{4,5},{5,6},{6,7},{8,9},{9,10},{10,11},{11... | collective-permute-start | bytes 786440 | tf_op jit(solution)/shard_map/ppermute | solution.py:21
  127.5 8.0 %collective-permute-start.1 = (bf16[128,1024]{1,0:T(8,128)(2,1)}, bf16[128,1024]{1,0:T(8,128)(2,1)}, u32[]{:S(2)}, u32[]{:S(2)}) collective-permute-start(bf16[128,1024]{1,0:T(8,128)(2,1)} %slice.240), channel_id=1, source_target_pairs={{1,0},{2,1},{3,2},{4,3},{5,4},{6,5},{7,6},{9,8},{10,9},{11,10},{12... | collective-permute-start | bytes 786440 | tf_op jit(solution)/shard_map/ppermute | solution.py:22
  137.9 8.5 %copy-start.3 = (f32[256,1024]{1,0:T(8,128)S(1)}, f32[256,1024]{1,0:T(8,128)}, u32[]{:S(2)}) copy-start(f32[256,1024]{1,0:T(8,128)} %fusion.77) | copy-start | bytes 3145732
  140.8 13.2 %collective-permute-start.3 = (bf16[128,1024]{1,0:T(8,128)(2,1)S(1)}, bf16[128,1024]{1,0:T(8,128)(2,1)S(1)}, u32[]{:S(2)}, u32[]{:S(2)}) collective-permute-start(bf16[128,1024]{1,0:T(8,128)(2,1)S(1)} %get-tuple-element.57), channel_id=1, source_target_pairs={{1,0},{2,1},{3,2},{4,3},{5,4},{6,5},{7,6},{9,8},{10,9},{11,10},{12... | collective-permute-start | bytes 786440 | tf_op jit(solution)/shard_map/ppermute | solution.py:22
  142.7 11.3 %collective-permute-start.2 = (bf16[128,1024]{1,0:T(8,128)(2,1)S(1)}, bf16[128,1024]{1,0:T(8,128)(2,1)S(1)}, u32[]{:S(2)}, u32[]{:S(2)}) collective-permute-start(bf16[128,1024]{1,0:T(8,128)(2,1)S(1)} %get-tuple-element.56), channel_id=1, source_target_pairs={{0,1},{1,2},{2,3},{3,4},{4,5},{5,6},{6,7},{8,9},{9,10},{10,11},{11... | collective-permute-start | bytes 786440 | tf_op jit(solution)/shard_map/ppermute | solution.py:21
  149.6 8.6 %collective-permute-start.6 = (bf16[128,1024]{1,0:T(8,128)(2,1)S(1)}, bf16[128,1024]{1,0:T(8,128)(2,1)S(1)}, u32[]{:S(2)}, u32[]{:S(2)}) collective-permute-start(bf16[128,1024]{1,0:T(8,128)(2,1)S(1)} %get-tuple-element.53), channel_id=1, source_target_pairs={{0,1},{1,2},{2,3},{3,4},{4,5},{5,6},{6,7},{8,9},{9,10},{10,11},{11... | collective-permute-start | bytes 786440 | tf_op jit(solution)/shard_map/ppermute | solution.py:21
  151.6 7.7 %collective-permute-start.7 = (bf16[128,1024]{1,0:T(8,128)(2,1)S(1)}, bf16[128,1024]{1,0:T(8,128)(2,1)S(1)}, u32[]{:S(2)}, u32[]{:S(2)}) collective-permute-start(bf16[128,1024]{1,0:T(8,128)(2,1)S(1)} %get-tuple-element.52), channel_id=1, source_target_pairs={{1,0},{2,1},{3,2},{4,3},{5,4},{6,5},{7,6},{9,8},{10,9},{11,10},{12... | collective-permute-start | bytes 786440 | tf_op jit(solution)/shard_map/ppermute | solution.py:22
  162.3 22.9 %all-to-all-start.1 = ((bf16[128,2,1024]{2,1,0:T(2,128)(2,1)}), bf16[128,2,1024]{2,1,0:T(2,128)(2,1)}, u32[]{:S(2)}, u32[]{:S(2)}) async-start(bf16[128,2,1024]{2,1,0:T(2,128)(2,1)} %reshape.177), calls=%async_computation.1 | async-start | bytes 1048576 | tf_op jit(solution)/shard_map/all_to_all | solution.py:158
where the time goes:
time: 189 us; the launch traced here: 187 us
  matrix products  96.6 us (51%)
  starting transfers between devices  41.9 us (22%)
  local copies, waits for them, and re-layouts  21 us (11%)
  waiting for transfers between devices  11.3 us (6%)
  between operations  8.92 us (5%)
  other arithmetic  7.85 us (4%)
    dot_general x1, matrix products, encode(): jnp.dot(states_rows, expand_weight, preferred_element_type=jnp.float32)  47 us
    dot_general x1, matrix products, encode(): jnp.dot(hidden, contract_weight, preferred_element_type=jnp.float32)  14.1 us
    dot_general x12, matrix products, spread_back(): lax.dot_general(values[row_tile, slot_index], grad_block, (((0,), (0,)),...  13.3 us
    ppermute x4, starting transfers between devices, extended_2(): before = lax.ppermute(last, axis, up)  12.7 us
    all_to_all x1, starting transfers between devices, local(): lax.all_to_all(outgoing.reshape(devices, capacity, features), ('enc', 'do...  11.5 us
    all_to_all x1, starting transfers between devices, local(): lax.all_to_all(grad_vertex.reshape(devices, capacity, features), ('enc',...  9.49 us
    dot_general x12, matrix products, aggregate(): jnp.dot(values[row_tile, slot_index], column_block, preferred_element_typ...  8.3 us
    ppermute x4, starting transfers between devices, extended_2(): after = lax.ppermute(initial, axis, down)  8.17 us
  transfers between devices with their start and end apart: 10, of which 3 were waited for; matrix products, arithmetic and copies ran while one was open for 23% of the time, Pallas kernels for 0%

commit v1 on v0

v1 whole, which is shorter than its diff:
```python
import jax
import jax.numpy as jnp
from jax import lax
from jax.experimental import pallas as pl
from jax.experimental.pallas import tpu as pltpu
from jax.sharding import PartitionSpec as P

NODES = 192
NPAD = 256
TOKENS = 1024
D = 1024
FF = 4096
HALF = 512
PEERS = 128
GROUP = 8
ROWS = 1024
TILE = 128
SLOTS = 256

CHUNK = 512
CHUNKS = FF // CHUNK
BLOCK = 256
BLOCKS = TOKENS // BLOCK
AHEAD = 2

bf16 = jnp.bfloat16
f32 = jnp.float32
EPS = 1e-07
ROOT_HALF = 0.7071067811865476
INV_ROOT_TAU = 0.3989422804014327

ANY = pl.BlockSpec(memory_space=pl.ANY)
VMEM = pl.BlockSpec(memory_space=pltpu.VMEM)
SMEM = pl.BlockSpec(memory_space=pltpu.SMEM)


def dot(a, b):
    return jnp.dot(a, b, preferred_element_type=f32)


def dot_t(a, b):
    return lax.dot_general(a, b, (((1,), (1,)), ((), ())), preferred_element_type=f32)


def iota(shape, dim):
    return lax.broadcasted_iota(jnp.int32, shape, dim)


def params(mib):
    return pltpu.CompilerParams(vmem_limit_bytes=mib * 2**20)


def cost(flops, moved):
    return pl.CostEstimate(flops=flops, bytes_accessed=moved, transcendentals=0)


def encode_kernel(
    upper_ref,
    owner_ref,
    node_ref,
    states_hbm,
    expand_hbm,
    contract_hbm,
    out_ref,
    target_ref,
    states,
    expand,
    contract,
    total,
    hidden_a,
    hidden_b,
    owner_pad,
    route,
    member,
    normed,
    state_sem,
    expand_sem,
    contract_sem,
):
    def chunk_of(c):
        return pl.ds(pl.multiple_of(c * CHUNK, CHUNK), CHUNK)

    def start(c):
        pltpu.make_async_copy(
            expand_hbm.at[:, chunk_of(c)], expand.at[c], expand_sem.at[c]
        ).start()
        pltpu.make_async_copy(
            contract_hbm.at[chunk_of(c), :], contract.at[c], contract_sem.at[c]
        ).start()

    def wait(c):
        pltpu.make_async_copy(
            expand_hbm.at[:, chunk_of(c)], expand.at[c], expand_sem.at[c]
        ).wait()
        pltpu.make_async_copy(
            contract_hbm.at[chunk_of(c), :], contract.at[c], contract_sem.at[c]
        ).wait()

    state_copy = pltpu.make_async_copy(states_hbm, states, state_sem)
    state_copy.start()
    for c in range(AHEAD):
        start(c)

    owner_pad[...] = jnp.full((8, NPAD), -4096, jnp.int32)
    owner_pad[0:1, 0:NODES] = owner_ref[...]
    owner = owner_pad[0:1, :]
    named = jnp.where(iota((PEERS, NPAD), 0) == owner, 1.0, 0.0).astype(bf16)
    before = jnp.where(iota((NPAD, NPAD), 0) < iota((NPAD, NPAD), 1), 1.0, 0.0).astype(bf16)
    earlier = dot(named, before)
    rank = jnp.sum(named.astype(f32) * earlier, axis=0, keepdims=True).astype(jnp.int32)
    own_row = owner * 8 + rank
    upper = upper_ref[0]
    beside = owner + jnp.where(upper == 1, 1, -1)
    edge = jnp.where(upper == 1, GROUP - 1, 0)
    has_beside = (owner & (GROUP - 1)) != edge
    halo_row = jnp.where(has_beside, beside * 8 + 2 + rank, -4096)
    target_ref[...] = jnp.where(iota((8, NPAD), 0) == 0, own_row, halo_row)
    rows = iota((ROWS, NPAD), 0)
    for u in range(2):
        shifted = rows - 4 * u
        hit = (shifted == own_row) | (shifted == halo_row)
        route[:, u * NPAD : (u + 1) * NPAD] = jnp.where(hit, 1.0, 0.0).astype(bf16)
    mask = jnp.where(iota((NPAD, TOKENS), 0) == node_ref[...], 1.0, 0.0)
    member[...] = mask.astype(bf16)
    counts = jnp.maximum(jnp.sum(mask, axis=1, keepdims=True), 1.0)

    def block_of(m):
        return pl.ds(m * BLOCK, BLOCK)

    def first(c, m):
        return dot(states[block_of(m), :], expand[c])

    def second(c, m, values):
        acted = 0.5 * values * (1.0 + lax.erf(values * ROOT_HALF))
        total[block_of(m), :] += dot(acted.astype(bf16), contract[c])

    state_copy.wait()
    total[...] = states[...].astype(f32)
    wait(0)
    hidden_a[...] = first(0, 0)
    buffers = (hidden_a, hidden_b)

    def step(c, carry):
        @pl.when(c + AHEAD < CHUNKS)
        def _():
            start(c + AHEAD)

        @pl.when(c + 1 < CHUNKS)
        def _():
            wait(c + 1)

        for m in range(BLOCKS):
            now, later = buffers[m % 2], buffers[(m + 1) % 2]
            if m + 1 < BLOCKS:
                later[...] = first(c, m + 1)
            else:
                later[...] = first(jnp.minimum(c + 1, CHUNKS - 1), 0)
            second(c, m, now[...])
        return carry

    lax.fori_loop(0, CHUNKS, step, 0)

    for m in range(BLOCKS):
        mixed = total[block_of(m), :]
        centred = mixed - jnp.mean(mixed, axis=1, keepdims=True)
        variance = jnp.mean(centred * centred, axis=1, keepdims=True)
        normed[block_of(m), :] = (centred * lax.rsqrt(variance + EPS)).astype(bf16)
    embeds = (dot(member[...], normed[...]) / counts).astype(bf16)
    stacked = jnp.concatenate([embeds[:, :HALF], embeds[:, HALF:]], axis=0)
    out_ref[...] = dot(route[...], stacked).astype(bf16)


def encode(upper, owner, node_ids, states, expand_weight, contract_weight):
    dma = pltpu.SemaphoreType.DMA
    return pl.pallas_call(
        encode_kernel,
        out_shape=(
            jax.ShapeDtypeStruct((ROWS, HALF), bf16),
            jax.ShapeDtypeStruct((8, NPAD), jnp.int32),
        ),
        in_specs=[SMEM, VMEM, VMEM, ANY, ANY, ANY],
        out_specs=(VMEM, VMEM),
        scratch_shapes=[
            pltpu.VMEM((TOKENS, D), bf16),
            pltpu.VMEM((CHUNKS, D, CHUNK), bf16),
            pltpu.VMEM((CHUNKS, CHUNK, D), bf16),
            pltpu.VMEM((TOKENS, D), f32),
            pltpu.VMEM((BLOCK, CHUNK), f32),
            pltpu.VMEM((BLOCK, CHUNK), f32),
            pltpu.VMEM((8, NPAD), jnp.int32),
            pltpu.VMEM((ROWS, 2 * NPAD), bf16),
            pltpu.VMEM((NPAD, TOKENS), bf16),
            pltpu.VMEM((TOKENS, D), bf16),
            dma,
            dma((CHUNKS,)),
            dma((CHUNKS,)),
        ],
        compiler_params=params(56),
        cost_estimate=cost(4 * TOKENS * D * FF, 20 * 2**20),
        name="encode",
    )(upper, owner, node_ids, states, expand_weight, contract_weight)


def prepare_kernel(
    columns_ref,
    count_ref,
    values_ref,
    target_ref,
    cotangent_ref,
    weight_ref,
    mix_ref,
    mix_t_ref,
    band_ref,
    pick_ref,
    inner_ref,
    low_ref,
    high_ref,
    band_t,
):
    band_ref[...] = jnp.zeros((SLOTS, 2 * SLOTS), bf16)
    band_t[...] = jnp.zeros((2 * SLOTS, SLOTS), bf16)
    for r in range(2):
        for c in range(r, r + 3):
            tile = jnp.zeros((TILE, TILE), f32)
            for s in range(3):
                used = (s < count_ref[0, r]) & (columns_ref[0, r, s] == c)
                tile += jnp.where(used, 1.0, 0.0) * values_ref[0, r, s].astype(f32)
            band_ref[r * TILE : (r + 1) * TILE, c * TILE : (c + 1) * TILE] = tile.astype(bf16)
            band_t[c * TILE : (c + 1) * TILE, r * TILE : (r + 1) * TILE] = tile.T.astype(bf16)

    def place(column, u):
        peer, slot = column >> 3, column & 3
        halo = jnp.where(peer < PEERS // 2, 2 * SLOTS - TILE, -PEERS) + 2 * peer + slot - 2
        source = jnp.where(slot < 2, TILE + 2 * peer + slot, halo)
        return jnp.where(((column >> 2) & 1) == u, source, -1)

    shape = (2 * SLOTS, ROWS)
    for u in range(2):
        moved = jnp.where(iota(shape, 0) == place(iota((1, ROWS), 1), u), 1.0, 0.0)
        mix_ref[u * SLOTS : (u + 1) * SLOTS, :] = dot(band_ref[...], moved.astype(bf16)).astype(bf16)
        back = jnp.where(iota(shape[::-1], 1) == place(iota((ROWS, 1), 0), u), 1.0, 0.0)
        mix_t_ref[:, u * SLOTS : (u + 1) * SLOTS] = dot(back.astype(bf16), band_t[...]).astype(bf16)

    diagonal = iota((NODES, NPAD), 0) == iota((NODES, NPAD), 1)
    own_row = jnp.sum(jnp.where(diagonal, target_ref[0:1, :], 0), axis=1, keepdims=True)
    halo_row = jnp.sum(jnp.where(diagonal, target_ref[1:2, :], 0), axis=1, keepdims=True)
    lanes = iota((NODES, ROWS), 1)
    for u in range(2):
        hit = (lanes - 4 * u == own_row) | (lanes - 4 * u == halo_row)
        pick_ref[u * NODES : (u + 1) * NODES, :] = jnp.where(hit, 1.0, 0.0).astype(bf16)

    grad_mix = dot_t(cotangent_ref[...], weight_ref[...]).astype(bf16)
    spread = dot(band_t[...], grad_mix)
    low_ref[...] = spread[:TILE].astype(bf16)
    inner_ref[...] = spread[TILE : TILE + SLOTS]
    high_ref[...] = spread[TILE + SLOTS :].astype(bf16)


def prepare(columns, counts, values, target, cotangent, weight):
    return pl.pallas_call(
        prepare_kernel,
        out_shape=(
            jax.ShapeDtypeStruct((2 * SLOTS, ROWS), bf16),
            jax.ShapeDtypeStruct((ROWS, 2 * SLOTS), bf16),
            jax.ShapeDtypeStruct((SLOTS, 2 * SLOTS), bf16),
            jax.ShapeDtypeStruct((2 * NODES, ROWS), bf16),
            jax.ShapeDtypeStruct((SLOTS, D), f32),
            jax.ShapeDtypeStruct((TILE, D), bf16),
            jax.ShapeDtypeStruct((TILE, D), bf16),
        ),
        in_specs=[SMEM, SMEM, VMEM, VMEM, VMEM, VMEM],
        out_specs=(VMEM,) * 7,
        scratch_shapes=[pltpu.VMEM((2 * SLOTS, SLOTS), bf16)],
        compiler_params=params(40),
        cost_estimate=cost(2 * 10**9, 10 * 2**20),
        name="prepare",
    )(columns, counts, values, target, cotangent, weight)


def middle_kernel(
    rows_hbm,
    mix_hbm,
    weight_hbm,
    inner_hbm,
    left_hbm,
    right_hbm,
    mix_t_hbm,
    top_ref,
    bottom_ref,
    out_ref,
    rows,
    mix,
    weight,
    inner,
    left,
    right,
    mix_t,
    sems,
):
    pairs = (
        (mix_hbm, mix),
        (rows_hbm, rows),
        (weight_hbm, weight),
        (inner_hbm, inner),
        (left_hbm, left),
        (right_hbm, right),
        (mix_t_hbm, mix_t),
    )
    copies = [pltpu.make_async_copy(a, b, sems.at[i]) for i, (a, b) in enumerate(pairs)]
    for copy in copies:
        copy.start()
    copies[0].wait()
    copies[1].wait()
    halves = dot(mix[...], rows[...]).astype(bf16)
    mixed = jnp.concatenate([halves[:SLOTS], halves[SLOTS:]], axis=1)
    copies[2].wait()
    before = dot(mixed, weight[...])
    erf = 0.5 * (1.0 + lax.erf(before * ROOT_HALF))
    acted = (before * erf).astype(bf16)
    top_ref[...] = acted[:TILE]
    bottom_ref[...] = acted[TILE:]
    slope = erf + before * (INV_ROOT_TAU * jnp.exp(-0.5 * before * before))
    for copy in copies[3:6]:
        copy.wait()
    rims = jnp.concatenate([left[...], right[...]], axis=0).astype(f32)
    grad_before = ((inner[...] + rims) * slope).astype(bf16)
    grad_mix = dot_t(grad_before, weight[...]).astype(bf16)
    stacked = jnp.concatenate([grad_mix[:, :HALF], grad_mix[:, HALF:]], axis=0)
    copies[6].wait()
    out_ref[...] = dot(mix_t[...], stacked).astype(bf16)


def middle(*arrays):
    return pl.pallas_call(
        middle_kernel,
        out_shape=(
            jax.ShapeDtypeStruct((TILE, D), bf16),
            jax.ShapeDtypeStruct((TILE, D), bf16),
            jax.ShapeDtypeStruct((ROWS, HALF), bf16),
        ),
        in_specs=[ANY] * 7,
        out_specs=(VMEM,) * 3,
        scratch_shapes=[pltpu.VMEM(a.shape, a.dtype) for a in arrays]
        + [pltpu.SemaphoreType.DMA((7,))],
        compiler_params=params(24),
        cost_estimate=cost(3 * 10**9, 8 * 2**20),
        name="middle",
    )(*arrays)


def finish_kernel(left_hbm, top_hbm, bottom_hbm, right_hbm, band_hbm, weight_hbm, out_ref, wide, band, weight, sems):
    sources = (left_hbm, top_hbm, bottom_hbm, right_hbm)
    copies = [
        pltpu.make_async_copy(a, wide.at[pl.ds(i * TILE, TILE), :], sems.at[i])
        for i, a in enumerate(sources)
    ]
    copies.append(pltpu.make_async_copy(band_hbm, band, sems.at[4]))
    copies.append(pltpu.make_async_copy(weight_hbm, weight, sems.at[5]))
    for copy in copies:
        copy.start()
    for copy in copies[:5]:
        copy.wait()
    mixed = dot(band[...], wide[...]).astype(bf16)
    copies[5].wait()
    out_ref[...] = dot(mixed, weight[...]).astype(bf16)


def finish(*arrays):
    return pl.pallas_call(
        finish_kernel,
        out_shape=jax.ShapeDtypeStruct((SLOTS, D), bf16),
        in_specs=[ANY] * 6,
        out_specs=VMEM,
        scratch_shapes=[
            pltpu.VMEM((2 * SLOTS, D), bf16),
            pltpu.VMEM((SLOTS, 2 * SLOTS), bf16),
            pltpu.VMEM((D, D), bf16),
            pltpu.SemaphoreType.DMA((6,)),
        ],
        compiler_params=params(16),
        cost_estimate=cost(10**9, 5 * 2**20),
        name="finish",
    )(*arrays)


def gather_kernel(pick_ref, rows_ref, out_ref):
    for u in range(2):
        picked = dot(pick_ref[u * NODES : (u + 1) * NODES, :], rows_ref[...])
        out_ref[:, u * HALF : (u + 1) * HALF] = picked.astype(bf16)


def gather(pick, rows):
    return pl.pallas_call(
        gather_kernel,
        out_shape=jax.ShapeDtypeStruct((NODES, D), bf16),
        in_specs=[VMEM, VMEM],
        out_specs=VMEM,
        compiler_params=params(16),
        cost_estimate=cost(4 * 10**8, 2 * 2**20),
        name="gather",
    )(pick, rows)


def swap(rows):
    return lax.all_to_all(
        rows.reshape(PEERS, 8, HALF), ("enc", "dom"), split_axis=0, concat_axis=0, tiled=True
    ).reshape(ROWS, HALF)


def local(
    token_states,
    token_nodes,
    expand_weight,
    contract_weight,
    node_owner,
    tile_columns,
    tile_count,
    tile_values,
    first_weight,
    second_weight,
    output_cotangent,
):
    device = lax.axis_index("enc") * GROUP + lax.axis_index("dom")
    upper = (device >= PEERS // 2).astype(jnp.int32).reshape(1)
    rightward = [(i, i + 1) for i in range(GROUP - 1)]
    leftward = [(i + 1, i) for i in range(GROUP - 1)]
    outgoing, target = encode(
        upper, node_owner.reshape(1, NODES), token_nodes, token_states, expand_weight, contract_weight
    )
    arrived = swap(outgoing)
    mix, mix_t, band, pick, inner, low, high = prepare(
        tile_columns, tile_count, tile_values, target, output_cotangent, second_weight
    )
    from_right = lax.ppermute(low, "dom", leftward)
    from_left = lax.ppermute(high, "dom", rightward)
    top, bottom, grads = middle(arrived, mix, first_weight, inner, from_left, from_right, mix_t)
    returned = swap(grads)
    left = lax.ppermute(bottom, "dom", rightward)
    right = lax.ppermute(top, "dom", leftward)
    graph_output = finish(left, top, bottom, right, band, second_weight)
    return (graph_output, gather(pick, returned))


def solution(mesh):
    rows = ("enc", "dom")
    placed = (
        P(rows, None),
        P(rows, None),
        P(),
        P(),
        P(rows, None),
        P(rows, None, None),
        P(rows, None),
        P(rows, None, None, None, None),
        P(),
        P(),
        P(rows, None),
    )
    return jax.shard_map(
        local,
        mesh=mesh,
        in_specs=placed,
        out_specs=(P(rows, None), P(rows, None)),
        check_vma=False,
    )
```

time: 189 us -> 106 us (0.56)
  matrix products: 96.6 us -> 0 us
  Pallas kernels: 0 us -> 36.5 us
  starting transfers between devices: 41.9 us -> 31.4 us
  between operations: 8.92 us -> 0.83 us
  other arithmetic: 7.85 us -> 0 us
  waiting for transfers between devices: 11.3 us -> 15.6 us
    dot_general x32 -> x0, matrix products: 96.6 us -> none  [the longest x1 47 us: encode(): jnp.dot(states_rows, expand_weight, preferred_element_type=jnp.float32)]
    pallas_call x0 -> x5, Pallas kernels: none -> 36.5 us  [the longest x1 26.1 us: encode(): pl.pallas_call(encode_kernel, out_shape=(jax.ShapeDtypeStruct((ROWS, HALF...]
    unnamed x19 -> x48, local copies, waits for them, and re-layouts: 7.09 us -> 20.5 us
    ppermute x8 -> x4, waiting for transfers between devices: 3.88 us -> 15.6 us  [the longest x1 8.52 us: local(): left = lax.ppermute(bottom, 'dom', rightward)]
    ppermute x8 -> x4, starting transfers between devices: 20.9 us -> 10.9 us  [the longest x1 3.54 us: local(): left = lax.ppermute(bottom, 'dom', rightward)]
    all_to_all x2, waiting for transfers between devices: 7.41 us -> 0.01 us  [swap(): lax.all_to_all(rows.reshape(PEERS, 8, HALF), ('enc', 'dom'), split_axis=0...]
    slice x10 -> x0, local copies, waits for them, and re-layouts: 6.61 us -> none  [the longest x2 2.41 us: collect(): interior = extended[TILE:TILE + slot_total]]
    reshape x4 -> x0, local copies, waits for them, and re-layouts: 4.5 us -> none  [the longest x1 2.06 us: local(): grad_vertex.reshape(devices, capacity, features)]
  transfers between devices with their start and end apart: 10 -> 6, of which waited for: 3 -> 4; matrix products, arithmetic and copies ran while one was open for 23% -> 0% of each run, Pallas kernels for 0% -> 5%
where the time goes in v1:
time: 106 us; the launch traced here: 105 us
  Pallas kernels  36.5 us (34%)
  starting transfers between devices  31.4 us (30%)
  local copies, waits for them, and re-layouts  20.5 us (19%)
  waiting for transfers between devices  15.6 us (15%)
    pallas_call x1, Pallas kernels, encode(): pl.pallas_call(encode_kernel, out_shape=(jax.ShapeDtypeStruct((ROWS, HALF...  26.1 us
    all_to_all x2, starting transfers between devices, swap(): lax.all_to_all(rows.reshape(PEERS, 8, HALF), ('enc', 'dom'), split_axis=0...  20.5 us
    unnamed x48, local copies, waits for them, and re-layouts  20.5 us
    ppermute x1, waiting for transfers between devices, local(): left = lax.ppermute(bottom, 'dom', rightward)  8.52 us
    pallas_call x1, Pallas kernels, middle(): pl.pallas_call(middle_kernel, out_shape=(jax.ShapeDtypeStruct((TILE, D),...  3.72 us
    ppermute x1, waiting for transfers between devices, local(): from_right = lax.ppermute(low, 'dom', leftward)  3.69 us
    ppermute x1, starting transfers between devices, local(): left = lax.ppermute(bottom, 'dom', rightward)  3.54 us
    ppermute x1, starting transfers between devices, local(): from_left = lax.ppermute(high, 'dom', rightward)  3.53 us
  transfers between devices with their start and end apart: 6, of which 4 were waited for; matrix products, arithmetic and copies ran while one was open for 0% of the time, Pallas kernels for 5%

profile of v1, /device:TPU:1, one launch (start us, length us, event | category | flops | bytes accessed | tf_op | source)
XLA Modules:
  0.0 104.8 jit_solution(6162181274982681173)
XLA Ops:
  0.6 26.1 %encode.1 = (bf16[1024,512]{1,0:T(8,128)(2,1)}, s32[8,256]{1,0:T(8,128)}) custom-call(s32[1]{0:T(128)} %bitcast.upper_ref, s32[1,192]{1,0:T(1,128)} %bitcast.10, s32[1,1024]{1,0:T(1,128)} %node_ref.1, bf16[1024,1024]{1,0:T(8,128)(2,1)} %states_hbm.1, bf16[1024,4096]{1,0:T(8,128)(2,1)} %expand_hbm.1, bf16[4096,1024]{1,0:T(8,128)(2,1)} %contract_hbm.1), custom_call_target="tpu_custom_call" | custom-call | flops 17179869184 | bytes 20971520 | tf_op jit(solution)/shard_map/encode/pallas_call | solution.py:175
  26.8 11.5 %all-to-all-start = ((bf16[128,8,512]{2,1,0:T(8,128)(2,1)}), bf16[128,8,512]{2,1,0:T(8,128)(2,1)S(1)}, u32[]{:S(2)}, u32[]{:S(2)}) async-start(bf16[128,8,512]{2,1,0:T(8,128)(2,1)} %bitcast.9), calls=%async_computation | async-start | bytes 2097152 | tf_op jit(solution)/shard_map/all_to_all | solution.py:405
  38.4 1.0 copy-done.9
  41.0 3.0 %prepare.1 = (bf16[512,1024]{1,0:T(8,128)(2,1)S(1)}, bf16[1024,512]{1,0:T(8,128)(2,1)S(1)}, bf16[256,512]{1,0:T(8,128)(2,1)S(1)}, bf16[384,1024]{1,0:T(8,128)(2,...) custom-call(s32[1,2,3]{2,1,0:T(2,128)S(1)} %copy-done.15, ...), custom_call_target="tpu_custom_call" | custom-call | flops 2000000000 | bytes 10485760 | tf_op jit(solution)/shard_map/prepare/pallas_call | solution.py:260
  45.9 1.0 copy-done.19
  46.9 1.0 copy-done.21
  47.9 3.5 %collective-permute-start = (bf16[128,1024]{1,0:T(8,128)(2,1)S(1)}, bf16[128,1024]{1,0:T(8,128)(2,1)S(1)}, u32[]{:S(2)}, u32[]{:S(2)}) collective-permute-start(bf16[128,1024]{1,0:T(8,128)(2,1)S(1)} %get-tuple-element.18), channel_id=1, source_target_pairs={{0,1},{1,2},{2,3},{3,4},{4,5},{5,6},{6,7},{8,9},{9,10},{10,11},{11... | collective-permute-start | bytes 786440 | tf_op jit(solution)/shard_map/ppermute | solution.py:435
  51.4 1.9 %collective-permute-start.1 = (bf16[128,1024]{1,0:T(8,128)(2,1)S(1)}, bf16[128,1024]{1,0:T(8,128)(2,1)S(1)}, u32[]{:S(2)}, u32[]{:S(2)}) collective-permute-start(bf16[128,1024]{1,0:T(8,128)(2,1)S(1)} %get-tuple-element.19), channel_id=1, source_target_pairs={{1,0},{2,1},{3,2},{4,3},{5,4},{6,5},{7,6},{9,8},{10,9},{11,10},{12... | collective-permute-start | bytes 786440 | tf_op jit(solution)/shard_map/ppermute | solution.py:434
  53.4 1.4 %collective-permute-done.left_hbm = bf16[128,1024]{1,0:T(8,128)(2,1)S(1)} collective-permute-done((bf16[128,1024]{1,0:T(8,128)(2,1)S(1)}, bf16[128,1024]{1,0:T(8,128)(2,1)S(1)}, u32[]{:S(2)}, u32[]{:S(2)}) %collective-permute-start) | collective-permute-done | bytes 262176 | tf_op jit(solution)/shard_map/ppermute | solution.py:435
  55.4 3.7 %collective-permute-done.1.right_hbm = bf16[128,1024]{1,0:T(8,128)(2,1)S(1)} collective-permute-done((bf16[128,1024]{1,0:T(8,128)(2,1)S(1)}, bf16[128,1024]{1,0:T(8,128)(2,1)S(1)}, u32[]{:S(2)}, u32[]{:S(2)}) %collective-permute-start.1) | collective-permute-done | bytes 262176 | tf_op jit(solution)/shard_map/ppermute | solution.py:434
  59.8 1.6 %copy-done.8 = bf16[1024,1024]{1,0:T(8,128)(2,1)S(1)} copy-done((bf16[1024,1024]{1,0:T(8,128)(2,1)S(1)}, bf16[1024,1024]{1,0:T(8,128)(2,1)}, u32[]{:S(2)}) %copy-start.8) | copy-done | bytes 2097176
  63.3 1.2 %copy-done.18 = bf16[512,1024]{1,0:T(8,128)(2,1)S(1)} copy-done((bf16[512,1024]{1,0:T(8,128)(2,1)S(1)}, bf16[512,1024]{1,0:T(8,128)(2,1)}, u32[]{:S(2)}) %copy-start.18) | copy-done | bytes 1048600
  64.6 1.2 %copy-done.20 = bf16[1024,512]{1,0:T(8,128)(2,1)S(1)} copy-done((bf16[1024,512]{1,0:T(8,128)(2,1)S(1)}, bf16[1024,512]{1,0:T(8,128)(2,1)}, u32[]{:S(2)}) %copy-start.20) | copy-done | bytes 1048600
  65.8 1.2 %copy-done.22 = f32[256,1024]{1,0:T(8,128)S(1)} copy-done((f32[256,1024]{1,0:T(8,128)S(1)}, f32[256,1024]{1,0:T(8,128)}, u32[]{:S(2)}) %copy-start.22) | copy-done | bytes 1048600
  67.0 3.7 %middle.1 = (bf16[128,1024]{1,0:T(8,128)(2,1)S(1)}, bf16[128,1024]{1,0:T(8,128)(2,1)S(1)}, bf16[1024,512]{1,0:T(8,128)(2,1)S(1)}) custom-call(bf16[1024,512]{1,0:T(8,128)(2,1)S(1)} %bitcast.7, bf16[512,1024]{1,0:T(8,128)(2,1)S(1)} %copy-done.18, bf16[1024,1024]{1,0:T(8,128)(2,1)S(1)} %copy-done.8, f32[256,1024]{1,0:T(8,128)S(1)} %copy-done.22, ...), custom_call_target="tpu_custom_call" | custom-call | flops 3000000000 | bytes 8388608 | tf_op jit(solution)/shard_map/middle/pallas_call | solution.py:334
  70.7 1.0 copy-done.1
  73.1 9.0 %all-to-all-start.1 = ((bf16[128,8,512]{2,1,0:T(8,128)(2,1)}), bf16[128,8,512]{2,1,0:T(8,128)(2,1)S(1)}, u32[]{:S(2)}, u32[]{:S(2)}) async-start(bf16[128,8,512]{2,1,0:T(8,128)(2,1)} %bitcast.8), calls=%async_computation.1 | async-start | bytes 2097152 | tf_op jit(solution)/shard_map/all_to_all | solution.py:405
  82.2 3.5 %collective-permute-start.2 = (bf16[128,1024]{1,0:T(8,128)(2,1)}, bf16[128,1024]{1,0:T(8,128)(2,1)S(1)}, u32[]{:S(2)}, u32[]{:S(2)}) collective-permute-start(bf16[128,1024]{1,0:T(8,128)(2,1)} %copy-done.6), channel_id=1, source_target_pairs={{0,1},{1,2},{2,3},{3,4},{4,5},{5,6},{6,7},{8,9},{9,10},{10,11},{11... | collective-permute-start | bytes 786440 | tf_op jit(solution)/shard_map/ppermute | solution.py:438
  85.7 1.9 %collective-permute-start.3 = (bf16[128,1024]{1,0:T(8,128)(2,1)}, bf16[128,1024]{1,0:T(8,128)(2,1)S(1)}, u32[]{:S(2)}, u32[]{:S(2)}) collective-permute-start(bf16[128,1024]{1,0:T(8,128)(2,1)} %copy-done.4), channel_id=1, source_target_pairs={{1,0},{2,1},{3,2},{4,3},{5,4},{6,5},{7,6},{9,8},{10,9},{11,10},{12... | collective-permute-start | bytes 786440 | tf_op jit(solution)/shard_map/ppermute | solution.py:439
  87.6 8.5 %collective-permute-done.2.left_hbm = bf16[128,1024]{1,0:T(8,128)(2,1)S(1)} collective-permute-done((bf16[128,1024]{1,0:T(8,128)(2,1)}, bf16[128,1024]{1,0:T(8,128)(2,1)S(1)}, u32[]{:S(2)}, u32[]{:S(2)}) %collective-permute-start.2) | collective-permute-done | bytes 262176 | tf_op jit(solution)/shard_map/ppermute | solution.py:438
  96.2 2.0 %collective-permute-done.3.right_hbm = bf16[128,1024]{1,0:T(8,128)(2,1)S(1)} collective-permute-done((bf16[128,1024]{1,0:T(8,128)(2,1)}, bf16[128,1024]{1,0:T(8,128)(2,1)S(1)}, u32[]{:S(2)}, u32[]{:S(2)}) %collective-permute-start.3) | collective-permute-done | bytes 262176 | tf_op jit(solution)/shard_map/ppermute | solution.py:439
  100.1 2.2 %finish.1 = bf16[256,1024]{1,0:T(8,128)(2,1)} custom-call(bf16[128,1024]{1,0:T(8,128)(2,1)S(1)} %collective-permute-done.2.left_hbm, bf16[128,1024]{1,0:T(8,128)(2,1)S(1)} %copy-done.5, bf16[128,1024]{1,0:T(8,128)(2,1)S(1)} %copy-done.7, bf16[128,1024]{1,0:T(8,128)(2,1)S(1)} %collective-permute-done.3.right_hbm, ...), custom_call_target="tpu_custom_call" | custom-call | flops 1000000000 | bytes 5242880 | tf_op jit(solution)/shard_map/finish/pallas_call | solution.py:369
  102.3 1.1 %copy-done.3 = bf16[384,1024]{1,0:T(8,128)(2,1)S(1)} copy-done((bf16[384,1024]{1,0:T(8,128)(2,1)S(1)}, bf16[384,1024]{1,0:T(8,128)(2,1)}, u32[]{:S(2)}) %copy-start.3) | copy-done | bytes 786456
  103.5 1.3 %gather.1 = bf16[192,1024]{1,0:T(8,128)(2,1)} custom-call(bf16[384,1024]{1,0:T(8,128)(2,1)S(1)} %copy-done.3, bf16[1024,512]{1,0:T(8,128)(2,1)S(1)} %bitcast.6), custom_call_target="tpu_custom_call" | custom-call | flops 400000000 | bytes 2097152 | tf_op jit(solution)/shard_map/gather/pallas_call | solution.py:393
  (41 shorter events, 10.1 us)
Async XLA Ops:
  26.8 11.5 %copy-start = (bf16[1024,1024]{1,0:T(8,128)(2,1)S(1)}, bf16[1024,1024]{1,0:T(8,128)(2,1)}, u32[]{:S(2)}) copy-start(bf16[1024,1024]{1,0:T(8,128)(2,1)} %weight_hbm.3) | copy-start | bytes 6291460
  26.8 11.5 %copy-start.15 = (s32[1,2,3]{2,1,0:T(2,128)S(1)}, s32[1,2,3]{2,1,0:T(2,128)}, u32[]{:S(2)}) copy-start(s32[1,2,3]{2,1,0:T(2,128)} %columns_ref.1) | copy-start | bytes 76
  26.8 11.5 %copy-start.16 = (s32[1,2]{1,0:T(1,128)S(1)}, s32[1,2]{1,0:T(1,128)}, u32[]{:S(2)}) copy-start(s32[1,2]{1,0:T(1,128)} %count_ref.1) | copy-start | bytes 28
  26.8 33.0 %all-to-all-start = ((bf16[128,8,512]{2,1,0:T(8,128)(2,1)}), bf16[128,8,512]{2,1,0:T(8,128)(2,1)S(1)}, u32[]{:S(2)}, u32[]{:S(2)}) async-start(bf16[128,8,512]{2,1,0:T(8,128)(2,1)} %bitcast.9), calls=%async_computation | async-start | bytes 2097152 | tf_op jit(solution)/shard_map/all_to_all | solution.py:405
  38.4 1.0 copy-start.9
  39.4 0.9 copy-start.14
  45.0 1.0 copy-start.17
  45.9 1.0 copy-start.19
  46.9 1.0 copy-start.21
  47.9 6.8 %collective-permute-start = (bf16[128,1024]{1,0:T(8,128)(2,1)S(1)}, bf16[128,1024]{1,0:T(8,128)(2,1)S(1)}, u32[]{:S(2)}, u32[]{:S(2)}) collective-permute-start(bf16[128,1024]{1,0:T(8,128)(2,1)S(1)} %get-tuple-element.18), channel_id=1, source_target_pairs={{0,1},{1,2},{2,3},{3,4},{4,5},{5,6},{6,7},{8,9},{9,10},{10,11},{11... | collective-permute-start | bytes 786440 | tf_op jit(solution)/shard_map/ppermute | solution.py:435
  51.4 7.7 %collective-permute-start.1 = (bf16[128,1024]{1,0:T(8,128)(2,1)S(1)}, bf16[128,1024]{1,0:T(8,128)(2,1)S(1)}, u32[]{:S(2)}, u32[]{:S(2)}) collective-permute-start(bf16[128,1024]{1,0:T(8,128)(2,1)S(1)} %get-tuple-element.19), channel_id=1, source_target_pairs={{1,0},{2,1},{3,2},{4,3},{5,4},{6,5},{7,6},{9,8},{10,9},{11,10},{12... | collective-permute-start | bytes 786440 | tf_op jit(solution)/shard_map/ppermute | solution.py:434
  59.8 1.6 %copy-start.8 = (bf16[1024,1024]{1,0:T(8,128)(2,1)S(1)}, bf16[1024,1024]{1,0:T(8,128)(2,1)}, u32[]{:S(2)}) copy-start(bf16[1024,1024]{1,0:T(8,128)(2,1)} %weight_hbm.2) | copy-start | bytes 6291460
  61.4 0.9 copy-start.11
  62.4 0.9 copy-start.13
  63.3 1.2 %copy-start.18 = (bf16[512,1024]{1,0:T(8,128)(2,1)S(1)}, bf16[512,1024]{1,0:T(8,128)(2,1)}, u32[]{:S(2)}) copy-start(bf16[512,1024]{1,0:T(8,128)(2,1)} %copy-done.17) | copy-start | bytes 3145732
  64.6 1.2 %copy-start.20 = (bf16[1024,512]{1,0:T(8,128)(2,1)S(1)}, bf16[1024,512]{1,0:T(8,128)(2,1)}, u32[]{:S(2)}) copy-start(bf16[1024,512]{1,0:T(8,128)(2,1)} %copy-done.19) | copy-start | bytes 3145732
  65.8 1.2 %copy-start.22 = (f32[256,1024]{1,0:T(8,128)S(1)}, f32[256,1024]{1,0:T(8,128)}, u32[]{:S(2)}) copy-start(f32[256,1024]{1,0:T(8,128)} %copy-done.21) | copy-start | bytes 3145732
  70.7 1.0 copy-start.1
  73.1 29.2 %all-to-all-start.1 = ((bf16[128,8,512]{2,1,0:T(8,128)(2,1)}), bf16[128,8,512]{2,1,0:T(8,128)(2,1)S(1)}, u32[]{:S(2)}, u32[]{:S(2)}) async-start(bf16[128,8,512]{2,1,0:T(8,128)(2,1)} %bitcast.8), calls=%async_computation.1 | async-start | bytes 2097152 | tf_op jit(solution)/shard_map/all_to_all | solution.py:405
  82.2 14.0 %collective-permute-start.2 = (bf16[128,1024]{1,0:T(8,128)(2,1)}, bf16[128,1024]{1,0:T(8,128)(2,1)S(1)}, u32[]{:S(2)}, u32[]{:S(2)}) collective-permute-start(bf16[128,1024]{1,0:T(8,128)(2,1)} %copy-done.6), channel_id=1, source_target_pairs={{0,1},{1,2},{2,3},{3,4},{4,5},{5,6},{6,7},{8,9},{9,10},{10,11},{11... | collective-permute-start | bytes 786440 | tf_op jit(solution)/shard_map/ppermute | solution.py:438
  85.7 12.5 %collective-permute-start.3 = (bf16[128,1024]{1,0:T(8,128)(2,1)}, bf16[128,1024]{1,0:T(8,128)(2,1)S(1)}, u32[]{:S(2)}, u32[]{:S(2)}) collective-permute-start(bf16[128,1024]{1,0:T(8,128)(2,1)} %copy-done.4), channel_id=1, source_target_pairs={{1,0},{2,1},{3,2},{4,3},{5,4},{6,5},{7,6},{9,8},{10,9},{11,10},{12... | collective-permute-start | bytes 786440 | tf_op jit(solution)/shard_map/ppermute | solution.py:439
  98.2 1.0 copy-start.5
  99.1 0.9 copy-start.7
  102.3 1.1 %copy-start.3 = (bf16[384,1024]{1,0:T(8,128)(2,1)S(1)}, bf16[384,1024]{1,0:T(8,128)(2,1)}, u32[]{:S(2)}) copy-start(bf16[384,1024]{1,0:T(8,128)(2,1)} %copy-done.2) | copy-start | bytes 2359300
  (6 other events, 4.4 us)

commit v2 on v1

--- a/solution.py
+++ b/solution.py
@@ -22,6 +22,7 @@
 BLOCK = 256
 BLOCKS = TOKENS // BLOCK
 AHEAD = 2
+PIECES = 4
 
 bf16 = jnp.bfloat16
 f32 = jnp.float32
@@ -52,6 +53,18 @@
 
 def cost(flops, moved):
     return pl.CostEstimate(flops=flops, bytes_accessed=moved, transcendentals=0)
+
+
+def send_rows(rows_of, out, out_hbm, sem):
+    size = ROWS // PIECES
+    copies = []
+    for i in range(PIECES):
+        rows = pl.ds(i * size, size)
+        out[rows, :] = rows_of(rows).astype(bf16)
+        copies.append(pltpu.make_async_copy(out.at[rows, :], out_hbm.at[rows, :], sem.at[i]))
+        copies[-1].start()
+    for copy in copies:
+        copy.wait()
 
 
 def encode_kernel(
@@ -61,8 +74,9 @@
     states_hbm,
     expand_hbm,
     contract_hbm,
-    out_ref,
+    out_hbm,
     target_ref,
+    out,
     states,
     expand,
     contract,
@@ -76,7 +90,11 @@
     state_sem,
     expand_sem,
     contract_sem,
+    out_sem,
 ):
+    def block_of(m):
+        return pl.ds(m * BLOCK, BLOCK)
+
     def chunk_of(c):
         return pl.ds(pl.multiple_of(c * CHUNK, CHUNK), CHUNK)
 
@@ -96,9 +114,16 @@
             contract_hbm.at[chunk_of(c), :], contract.at[c], contract_sem.at[c]
         ).wait()
 
-    state_copy = pltpu.make_async_copy(states_hbm, states, state_sem)
-    state_copy.start()
-    for c in range(AHEAD):
+    def state_copy(m):
+        return pltpu.make_async_copy(
+            states_hbm.at[block_of(m), :], states.at[block_of(m), :], state_sem.at[m]
+        )
+
+    state_copy(0).start()
+    start(0)
+    for m in range(1, BLOCKS):
+        state_copy(m).start()
+    for c in range(1, AHEAD):
         start(c)
 
     owner_pad[...] = jnp.full((8, NPAD), -4096, jnp.int32)
@@ -124,9 +149,6 @@
     member[...] = mask.astype(bf16)
     counts = jnp.maximum(jnp.sum(mask, axis=1, keepdims=True), 1.0)
 
-    def block_of(m):
-        return pl.ds(m * BLOCK, BLOCK)
-
     def first(c, m):
         return dot(states[block_of(m), :], expand[c])
 
@@ -134,40 +156,44 @@
         acted = 0.5 * values * (1.0 + lax.erf(values * ROOT_HALF))
         total[block_of(m), :] += dot(acted.astype(bf16), contract[c])
 
-    state_copy.wait()
-    total[...] = states[...].astype(f32)
-    wait(0)
-    hidden_a[...] = first(0, 0)
     buffers = (hidden_a, hidden_b)
+    for m in range(BLOCKS):
+        state_copy(m).wait()
+        total[block_of(m), :] = states[block_of(m), :].astype(f32)
+        if m == 0:
+            wait(0)
+            hidden_a[...] = first(0, 0)
 
     def step(c, carry):
         @pl.when(c + AHEAD < CHUNKS)
         def _():
             start(c + AHEAD)
 
-        @pl.when(c + 1 < CHUNKS)
-        def _():
-            wait(c + 1)
-
+        wait(c + 1)
         for m in range(BLOCKS):
             now, later = buffers[m % 2], buffers[(m + 1) % 2]
             if m + 1 < BLOCKS:
                 later[...] = first(c, m + 1)
             else:
-                later[...] = first(jnp.minimum(c + 1, CHUNKS - 1), 0)
+                later[...] = first(c + 1, 0)
             second(c, m, now[...])
         return carry
 
-    lax.fori_loop(0, CHUNKS, step, 0)
+    lax.fori_loop(0, CHUNKS - 1, step, 0)
 
     for m in range(BLOCKS):
+        now, later = buffers[m % 2], buffers[(m + 1) % 2]
+        if m + 1 < BLOCKS:
+            later[...] = first(CHUNKS - 1, m + 1)
+        second(CHUNKS - 1, m, now[...])
         mixed = total[block_of(m), :]
         centred = mixed - jnp.mean(mixed, axis=1, keepdims=True)
         variance = jnp.mean(centred * centred, axis=1, keepdims=True)
         normed[block_of(m), :] = (centred * lax.rsqrt(variance + EPS)).astype(bf16)
-    embeds = (dot(member[...], normed[...]) / counts).astype(bf16)
+    summed = dot(member[...], normed[...])
+    embeds = (summed / counts).astype(bf16)
     stacked = jnp.concatenate([embeds[:, :HALF], embeds[:, HALF:]], axis=0)
-    out_ref[...] = dot(route[...], stacked).astype(bf16)
+    send_rows(lambda r: dot(route[r, :], stacked), out, out_hbm, out_sem)
 
 
 def encode(upper, owner, node_ids, states, expand_weight, contract_weight):
@@ -179,8 +205,9 @@
             jax.ShapeDtypeStruct((8, NPAD), jnp.int32),
         ),
         in_specs=[SMEM, VMEM, VMEM, ANY, ANY, ANY],
-        out_specs=(VMEM, VMEM),
+        out_specs=(ANY, VMEM),
         scratch_shapes=[
+            pltpu.VMEM((ROWS, HALF), bf16),
             pltpu.VMEM((TOKENS, D), bf16),
             pltpu.VMEM((CHUNKS, D, CHUNK), bf16),
             pltpu.VMEM((CHUNKS, CHUNK, D), bf16),
@@ -191,9 +218,10 @@
             pltpu.VMEM((ROWS, 2 * NPAD), bf16),
             pltpu.VMEM((NPAD, TOKENS), bf16),
             pltpu.VMEM((TOKENS, D), bf16),
-            dma,
+            dma((BLOCKS,)),
             dma((CHUNKS,)),
             dma((CHUNKS,)),
+            dma((PIECES,)),
         ],
         compiler_params=params(56),
         cost_estimate=cost(4 * TOKENS * D * FF, 20 * 2**20),
@@ -205,13 +233,11 @@
     columns_ref,
     count_ref,
     values_ref,
-    target_ref,
     cotangent_ref,
     weight_ref,
     mix_ref,
     mix_t_ref,
     band_ref,
-    pick_ref,
     inner_ref,
     low_ref,
     high_ref,
@@ -241,14 +267,6 @@
         back = jnp.where(iota(shape[::-1], 1) == place(iota((ROWS, 1), 0), u), 1.0, 0.0)
         mix_t_ref[:, u * SLOTS : (u + 1) * SLOTS] = dot(back.astype(bf16), band_t[...]).astype(bf16)
 
-    diagonal = iota((NODES, NPAD), 0) == iota((NODES, NPAD), 1)
-    own_row = jnp.sum(jnp.where(diagonal, target_ref[0:1, :], 0), axis=1, keepdims=True)
-    halo_row = jnp.sum(jnp.where(diagonal, target_ref[1:2, :], 0), axis=1, keepdims=True)
-    lanes = iota((NODES, ROWS), 1)
-    for u in range(2):
-        hit = (lanes - 4 * u == own_row) | (lanes - 4 * u == halo_row)
-        pick_ref[u * NODES : (u + 1) * NODES, :] = jnp.where(hit, 1.0, 0.0).astype(bf16)
-
     grad_mix = dot_t(cotangent_ref[...], weight_ref[...]).astype(bf16)
     spread = dot(band_t[...], grad_mix)
     low_ref[...] = spread[:TILE].astype(bf16)
@@ -256,25 +274,24 @@
     high_ref[...] = spread[TILE + SLOTS :].astype(bf16)
 
 
-def prepare(columns, counts, values, target, cotangent, weight):
+def prepare(columns, counts, values, cotangent, weight):
     return pl.pallas_call(
         prepare_kernel,
         out_shape=(
             jax.ShapeDtypeStruct((2 * SLOTS, ROWS), bf16),
             jax.ShapeDtypeStruct((ROWS, 2 * SLOTS), bf16),
             jax.ShapeDtypeStruct((SLOTS, 2 * SLOTS), bf16),
-            jax.ShapeDtypeStruct((2 * NODES, ROWS), bf16),
             jax.ShapeDtypeStruct((SLOTS, D), f32),
             jax.ShapeDtypeStruct((TILE, D), bf16),
             jax.ShapeDtypeStruct((TILE, D), bf16),
         ),
-        in_specs=[SMEM, SMEM, VMEM, VMEM, VMEM, VMEM],
-        out_specs=(VMEM,) * 7,
+        in_specs=[SMEM, SMEM, VMEM, VMEM, VMEM],
+        out_specs=(VMEM,) * 6,
         scratch_shapes=[pltpu.VMEM((2 * SLOTS, SLOTS), bf16)],
         compiler_params=params(40),
         cost_estimate=cost(2 * 10**9, 10 * 2**20),
         name="prepare",
-    )(columns, counts, values, target, cotangent, weight)
+    )(columns, counts, values, cotangent, weight)
 
 
 def middle_kernel(
@@ -285,9 +302,11 @@
     left_hbm,
     right_hbm,
     mix_t_hbm,
-    top_ref,
-    bottom_ref,
-    out_ref,
+    top_hbm,
+    bottom_hbm,
+    out_hbm,
+    acts,
+    out,
     rows,
     mix,
     weight,
@@ -296,6 +315,8 @@
     right,
     mix_t,
     sems,
+    act_sems,
+    out_sems,
 ):
     pairs = (
         (mix_hbm, mix),
@@ -317,8 +338,13 @@
     before = dot(mixed, weight[...])
     erf = 0.5 * (1.0 + lax.erf(before * ROOT_HALF))
     acted = (before * erf).astype(bf16)
-    top_ref[...] = acted[:TILE]
-    bottom_ref[...] = acted[TILE:]
+    acts[...] = acted
+    act_copies = [
+        pltpu.make_async_copy(acts.at[pl.ds(i * TILE, TILE), :], to, act_sems.at[i])
+        for i, to in enumerate((top_hbm, bottom_hbm))
+    ]
+    for copy in act_copies:
+        copy.start()
     slope = erf + before * (INV_ROOT_TAU * jnp.exp(-0.5 * before * before))
     for copy in copies[3:6]:
         copy.wait()
@@ -327,7 +353,9 @@
     grad_mix = dot_t(grad_before, weight[...]).astype(bf16)
     stacked = jnp.concatenate([grad_mix[:, :HALF], grad_mix[:, HALF:]], axis=0)
     copies[6].wait()
-    out_ref[...] = dot(mix_t[...], stacked).astype(bf16)
+    send_rows(lambda r: dot(mix_t[r, :], stacked), out, out_hbm, out_sems)
+    for copy in act_copies:
+        copy.wait()
 
 
 def middle(*arrays):
@@ -339,10 +367,11 @@
             jax.ShapeDtypeStruct((ROWS, HALF), bf16),
         ),
         in_specs=[ANY] * 7,
-        out_specs=(VMEM,) * 3,
-        scratch_shapes=[pltpu.VMEM(a.shape, a.dtype) for a in arrays]
-        + [pltpu.SemaphoreType.DMA((7,))],
-        compiler_params=params(24),
+        out_specs=(ANY,) * 3,
+        scratch_shapes=[pltpu.VMEM((SLOTS, D), bf16), pltpu.VMEM((ROWS, HALF), bf16)]
+        + [pltpu.VMEM(a.shape, a.dtype) for a in arrays]
+        + [pltpu.SemaphoreType.DMA((n,)) for n in (7, 2, PIECES)],
+        compiler_params=params(62),
         cost_estimate=cost(3 * 10**9, 8 * 2**20),
         name="middle",
     )(*arrays)
@@ -383,22 +412,30 @@
     )(*arrays)
 
 
-def gather_kernel(pick_ref, rows_ref, out_ref):
+def gather_kernel(target_ref, rows_ref, out_ref, pick):
+    diagonal = iota((NODES, NPAD), 0) == iota((NODES, NPAD), 1)
+    own_row = jnp.sum(jnp.where(diagonal, target_ref[0:1, :], 0), axis=1, keepdims=True)
+    halo_row = jnp.sum(jnp.where(diagonal, target_ref[1:2, :], 0), axis=1, keepdims=True)
+    lanes = iota((NODES, ROWS), 1)
     for u in range(2):
-        picked = dot(pick_ref[u * NODES : (u + 1) * NODES, :], rows_ref[...])
+        hit = (lanes - 4 * u == own_row) | (lanes - 4 * u == halo_row)
+        pick[u * NODES : (u + 1) * NODES, :] = jnp.where(hit, 1.0, 0.0).astype(bf16)
+    for u in range(2):
+        picked = dot(pick[u * NODES : (u + 1) * NODES, :], rows_ref[...])
         out_ref[:, u * HALF : (u + 1) * HALF] = picked.astype(bf16)
 
 
-def gather(pick, rows):
+def gather(target, rows):
     return pl.pallas_call(
         gather_kernel,
         out_shape=jax.ShapeDtypeStruct((NODES, D), bf16),
         in_specs=[VMEM, VMEM],
         out_specs=VMEM,
+        scratch_shapes=[pltpu.VMEM((2 * NODES, ROWS), bf16)],
         compiler_params=params(16),
         cost_estimate=cost(4 * 10**8, 2 * 2**20),
         name="gather",
-    )(pick, rows)
+    )(target, rows)
 
 
 def swap(rows):
@@ -428,8 +465,9 @@
         upper, node_owner.reshape(1, NODES), token_nodes, token_states, expand_weight, contract_weight
     )
     arrived = swap(outgoing)
-    mix, mix_t, band, pick, inner, low, high = prepare(
-        tile_columns, tile_count, tile_values, target, output_cotangent, second_weight
+    target, later_cotangent = lax.optimization_barrier((target, output_cotangent))
+    mix, mix_t, band, inner, low, high = prepare(
+        tile_columns, tile_count, tile_values, later_cotangent, second_weight
     )
     from_right = lax.ppermute(low, "dom", leftward)
     from_left = lax.ppermute(high, "dom", rightward)
@@ -438,7 +476,7 @@
     left = lax.ppermute(bottom, "dom", rightward)
     right = lax.ppermute(top, "dom", leftward)
     graph_output = finish(left, top, bottom, right, band, second_weight)
-    return (graph_output, gather(pick, returned))
+    return (graph_output, gather(target, returned))
 
 
 def solution(mesh):

time: 106 us -> 92.6 us (0.87)
  local copies, waits for them, and re-layouts: 20.5 us -> 4.87 us
  waiting for transfers between devices: 15.6 us -> 18 us
  Pallas kernels: 36.5 us -> 37.6 us
    unnamed x48 -> x28, local copies, waits for them, and re-layouts: 20.5 us -> 4.87 us
    pallas_call x1, Pallas kernels: 3.72 us -> 5.59 us  [middle(): pl.pallas_call(middle_kernel, out_shape=(jax.ShapeDtypeStruct((TILE, D),...]
    all_to_all x2, waiting for transfers between devices: 0.01 us -> 1.48 us  [swap(): lax.all_to_all(rows.reshape(PEERS, 8, HALF), ('enc', 'dom'), split_axis=0...]
  transfers between devices with their start and end apart: 6 -> 6, of which waited for: 4 -> 5; matrix products, arithmetic and copies ran while one was open for 0% -> 0% of each run, Pallas kernels for 5% -> 6%
where the time goes in v2:
time: 92.6 us; the launch traced here: 92.2 us
  Pallas kernels  37.6 us (41%)
  starting transfers between devices  30.9 us (33%)
  waiting for transfers between devices  18 us (19%)
  local copies, waits for them, and re-layouts  4.87 us (5%)
    pallas_call x1, Pallas kernels, encode(): pl.pallas_call(encode_kernel, out_shape=(jax.ShapeDtypeStruct((ROWS, HALF...  25.5 us
    all_to_all x2, starting transfers between devices, swap(): lax.all_to_all(rows.reshape(PEERS, 8, HALF), ('enc', 'dom'), split_axis=0...  19.8 us
    ppermute x1, waiting for transfers between devices, local(): left = lax.ppermute(bottom, 'dom', rightward)  8.52 us
    pallas_call x1, Pallas kernels, middle(): pl.pallas_call(middle_kernel, out_shape=(jax.ShapeDtypeStruct((TILE, D),...  5.59 us
    unnamed x28, local copies, waits for them, and re-layouts  4.87 us
    ppermute x1, waiting for transfers between devices, local(): from_right = lax.ppermute(low, 'dom', leftward)  4.07 us
    ppermute x1, starting transfers between devices, local(): left = lax.ppermute(bottom, 'dom', rightward)  3.54 us
    ppermute x1, starting transfers between devices, local(): from_left = lax.ppermute(high, 'dom', rightward)  3.53 us
  transfers between devices with their start and end apart: 6, of which 5 were waited for; matrix products, arithmetic and copies ran while one was open for 0% of the time, Pallas kernels for 6%

profile of v2, /device:TPU:1, one launch (start us, length us, event | category | flops | bytes accessed | tf_op | source)
XLA Modules:
  0.0 92.2 jit_solution(2612147951632334999)
XLA Ops:
  0.7 25.5 %encode.1 = (bf16[1024,512]{1,0:T(8,128)(2,1)}, s32[8,256]{1,0:T(8,128)}) custom-call(s32[1]{0:T(128)} %bitcast.upper_ref, s32[1,192]{1,0:T(1,128)} %bitcast.9, s32[1,1024]{1,0:T(1,128)} %node_ref.1, bf16[1024,1024]{1,0:T(8,128)(2,1)} %states_hbm.1, bf16[1024,4096]{1,0:T(8,128)(2,1)} %expand_hbm.1, bf16[4096,1024]{1,0:T(8,128)(2,1)} %contract_hbm.1), custom_call_target="tpu_custom_call" | custom-call | flops 17179869184 | bytes 20971520 | tf_op jit(solution)/shard_map/encode/pallas_call | solution.py:201
  26.1 0.0 copy-start
  26.2 0.0 copy-start.7
  26.2 12.0 %all-to-all-start = ((bf16[128,8,512]{2,1,0:T(8,128)(2,1)}), bf16[128,8,512]{2,1,0:T(8,128)(2,1)}, u32[]{:S(2)}, u32[]{:S(2)}) async-start(bf16[128,8,512]{2,1,0:T(8,128)(2,1)} %bitcast.8), calls=%async_computation | async-start | bytes 2097152 | tf_op jit(solution)/shard_map/all_to_all | solution.py:442
  38.2 2.9 %prepare.1 = (bf16[512,1024]{1,0:T(8,128)(2,1)S(1)}, bf16[1024,512]{1,0:T(8,128)(2,1)S(1)}, bf16[256,512]{1,0:T(8,128)(2,1)S(1)}, f32[256,1024]{1,0:T(8,128)S(1)...) custom-call(s32[1,2,3]{2,1,0:T(2,128)S(1)} %copy-done.6, s32[1,2]{1,0:T(1,128)S(1)} %copy-done.7, ...), custom_call_target="tpu_custom_call" | custom-call | flops 2000000000 | bytes 10485760 | tf_op jit(solution)/shard_map/prepare/pallas_call | solution.py:278
  41.1 1.0 %copy-done.9 = bf16[512,1024]{1,0:T(8,128)(2,1)} copy-done((bf16[512,1024]{1,0:T(8,128)(2,1)}, bf16[512,1024]{1,0:T(8,128)(2,1)S(1)}, u32[]{:S(2)}) %copy-start.9) | copy-done | bytes 1048600
  42.1 1.0 %copy-done.10 = bf16[1024,512]{1,0:T(8,128)(2,1)} copy-done((bf16[1024,512]{1,0:T(8,128)(2,1)}, bf16[1024,512]{1,0:T(8,128)(2,1)S(1)}, u32[]{:S(2)}) %copy-start.10) | copy-done | bytes 1048600
  43.0 1.0 %copy-done.11 = f32[256,1024]{1,0:T(8,128)} copy-done((f32[256,1024]{1,0:T(8,128)}, f32[256,1024]{1,0:T(8,128)S(1)}, u32[]{:S(2)}) %copy-start.11) | copy-done | bytes 1048600
  44.0 3.5 %collective-permute-start = (bf16[128,1024]{1,0:T(8,128)(2,1)S(1)}, bf16[128,1024]{1,0:T(8,128)(2,1)S(1)}, u32[]{:S(2)}, u32[]{:S(2)}) collective-permute-start(bf16[128,1024]{1,0:T(8,128)(2,1)S(1)} %get-tuple-element.20), channel_id=1, source_target_pairs={{0,1},{1,2},{2,3},{3,4},{4,5},{5,6},{6,7},{8,9},{9,10},{10,11},{11... | collective-permute-start | bytes 786440 | tf_op jit(solution)/shard_map/ppermute | solution.py:473
  47.6 2.1 %collective-permute-start.1 = (bf16[128,1024]{1,0:T(8,128)(2,1)S(1)}, bf16[128,1024]{1,0:T(8,128)(2,1)S(1)}, u32[]{:S(2)}, u32[]{:S(2)}) collective-permute-start(bf16[128,1024]{1,0:T(8,128)(2,1)S(1)} %get-tuple-element.21), channel_id=1, source_target_pairs={{1,0},{2,1},{3,2},{4,3},{5,4},{6,5},{7,6},{9,8},{10,9},{11,10},{12... | collective-permute-start | bytes 786440 | tf_op jit(solution)/shard_map/ppermute | solution.py:472
  49.7 1.9 %collective-permute-done.left_hbm = bf16[128,1024]{1,0:T(8,128)(2,1)S(1)} collective-permute-done((bf16[128,1024]{1,0:T(8,128)(2,1)S(1)}, bf16[128,1024]{1,0:T(8,128)(2,1)S(1)}, u32[]{:S(2)}, u32[]{:S(2)}) %collective-permute-start) | collective-permute-done | bytes 262176 | tf_op jit(solution)/shard_map/ppermute | solution.py:473
  51.6 4.1 %collective-permute-done.1.right_hbm = bf16[128,1024]{1,0:T(8,128)(2,1)S(1)} collective-permute-done((bf16[128,1024]{1,0:T(8,128)(2,1)S(1)}, bf16[128,1024]{1,0:T(8,128)(2,1)S(1)}, u32[]{:S(2)}, u32[]{:S(2)}) %collective-permute-start.1) | collective-permute-done | bytes 262176 | tf_op jit(solution)/shard_map/ppermute | solution.py:472
  55.6 1.5 %all-to-all-done = bf16[128,8,512]{2,1,0:T(8,128)(2,1)} async-done(((bf16[128,8,512]{2,1,0:T(8,128)(2,1)}), bf16[128,8,512]{2,1,0:T(8,128)(2,1)}, u32[]{:S(2)}, u32[]{:S(2)}) %all-to-all-start) | async-done | bytes 1048608 | tf_op jit(solution)/shard_map/all_to_all | solution.py:442
  57.1 5.6 %middle.1 = (bf16[128,1024]{1,0:T(8,128)(2,1)}, bf16[128,1024]{1,0:T(8,128)(2,1)}, bf16[1024,512]{1,0:T(8,128)(2,1)}) custom-call(bf16[1024,512]{1,0:T(8,128)(2,1)} %bitcast.3.rows_hbm, bf16[512,1024]{1,0:T(8,128)(2,1)} %copy-done.9, bf16[1024,1024]{1,0:T(8,128)(2,1)} %weight_hbm.2, f32[256,1024]{1,0:T(8,128)} %copy-done.11, bf16[128,1024]{1,0:T(8,128)(2,1)} %copy-done.12, ...), custom_call_target="tpu_custom_call" | custom-call | flops 3000000000 | bytes 8388608 | tf_op jit(solution)/shard_map/middle/pallas_call | solution.py:362
  62.7 0.0 copy-start.1
  62.8 7.9 %all-to-all-start.1 = ((bf16[128,8,512]{2,1,0:T(8,128)(2,1)}), bf16[128,8,512]{2,1,0:T(8,128)(2,1)S(1)}, u32[]{:S(2)}, u32[]{:S(2)}) async-start(bf16[128,8,512]{2,1,0:T(8,128)(2,1)} %bitcast.7), calls=%async_computation.1 | async-start | bytes 2097152 | tf_op jit(solution)/shard_map/all_to_all | solution.py:442
  70.6 3.5 %collective-permute-start.2 = (bf16[128,1024]{1,0:T(8,128)(2,1)}, bf16[128,1024]{1,0:T(8,128)(2,1)S(1)}, u32[]{:S(2)}, u32[]{:S(2)}) collective-permute-start(bf16[128,1024]{1,0:T(8,128)(2,1)} %get-tuple-element.23.bottom_hbm), channel_id=1, source_target_pairs={{0,1},{1,2},{2,3},{3,4},{4,5},{5,6},{6,7},{8,9},{9,10},{10,11},{11... | collective-permute-start | bytes 786440 | tf_op jit(solution)/shard_map/ppermute | solution.py:476
  74.2 1.9 %collective-permute-start.3 = (bf16[128,1024]{1,0:T(8,128)(2,1)}, bf16[128,1024]{1,0:T(8,128)(2,1)S(1)}, u32[]{:S(2)}, u32[]{:S(2)}) collective-permute-start(bf16[128,1024]{1,0:T(8,128)(2,1)} %get-tuple-element.24.top_hbm), channel_id=1, source_target_pairs={{1,0},{2,1},{3,2},{4,3},{5,4},{6,5},{7,6},{9,8},{10,9},{11,10},{12... | collective-permute-start | bytes 786440 | tf_op jit(solution)/shard_map/ppermute | solution.py:477
  76.1 8.5 %collective-permute-done.2.left_hbm = bf16[128,1024]{1,0:T(8,128)(2,1)S(1)} collective-permute-done((bf16[128,1024]{1,0:T(8,128)(2,1)}, bf16[128,1024]{1,0:T(8,128)(2,1)S(1)}, u32[]{:S(2)}, u32[]{:S(2)}) %collective-permute-start.2) | collective-permute-done | bytes 262176 | tf_op jit(solution)/shard_map/ppermute | solution.py:476
  84.6 2.0 %collective-permute-done.3.right_hbm = bf16[128,1024]{1,0:T(8,128)(2,1)S(1)} collective-permute-done((bf16[128,1024]{1,0:T(8,128)(2,1)}, bf16[128,1024]{1,0:T(8,128)(2,1)S(1)}, u32[]{:S(2)}, u32[]{:S(2)}) %collective-permute-start.3) | collective-permute-done | bytes 262176 | tf_op jit(solution)/shard_map/ppermute | solution.py:477
  86.6 0.9 %copy-done.2 = bf16[128,1024]{1,0:T(8,128)(2,1)S(1)} copy-done((bf16[128,1024]{1,0:T(8,128)(2,1)S(1)}, bf16[128,1024]{1,0:T(8,128)(2,1)}, u32[]{:S(2)}) %copy-start.2) | copy-done | bytes 262168
  87.6 0.9 %copy-done.3 = bf16[128,1024]{1,0:T(8,128)(2,1)S(1)} copy-done((bf16[128,1024]{1,0:T(8,128)(2,1)S(1)}, bf16[128,1024]{1,0:T(8,128)(2,1)}, u32[]{:S(2)}) %copy-start.3) | copy-done | bytes 262168
  88.5 2.2 %finish.1 = bf16[256,1024]{1,0:T(8,128)(2,1)} custom-call(bf16[128,1024]{1,0:T(8,128)(2,1)S(1)} %collective-permute-done.2.left_hbm, bf16[128,1024]{1,0:T(8,128)(2,1)S(1)} %copy-done.2, bf16[128,1024]{1,0:T(8,128)(2,1)S(1)} %copy-done.3, bf16[128,1024]{1,0:T(8,128)(2,1)S(1)} %collective-permute-done.3.right_hbm, ...), custom_call_target="tpu_custom_call" | custom-call | flops 1000000000 | bytes 5242880 | tf_op jit(solution)/shard_map/finish/pallas_call | solution.py:398
  90.8 1.4 %gather.1 = bf16[192,1024]{1,0:T(8,128)(2,1)} custom-call(s32[8,256]{1,0:T(8,128)S(1)} %copy-done.8, bf16[1024,512]{1,0:T(8,128)(2,1)S(1)} %bitcast.6), custom_call_target="tpu_custom_call" | custom-call | flops 400000000 | bytes 2097152 | tf_op jit(solution)/shard_map/gather/pallas_call | solution.py:429
  (21 shorter events, 0.0 us)
Async XLA Ops:
  0.6 37.5 %copy-start.4 = (bf16[256,1024]{1,0:T(8,128)(2,1)S(1)}, bf16[256,1024]{1,0:T(8,128)(2,1)}, u32[]{:S(2)}) copy-start(bf16[256,1024]{1,0:T(8,128)(2,1)} %cotangent_ref) | copy-start | bytes 1572868
  0.6 37.5 %copy-start.5 = (bf16[1,2,3,128,128]{4,3,2,1,0:T(8,128)(2,1)S(1)}, bf16[1,2,3,128,128]{4,3,2,1,0:T(8,128)(2,1)}, u32[]{:S(2)}) copy-start(bf16[1,2,3,128,128]{4,3,2,1,0:T(8,128)(2,1)} %values_ref.1) | copy-start | bytes 589828
  26.1 12.0 %copy-start = (bf16[1024,1024]{1,0:T(8,128)(2,1)S(1)}, bf16[1024,1024]{1,0:T(8,128)(2,1)}, u32[]{:S(2)}) copy-start(bf16[1024,1024]{1,0:T(8,128)(2,1)} %weight_hbm.3) | copy-start | bytes 6291460
  26.1 12.0 %copy-start.6 = (s32[1,2,3]{2,1,0:T(2,128)S(1)}, s32[1,2,3]{2,1,0:T(2,128)}, u32[]{:S(2)}) copy-start(s32[1,2,3]{2,1,0:T(2,128)} %columns_ref.1) | copy-start | bytes 76
  26.2 12.0 %copy-start.7 = (s32[1,2]{1,0:T(1,128)S(1)}, s32[1,2]{1,0:T(1,128)}, u32[]{:S(2)}) copy-start(s32[1,2]{1,0:T(1,128)} %count_ref.1) | copy-start | bytes 28
  26.2 31.0 %all-to-all-start = ((bf16[128,8,512]{2,1,0:T(8,128)(2,1)}), bf16[128,8,512]{2,1,0:T(8,128)(2,1)}, u32[]{:S(2)}, u32[]{:S(2)}) async-start(bf16[128,8,512]{2,1,0:T(8,128)(2,1)} %bitcast.8), calls=%async_computation | async-start | bytes 2097152 | tf_op jit(solution)/shard_map/all_to_all | solution.py:442
  41.1 1.0 %copy-start.9 = (bf16[512,1024]{1,0:T(8,128)(2,1)}, bf16[512,1024]{1,0:T(8,128)(2,1)S(1)}, u32[]{:S(2)}) copy-start(bf16[512,1024]{1,0:T(8,128)(2,1)S(1)} %get-tuple-element.18.mix_hbm) | copy-start | bytes 3145732
  42.1 1.0 %copy-start.10 = (bf16[1024,512]{1,0:T(8,128)(2,1)}, bf16[1024,512]{1,0:T(8,128)(2,1)S(1)}, u32[]{:S(2)}) copy-start(bf16[1024,512]{1,0:T(8,128)(2,1)S(1)} %get-tuple-element.22.mix_t_hbm) | copy-start | bytes 3145732
  43.0 1.0 %copy-start.11 = (f32[256,1024]{1,0:T(8,128)}, f32[256,1024]{1,0:T(8,128)S(1)}, u32[]{:S(2)}) copy-start(f32[256,1024]{1,0:T(8,128)S(1)} %get-tuple-element.19.inner_hbm) | copy-start | bytes 3145732
  44.0 7.6 %collective-permute-start = (bf16[128,1024]{1,0:T(8,128)(2,1)S(1)}, bf16[128,1024]{1,0:T(8,128)(2,1)S(1)}, u32[]{:S(2)}, u32[]{:S(2)}) collective-permute-start(bf16[128,1024]{1,0:T(8,128)(2,1)S(1)} %get-tuple-element.20), channel_id=1, source_target_pairs={{0,1},{1,2},{2,3},{3,4},{4,5},{5,6},{6,7},{8,9},{9,10},{10,11},{11... | collective-permute-start | bytes 786440 | tf_op jit(solution)/shard_map/ppermute | solution.py:473
  47.6 8.1 %collective-permute-start.1 = (bf16[128,1024]{1,0:T(8,128)(2,1)S(1)}, bf16[128,1024]{1,0:T(8,128)(2,1)S(1)}, u32[]{:S(2)}, u32[]{:S(2)}) collective-permute-start(bf16[128,1024]{1,0:T(8,128)(2,1)S(1)} %get-tuple-element.21), channel_id=1, source_target_pairs={{1,0},{2,1},{3,2},{4,3},{5,4},{6,5},{7,6},{9,8},{10,9},{11,10},{12... | collective-permute-start | bytes 786440 | tf_op jit(solution)/shard_map/ppermute | solution.py:472
  51.6 5.6 %copy-start.12 = (bf16[128,1024]{1,0:T(8,128)(2,1)}, bf16[128,1024]{1,0:T(8,128)(2,1)S(1)}, u32[]{:S(2)}) copy-start(bf16[128,1024]{1,0:T(8,128)(2,1)S(1)} %collective-permute-done.left_hbm) | copy-start | bytes 786436
  55.6 1.5 %copy-start.13 = (bf16[128,1024]{1,0:T(8,128)(2,1)}, bf16[128,1024]{1,0:T(8,128)(2,1)S(1)}, u32[]{:S(2)}) copy-start(bf16[128,1024]{1,0:T(8,128)(2,1)S(1)} %collective-permute-done.1.right_hbm) | copy-start | bytes 786436
  62.7 23.9 %copy-start.1 = (bf16[1024,1024]{1,0:T(8,128)(2,1)S(1)}, bf16[1024,1024]{1,0:T(8,128)(2,1)}, u32[]{:S(2)}) copy-start(bf16[1024,1024]{1,0:T(8,128)(2,1)} %weight_hbm.3) | copy-start | bytes 6291460
  62.7 28.0 %copy-start.8 = (s32[8,256]{1,0:T(8,128)S(1)}, s32[8,256]{1,0:T(8,128)}, u32[]{:S(2)}) copy-start(s32[8,256]{1,0:T(8,128)} %get-tuple-element.26.target_ref) | copy-start | bytes 24580
  62.8 28.0 %all-to-all-start.1 = ((bf16[128,8,512]{2,1,0:T(8,128)(2,1)}), bf16[128,8,512]{2,1,0:T(8,128)(2,1)S(1)}, u32[]{:S(2)}, u32[]{:S(2)}) async-start(bf16[128,8,512]{2,1,0:T(8,128)(2,1)} %bitcast.7), calls=%async_computation.1 | async-start | bytes 2097152 | tf_op jit(solution)/shard_map/all_to_all | solution.py:442
  70.6 14.0 %collective-permute-start.2 = (bf16[128,1024]{1,0:T(8,128)(2,1)}, bf16[128,1024]{1,0:T(8,128)(2,1)S(1)}, u32[]{:S(2)}, u32[]{:S(2)}) collective-permute-start(bf16[128,1024]{1,0:T(8,128)(2,1)} %get-tuple-element.23.bottom_hbm), channel_id=1, source_target_pairs={{0,1},{1,2},{2,3},{3,4},{4,5},{5,6},{6,7},{8,9},{9,10},{10,11},{11... | collective-permute-start | bytes 786440 | tf_op jit(solution)/shard_map/ppermute | solution.py:476
  74.2 12.5 %collective-permute-start.3 = (bf16[128,1024]{1,0:T(8,128)(2,1)}, bf16[128,1024]{1,0:T(8,128)(2,1)S(1)}, u32[]{:S(2)}, u32[]{:S(2)}) collective-permute-start(bf16[128,1024]{1,0:T(8,128)(2,1)} %get-tuple-element.24.top_hbm), channel_id=1, source_target_pairs={{1,0},{2,1},{3,2},{4,3},{5,4},{6,5},{7,6},{9,8},{10,9},{11,10},{12... | collective-permute-start | bytes 786440 | tf_op jit(solution)/shard_map/ppermute | solution.py:477
  86.6 1.0 %copy-start.2 = (bf16[128,1024]{1,0:T(8,128)(2,1)S(1)}, bf16[128,1024]{1,0:T(8,128)(2,1)}, u32[]{:S(2)}) copy-start(bf16[128,1024]{1,0:T(8,128)(2,1)} %get-tuple-element.24.top_hbm) | copy-start | bytes 786436
  87.6 0.9 %copy-start.3 = (bf16[128,1024]{1,0:T(8,128)(2,1)S(1)}, bf16[128,1024]{1,0:T(8,128)(2,1)}, u32[]{:S(2)}) copy-start(bf16[128,1024]{1,0:T(8,128)(2,1)} %get-tuple-element.23.bottom_hbm) | copy-start | bytes 786436

commit v3 on v2

--- a/solution.py
+++ b/solution.py
@@ -19,7 +19,7 @@
 
 CHUNK = 512
 CHUNKS = FF // CHUNK
-BLOCK = 256
+BLOCK = 512
 BLOCKS = TOKENS // BLOCK
 AHEAD = 2
 PIECES = 4
@@ -48,7 +48,7 @@
 
 
 def params(mib):
-    return pltpu.CompilerParams(vmem_limit_bytes=mib * 2**20)
+    return pltpu.CompilerParams(vmem_limit_bytes=int(mib * 2**20))
 
 
 def cost(flops, moved):
@@ -98,18 +98,26 @@
     def chunk_of(c):
         return pl.ds(pl.multiple_of(c * CHUNK, CHUNK), CHUNK)
 
-    def start(c):
+    def start_expand(c):
         pltpu.make_async_copy(
             expand_hbm.at[:, chunk_of(c)], expand.at[c], expand_sem.at[c]
         ).start()
+
+    def start(c):
+        if not isinstance(c, int) or c > 0:
+            start_expand(c)
         pltpu.make_async_copy(
             contract_hbm.at[chunk_of(c), :], contract.at[c], contract_sem.at[c]
         ).start()
 
-    def wait(c):
+    def wait_expand(c):
         pltpu.make_async_copy(
             expand_hbm.at[:, chunk_of(c)], expand.at[c], expand_sem.at[c]
         ).wait()
+
+    def wait(c):
+        if not isinstance(c, int) or c > 0:
+            wait_expand(c)
         pltpu.make_async_copy(
             contract_hbm.at[chunk_of(c), :], contract.at[c], contract_sem.at[c]
         ).wait()
@@ -120,11 +128,10 @@
         )
 
     state_copy(0).start()
-    start(0)
+    start_expand(0)
     for m in range(1, BLOCKS):
         state_copy(m).start()
-    for c in range(1, AHEAD):
-        start(c)
+    start(0)
 
     owner_pad[...] = jnp.full((8, NPAD), -4096, jnp.int32)
     owner_pad[0:1, 0:NODES] = owner_ref[...]
@@ -149,47 +156,57 @@
     member[...] = mask.astype(bf16)
     counts = jnp.maximum(jnp.sum(mask, axis=1, keepdims=True), 1.0)
 
+
     def first(c, m):
         return dot(states[block_of(m), :], expand[c])
 
-    def second(c, m, values):
+    def second(c, m, values, opening):
         acted = 0.5 * values * (1.0 + lax.erf(values * ROOT_HALF))
-        total[block_of(m), :] += dot(acted.astype(bf16), contract[c])
+        product = dot(acted.astype(bf16), contract[c])
+        total[block_of(m), :] = product if opening else total[block_of(m), :] + product
 
     buffers = (hidden_a, hidden_b)
-    for m in range(BLOCKS):
-        state_copy(m).wait()
-        total[block_of(m), :] = states[block_of(m), :].astype(f32)
-        if m == 0:
-            wait(0)
-            hidden_a[...] = first(0, 0)
-
-    def step(c, carry):
-        @pl.when(c + AHEAD < CHUNKS)
-        def _():
-            start(c + AHEAD)
-
-        wait(c + 1)
+
+    def step(c, opening=False, closing=False):
         for m in range(BLOCKS):
             now, later = buffers[m % 2], buffers[(m + 1) % 2]
             if m + 1 < BLOCKS:
                 later[...] = first(c, m + 1)
-            else:
+            elif not closing:
+                if opening:
+                    start(2)
+                    wait(1)
                 later[...] = first(c + 1, 0)
-            second(c, m, now[...])
-        return carry
-
-    lax.fori_loop(0, CHUNKS - 1, step, 0)
-
-    for m in range(BLOCKS):
-        now, later = buffers[m % 2], buffers[(m + 1) % 2]
-        if m + 1 < BLOCKS:
-            later[...] = first(CHUNKS - 1, m + 1)
-        second(CHUNKS - 1, m, now[...])
-        mixed = total[block_of(m), :]
+            second(c, m, now[...], opening)
+            if closing:
+                settle(m)
+
+    def settle(m):
+        mixed = total[block_of(m), :] + states[block_of(m), :].astype(f32)
         centred = mixed - jnp.mean(mixed, axis=1, keepdims=True)
         variance = jnp.mean(centred * centred, axis=1, keepdims=True)
         normed[block_of(m), :] = (centred * lax.rsqrt(variance + EPS)).astype(bf16)
+
+    state_copy(0).wait()
+    wait_expand(0)
+    start(1)
+    hidden_a[...] = first(0, 0)
+    for m in range(1, BLOCKS):
+        state_copy(m).wait()
+    wait(0)
+    step(0, opening=True)
+
+    def middle_step(c, carry):
+        @pl.when(c + AHEAD < CHUNKS)
+        def _():
+            start(c + AHEAD)
+
+        wait(c + 1)
+        step(c)
+        return carry
+
+    lax.fori_loop(1, CHUNKS - 1, middle_step, 0)
+    step(CHUNKS - 1, closing=True)
     summed = dot(member[...], normed[...])
     embeds = (summed / counts).astype(bf16)
     stacked = jnp.concatenate([embeds[:, :HALF], embeds[:, HALF:]], axis=0)
@@ -229,30 +246,70 @@
     )(upper, owner, node_ids, states, expand_weight, contract_weight)
 
 
-def prepare_kernel(
-    columns_ref,
-    count_ref,
-    values_ref,
-    cotangent_ref,
-    weight_ref,
-    mix_ref,
-    mix_t_ref,
-    band_ref,
-    inner_ref,
-    low_ref,
-    high_ref,
-    band_t,
-):
-    band_ref[...] = jnp.zeros((SLOTS, 2 * SLOTS), bf16)
-    band_t[...] = jnp.zeros((2 * SLOTS, SLOTS), bf16)
+def fill_band(columns_ref, count_ref, values_ref, band, transposed):
+    band[...] = jnp.zeros(band.shape, bf16)
     for r in range(2):
         for c in range(r, r + 3):
             tile = jnp.zeros((TILE, TILE), f32)
             for s in range(3):
                 used = (s < count_ref[0, r]) & (columns_ref[0, r, s] == c)
                 tile += jnp.where(used, 1.0, 0.0) * values_ref[0, r, s].astype(f32)
-            band_ref[r * TILE : (r + 1) * TILE, c * TILE : (c + 1) * TILE] = tile.astype(bf16)
-            band_t[c * TILE : (c + 1) * TILE, r * TILE : (r + 1) * TILE] = tile.T.astype(bf16)
+            rows, lanes = slice(r * TILE, (r + 1) * TILE), slice(c * TILE, (c + 1) * TILE)
+            if transposed:
+                band[lanes, rows] = tile.T.astype(bf16)
+            else:
+                band[rows, lanes] = tile.astype(bf16)
+
+
+def spread_kernel(
+    columns_ref, count_ref, values_ref, cotangent_ref, weight_ref, low_ref, high_ref, inner_hbm, band_t, inner, sem
+):
+    fill_band(columns_ref, count_ref, values_ref, band_t, True)
+    grad_mix = dot_t(cotangent_ref[...], weight_ref[...]).astype(bf16)
+    inner[...] = dot(band_t[TILE : TILE + SLOTS, :], grad_mix)
+    copy = pltpu.make_async_copy(inner, inner_hbm, sem)
+    copy.start()
+    low_ref[...] = dot(band_t[:TILE, :], grad_mix).astype(bf16)
+    high_ref[...] = dot(band_t[TILE + SLOTS :, :], grad_mix).astype(bf16)
+    copy.wait()
+
+
+def spread(columns, counts, values, cotangent, weight):
+    return pl.pallas_call(
+        spread_kernel,
+        out_shape=(
+            jax.ShapeDtypeStruct((TILE, D), bf16),
+            jax.ShapeDtypeStruct((TILE, D), bf16),
+            jax.ShapeDtypeStruct((SLOTS, D), f32),
+        ),
+        in_specs=[SMEM, SMEM, VMEM, VMEM, VMEM],
+        out_specs=(VMEM, VMEM, ANY),
+        scratch_shapes=[
+            pltpu.VMEM((2 * SLOTS, SLOTS), bf16),
+            pltpu.VMEM((SLOTS, D), f32),
+            pltpu.SemaphoreType.DMA,
+        ],
+        compiler_params=params(63.9),
+        cost_estimate=cost(10**9, 5 * 2**20),
+        name="spread",
+    )(columns, counts, values, cotangent, weight)
+
+
+def prepare_kernel(
+    columns_ref,
+    count_ref,
+    values_ref,
+    order_ref,
+    mix_hbm,
+    mix_t_hbm,
+    band_ref,
+    band_t,
+    mix,
+    mix_t,
+    sems,
+):
+    fill_band(columns_ref, count_ref, values_ref, band_ref, False)
+    fill_band(columns_ref, count_ref, values_ref, band_t, True)
 
     def place(column, u):
         peer, slot = column >> 3, column & 3
@@ -263,35 +320,39 @@
     shape = (2 * SLOTS, ROWS)
     for u in range(2):
         moved = jnp.where(iota(shape, 0) == place(iota((1, ROWS), 1), u), 1.0, 0.0)
-        mix_ref[u * SLOTS : (u + 1) * SLOTS, :] = dot(band_ref[...], moved.astype(bf16)).astype(bf16)
+        mix[u * SLOTS : (u + 1) * SLOTS, :] = dot(band_ref[...], moved.astype(bf16)).astype(bf16)
         back = jnp.where(iota(shape[::-1], 1) == place(iota((ROWS, 1), 0), u), 1.0, 0.0)
-        mix_t_ref[:, u * SLOTS : (u + 1) * SLOTS] = dot(back.astype(bf16), band_t[...]).astype(bf16)
-
-    grad_mix = dot_t(cotangent_ref[...], weight_ref[...]).astype(bf16)
-    spread = dot(band_t[...], grad_mix)
-    low_ref[...] = spread[:TILE].astype(bf16)
-    inner_ref[...] = spread[TILE : TILE + SLOTS]
-    high_ref[...] = spread[TILE + SLOTS :].astype(bf16)
-
-
-def prepare(columns, counts, values, cotangent, weight):
+        mix_t[:, u * SLOTS : (u + 1) * SLOTS] = dot(back.astype(bf16), band_t[...]).astype(bf16)
+    copies = [
+        pltpu.make_async_copy(mix, mix_hbm, sems.at[0]),
+        pltpu.make_async_copy(mix_t, mix_t_hbm, sems.at[1]),
+    ]
+    for copy in copies:
+        copy.start()
+    for copy in copies:
+        copy.wait()
+
+
+def prepare(columns, counts, values, order):
     return pl.pallas_call(
         prepare_kernel,
         out_shape=(
             jax.ShapeDtypeStruct((2 * SLOTS, ROWS), bf16),
             jax.ShapeDtypeStruct((ROWS, 2 * SLOTS), bf16),
             jax.ShapeDtypeStruct((SLOTS, 2 * SLOTS), bf16),
-            jax.ShapeDtypeStruct((SLOTS, D), f32),
-            jax.ShapeDtypeStruct((TILE, D), bf16),
-            jax.ShapeDtypeStruct((TILE, D), bf16),
         ),
-        in_specs=[SMEM, SMEM, VMEM, VMEM, VMEM],
-        out_specs=(VMEM,) * 6,
-        scratch_shapes=[pltpu.VMEM((2 * SLOTS, SLOTS), bf16)],
-        compiler_params=params(40),
-        cost_estimate=cost(2 * 10**9, 10 * 2**20),
+        in_specs=[SMEM, SMEM, VMEM, ANY],
+        out_specs=(ANY, ANY, VMEM),
+        scratch_shapes=[
+            pltpu.VMEM((2 * SLOTS, SLOTS), bf16),
+            pltpu.VMEM((2 * SLOTS, ROWS), bf16),
+            pltpu.VMEM((ROWS, 2 * SLOTS), bf16),
+            pltpu.SemaphoreType.DMA((2,)),
+        ],
+        compiler_params=params(63.9),
+        cost_estimate=cost(10**9, 4 * 2**20),
         name="prepare",
-    )(columns, counts, values, cotangent, weight)
+    )(columns, counts, values, order)
 
 
 def middle_kernel(
@@ -371,7 +432,7 @@
         scratch_shapes=[pltpu.VMEM((SLOTS, D), bf16), pltpu.VMEM((ROWS, HALF), bf16)]
         + [pltpu.VMEM(a.shape, a.dtype) for a in arrays]
         + [pltpu.SemaphoreType.DMA((n,)) for n in (7, 2, PIECES)],
-        compiler_params=params(62),
+        compiler_params=params(63.9),
         cost_estimate=cost(3 * 10**9, 8 * 2**20),
         name="middle",
     )(*arrays)
@@ -466,9 +527,8 @@
     )
     arrived = swap(outgoing)
     target, later_cotangent = lax.optimization_barrier((target, output_cotangent))
-    mix, mix_t, band, inner, low, high = prepare(
-        tile_columns, tile_count, tile_values, later_cotangent, second_weight
-    )
+    low, high, inner = spread(tile_columns, tile_count, tile_values, later_cotangent, second_weight)
+    mix, mix_t, band = prepare(tile_columns, tile_count, tile_values, inner)
     from_right = lax.ppermute(low, "dom", leftward)
     from_left = lax.ppermute(high, "dom", rightward)
     top, bottom, grads = middle(arrived, mix, first_weight, inner, from_left, from_right, mix_t)

time: 92.6 us -> 91.4 us (0.987)
  Pallas kernels: 37.6 us -> 43.5 us
  waiting for transfers between devices: 18 us -> 14.6 us
  local copies, waits for them, and re-layouts: 4.87 us -> 2.86 us
  starting transfers between devices: 30.9 us -> 29.3 us
    pallas_call x0 -> x1, Pallas kernels: none -> 4.58 us  [spread(): pl.pallas_call(spread_kernel, out_shape=(jax.ShapeDtypeStruct((TILE, D),...]
    ppermute x1, waiting for transfers between devices: 4.07 us -> 1.49 us  [local(): from_right = lax.ppermute(low, 'dom', leftward)]
    unnamed x28 -> x10, local copies, waits for them, and re-layouts: 4.87 us -> 2.86 us
    ppermute x1, waiting for transfers between devices: 1.91 us -> 0.01 us  [local(): from_left = lax.ppermute(high, 'dom', rightward)]
    pallas_call x1, Pallas kernels: 2.88 us -> 4.68 us  [prepare(): pl.pallas_call(prepare_kernel, out_shape=(jax.ShapeDtypeStruct((2 * SLOTS...]
    all_to_all x2, starting transfers between devices: 19.8 us -> 18.2 us  [swap(): lax.all_to_all(rows.reshape(PEERS, 8, HALF), ('enc', 'dom'), split_axis=0...]
    all_to_all x2, waiting for transfers between devices: 1.48 us -> 2.56 us  [swap(): lax.all_to_all(rows.reshape(PEERS, 8, HALF), ('enc', 'dom'), split_axis=0...]
  transfers between devices with their start and end apart: 6 -> 6, of which waited for: 5 -> 4; matrix products, arithmetic and copies ran while one was open for 0% -> 0% of each run, Pallas kernels for 6% -> 13%
where the time goes in v3:
time: 91.4 us; the launch traced here: 90.9 us
  Pallas kernels  43.5 us (48%)
  starting transfers between devices  29.3 us (32%)
  waiting for transfers between devices  14.6 us (16%)
  local copies, waits for them, and re-layouts  2.86 us (3%)
    pallas_call x1, Pallas kernels, encode(): pl.pallas_call(encode_kernel, out_shape=(jax.ShapeDtypeStruct((ROWS, HALF...  24.9 us
    all_to_all x2, starting transfers between devices, swap(): lax.all_to_all(rows.reshape(PEERS, 8, HALF), ('enc', 'dom'), split_axis=0...  18.2 us
    ppermute x1, waiting for transfers between devices, local(): left = lax.ppermute(bottom, 'dom', rightward)  8.52 us
    pallas_call x1, Pallas kernels, middle(): pl.pallas_call(middle_kernel, out_shape=(jax.ShapeDtypeStruct((TILE, D),...  5.6 us
    pallas_call x1, Pallas kernels, prepare(): pl.pallas_call(prepare_kernel, out_shape=(jax.ShapeDtypeStruct((2 * SLOTS...  4.68 us
    pallas_call x1, Pallas kernels, spread(): pl.pallas_call(spread_kernel, out_shape=(jax.ShapeDtypeStruct((TILE, D),...  4.58 us
    ppermute x1, starting transfers between devices, local(): left = lax.ppermute(bottom, 'dom', rightward)  3.54 us
    ppermute x1, starting transfers between devices, local(): from_left = lax.ppermute(high, 'dom', rightward)  3.53 us
  transfers between devices with their start and end apart: 6, of which 4 were waited for; matrix products, arithmetic and copies ran while one was open for 0% of the time, Pallas kernels for 13%

profile of v3, /device:TPU:1, one launch (start us, length us, event | category | flops | bytes accessed | tf_op | source)
XLA Modules:
  0.0 90.9 jit_solution(4905544205813905050)
XLA Ops:
  0.6 24.9 %encode.1 = (bf16[1024,512]{1,0:T(8,128)(2,1)}, s32[8,256]{1,0:T(8,128)}) custom-call(s32[1]{0:T(128)} %bitcast.upper_ref, s32[1,192]{1,0:T(1,128)} %bitcast.9, s32[1,1024]{1,0:T(1,128)} %node_ref.1, bf16[1024,1024]{1,0:T(8,128)(2,1)} %states_hbm.1, bf16[1024,4096]{1,0:T(8,128)(2,1)} %expand_hbm.1, bf16[4096,1024]{1,0:T(8,128)(2,1)} %contract_hbm.1), custom_call_target="tpu_custom_call" | custom-call | flops 17179869184 | bytes 20971520 | tf_op jit(solution)/shard_map/encode/pallas_call | solution.py:218
  25.6 12.0 %all-to-all-start = ((bf16[128,8,512]{2,1,0:T(8,128)(2,1)}), bf16[128,8,512]{2,1,0:T(8,128)(2,1)}, u32[]{:S(2)}, u32[]{:S(2)}) async-start(bf16[128,8,512]{2,1,0:T(8,128)(2,1)} %bitcast.7), calls=%async_computation | async-start | bytes 2097152 | tf_op jit(solution)/shard_map/all_to_all | solution.py:503
  37.5 4.6 %spread.1 = (bf16[128,1024]{1,0:T(8,128)(2,1)}, bf16[128,1024]{1,0:T(8,128)(2,1)}, f32[256,1024]{1,0:T(8,128)}) custom-call(s32[1,2,3]{2,1,0:T(2,128)} %columns_ref.3, s32[1,2]{1,0:T(1,128)} %count_ref.3, bf16[1,2,3,128,128]{4,3,2,1,0:T(8,128)(2,1)} %values_ref.3, bf16[256,1024]{1,0:T(8,128)(2,1)} %cotangent_ref, bf16[1024,1024]{1,0:T(8,128)(2,1)} %weight_hbm.3), custom_call_target="tpu_custom_call" | custom-call | flops 1000000000 | bytes 5242880 | tf_op jit(solution)/shard_map/spread/pallas_call | solution.py:278
  42.1 3.5 %collective-permute-start = (bf16[128,1024]{1,0:T(8,128)(2,1)}, bf16[128,1024]{1,0:T(8,128)(2,1)}, u32[]{:S(2)}, u32[]{:S(2)}) collective-permute-start(bf16[128,1024]{1,0:T(8,128)(2,1)} %get-tuple-element.20), channel_id=1, source_target_pairs={{0,1},{1,2},{2,3},{3,4},{4,5},{5,6},{6,7},{8,9},{9,10},{10,11},{11... | collective-permute-start | bytes 786440 | tf_op jit(solution)/shard_map/ppermute | solution.py:533
  45.7 2.1 %collective-permute-start.1 = (bf16[128,1024]{1,0:T(8,128)(2,1)}, bf16[128,1024]{1,0:T(8,128)(2,1)}, u32[]{:S(2)}, u32[]{:S(2)}) collective-permute-start(bf16[128,1024]{1,0:T(8,128)(2,1)} %get-tuple-element.21), channel_id=1, source_target_pairs={{1,0},{2,1},{3,2},{4,3},{5,4},{6,5},{7,6},{9,8},{10,9},{11,10},{12... | collective-permute-start | bytes 786440 | tf_op jit(solution)/shard_map/ppermute | solution.py:532
  47.8 4.7 %prepare.1 = (bf16[512,1024]{1,0:T(8,128)(2,1)}, bf16[1024,512]{1,0:T(8,128)(2,1)}, bf16[256,512]{1,0:T(8,128)(2,1)}) custom-call(s32[1,2,3]{2,1,0:T(2,128)} %columns_ref.3, s32[1,2]{1,0:T(1,128)} %count_ref.3, bf16[1,2,3,128,128]{4,3,2,1,0:T(8,128)(2,1)} %values_ref.3, f32[256,1024]{1,0:T(8,128)} %get-tuple-element.18.order_ref.inner_hbm), custom_call_target="tpu_custom_call" | custom-call | flops 1000000000 | bytes 4194304 | tf_op jit(solution)/shard_map/prepare/pallas_call | solution.py:337
  52.5 0.0 collective-permute-done.left_hbm
  52.5 1.5 %collective-permute-done.1.right_hbm = bf16[128,1024]{1,0:T(8,128)(2,1)} collective-permute-done((bf16[128,1024]{1,0:T(8,128)(2,1)}, bf16[128,1024]{1,0:T(8,128)(2,1)}, u32[]{:S(2)}, u32[]{:S(2)}) %collective-permute-start.1) | collective-permute-done | bytes 262176 | tf_op jit(solution)/shard_map/ppermute | solution.py:532
  54.0 2.6 %all-to-all-done = bf16[128,8,512]{2,1,0:T(8,128)(2,1)} async-done(((bf16[128,8,512]{2,1,0:T(8,128)(2,1)}), bf16[128,8,512]{2,1,0:T(8,128)(2,1)}, u32[]{:S(2)}, u32[]{:S(2)}) %all-to-all-start) | async-done | bytes 1048608 | tf_op jit(solution)/shard_map/all_to_all | solution.py:503
  56.5 5.6 %middle.1 = (bf16[128,1024]{1,0:T(8,128)(2,1)}, bf16[128,1024]{1,0:T(8,128)(2,1)}, bf16[1024,512]{1,0:T(8,128)(2,1)}) custom-call(bf16[1024,512]{1,0:T(8,128)(2,1)} %bitcast.3.rows_hbm, bf16[512,1024]{1,0:T(8,128)(2,1)} %get-tuple-element.19.mix_hbm, bf16[1024,1024]{1,0:T(8,128)(2,1)} %weight_hbm.2, f32[256,1024]{1,0:T(8,128)} %get-tuple-element.18.order_ref.inner_hbm, ...), custom_call_target="tpu_custom_call" | custom-call | flops 3000000000 | bytes 8388608 | tf_op jit(solution)/shard_map/middle/pallas_call | solution.py:423
  62.1 0.0 copy-start
  62.2 0.0 copy-start.4
  62.2 6.2 %all-to-all-start.1 = ((bf16[128,8,512]{2,1,0:T(8,128)(2,1)}), bf16[128,8,512]{2,1,0:T(8,128)(2,1)S(1)}, u32[]{:S(2)}, u32[]{:S(2)}) async-start(bf16[128,8,512]{2,1,0:T(8,128)(2,1)} %bitcast.8), calls=%async_computation.1 | async-start | bytes 2097152 | tf_op jit(solution)/shard_map/all_to_all | solution.py:503
  68.4 3.5 %collective-permute-start.2 = (bf16[128,1024]{1,0:T(8,128)(2,1)}, bf16[128,1024]{1,0:T(8,128)(2,1)S(1)}, u32[]{:S(2)}, u32[]{:S(2)}) collective-permute-start(bf16[128,1024]{1,0:T(8,128)(2,1)} %get-tuple-element.23.bottom_hbm), channel_id=1, source_target_pairs={{0,1},{1,2},{2,3},{3,4},{4,5},{5,6},{6,7},{8,9},{9,10},{10,11},{11... | collective-permute-start | bytes 786440 | tf_op jit(solution)/shard_map/ppermute | solution.py:536
  71.9 1.9 %collective-permute-start.3 = (bf16[128,1024]{1,0:T(8,128)(2,1)}, bf16[128,1024]{1,0:T(8,128)(2,1)S(1)}, u32[]{:S(2)}, u32[]{:S(2)}) collective-permute-start(bf16[128,1024]{1,0:T(8,128)(2,1)} %get-tuple-element.24.top_hbm), channel_id=1, source_target_pairs={{1,0},{2,1},{3,2},{4,3},{5,4},{6,5},{7,6},{9,8},{10,9},{11,10},{12... | collective-permute-start | bytes 786440 | tf_op jit(solution)/shard_map/ppermute | solution.py:537
  73.8 8.5 %collective-permute-done.2.left_hbm = bf16[128,1024]{1,0:T(8,128)(2,1)S(1)} collective-permute-done((bf16[128,1024]{1,0:T(8,128)(2,1)}, bf16[128,1024]{1,0:T(8,128)(2,1)S(1)}, u32[]{:S(2)}, u32[]{:S(2)}) %collective-permute-start.2) | collective-permute-done | bytes 262176 | tf_op jit(solution)/shard_map/ppermute | solution.py:536
  82.4 2.0 %collective-permute-done.3.right_hbm = bf16[128,1024]{1,0:T(8,128)(2,1)S(1)} collective-permute-done((bf16[128,1024]{1,0:T(8,128)(2,1)}, bf16[128,1024]{1,0:T(8,128)(2,1)S(1)}, u32[]{:S(2)}, u32[]{:S(2)}) %collective-permute-start.3) | collective-permute-done | bytes 262176 | tf_op jit(solution)/shard_map/ppermute | solution.py:537
  84.4 0.0 copy-done
  84.4 0.9 %copy-done.1 = bf16[256,512]{1,0:T(8,128)(2,1)S(1)} copy-done((bf16[256,512]{1,0:T(8,128)(2,1)S(1)}, bf16[256,512]{1,0:T(8,128)(2,1)}, u32[]{:S(2)}) %copy-start.1) | copy-done | bytes 262168
  85.3 0.9 %copy-done.2 = bf16[128,1024]{1,0:T(8,128)(2,1)S(1)} copy-done((bf16[128,1024]{1,0:T(8,128)(2,1)S(1)}, bf16[128,1024]{1,0:T(8,128)(2,1)}, u32[]{:S(2)}) %copy-start.2) | copy-done | bytes 262168
  86.3 0.9 %copy-done.3 = bf16[128,1024]{1,0:T(8,128)(2,1)S(1)} copy-done((bf16[128,1024]{1,0:T(8,128)(2,1)S(1)}, bf16[128,1024]{1,0:T(8,128)(2,1)}, u32[]{:S(2)}) %copy-start.3) | copy-done | bytes 262168
  87.2 2.2 %finish.1 = bf16[256,1024]{1,0:T(8,128)(2,1)} custom-call(bf16[128,1024]{1,0:T(8,128)(2,1)S(1)} %collective-permute-done.2.left_hbm, bf16[128,1024]{1,0:T(8,128)(2,1)S(1)} %copy-done.2, bf16[128,1024]{1,0:T(8,128)(2,1)S(1)} %copy-done.3, bf16[128,1024]{1,0:T(8,128)(2,1)S(1)} %collective-permute-done.3.right_hbm, bf16[256,512]{1,0:T(8,128)(2,1)S(1)} %copy-done.1, ...), custom_call_target="tpu_custom_call" | custom-call | flops 1000000000 | bytes 5242880 | tf_op jit(solution)/shard_map/finish/pallas_call | solution.py:459
  89.5 0.0 all-to-all-done.1
  89.5 1.4 %gather.1 = bf16[192,1024]{1,0:T(8,128)(2,1)} custom-call(s32[8,256]{1,0:T(8,128)S(1)} %copy-done.4, bf16[1024,512]{1,0:T(8,128)(2,1)S(1)} %bitcast.6), custom_call_target="tpu_custom_call" | custom-call | flops 400000000 | bytes 2097152 | tf_op jit(solution)/shard_map/gather/pallas_call | solution.py:490
  (4 shorter events, 0.0 us)
Async XLA Ops:
  25.6 31.0 %all-to-all-start = ((bf16[128,8,512]{2,1,0:T(8,128)(2,1)}), bf16[128,8,512]{2,1,0:T(8,128)(2,1)}, u32[]{:S(2)}, u32[]{:S(2)}) async-start(bf16[128,8,512]{2,1,0:T(8,128)(2,1)} %bitcast.7), calls=%async_computation | async-start | bytes 2097152 | tf_op jit(solution)/shard_map/all_to_all | solution.py:503
  42.1 10.3 %collective-permute-start = (bf16[128,1024]{1,0:T(8,128)(2,1)}, bf16[128,1024]{1,0:T(8,128)(2,1)}, u32[]{:S(2)}, u32[]{:S(2)}) collective-permute-start(bf16[128,1024]{1,0:T(8,128)(2,1)} %get-tuple-element.20), channel_id=1, source_target_pairs={{0,1},{1,2},{2,3},{3,4},{4,5},{5,6},{6,7},{8,9},{9,10},{10,11},{11... | collective-permute-start | bytes 786440 | tf_op jit(solution)/shard_map/ppermute | solution.py:533
  45.7 8.3 %collective-permute-start.1 = (bf16[128,1024]{1,0:T(8,128)(2,1)}, bf16[128,1024]{1,0:T(8,128)(2,1)}, u32[]{:S(2)}, u32[]{:S(2)}) collective-permute-start(bf16[128,1024]{1,0:T(8,128)(2,1)} %get-tuple-element.21), channel_id=1, source_target_pairs={{1,0},{2,1},{3,2},{4,3},{5,4},{6,5},{7,6},{9,8},{10,9},{11,10},{12... | collective-permute-start | bytes 786440 | tf_op jit(solution)/shard_map/ppermute | solution.py:532
  62.1 22.2 %copy-start = (bf16[1024,1024]{1,0:T(8,128)(2,1)S(1)}, bf16[1024,1024]{1,0:T(8,128)(2,1)}, u32[]{:S(2)}) copy-start(bf16[1024,1024]{1,0:T(8,128)(2,1)} %weight_hbm.3) | copy-start | bytes 6291460
  62.2 27.3 %copy-start.4 = (s32[8,256]{1,0:T(8,128)S(1)}, s32[8,256]{1,0:T(8,128)}, u32[]{:S(2)}) copy-start(s32[8,256]{1,0:T(8,128)} %get-tuple-element.26.target_ref) | copy-start | bytes 24580
  62.2 27.3 %all-to-all-start.1 = ((bf16[128,8,512]{2,1,0:T(8,128)(2,1)}), bf16[128,8,512]{2,1,0:T(8,128)(2,1)S(1)}, u32[]{:S(2)}, u32[]{:S(2)}) async-start(bf16[128,8,512]{2,1,0:T(8,128)(2,1)} %bitcast.8), calls=%async_computation.1 | async-start | bytes 2097152 | tf_op jit(solution)/shard_map/all_to_all | solution.py:503
  68.4 14.0 %collective-permute-start.2 = (bf16[128,1024]{1,0:T(8,128)(2,1)}, bf16[128,1024]{1,0:T(8,128)(2,1)S(1)}, u32[]{:S(2)}, u32[]{:S(2)}) collective-permute-start(bf16[128,1024]{1,0:T(8,128)(2,1)} %get-tuple-element.23.bottom_hbm), channel_id=1, source_target_pairs={{0,1},{1,2},{2,3},{3,4},{4,5},{5,6},{6,7},{8,9},{9,10},{10,11},{11... | collective-permute-start | bytes 786440 | tf_op jit(solution)/shard_map/ppermute | solution.py:536
  71.9 12.5 %collective-permute-start.3 = (bf16[128,1024]{1,0:T(8,128)(2,1)}, bf16[128,1024]{1,0:T(8,128)(2,1)S(1)}, u32[]{:S(2)}, u32[]{:S(2)}) collective-permute-start(bf16[128,1024]{1,0:T(8,128)(2,1)} %get-tuple-element.24.top_hbm), channel_id=1, source_target_pairs={{1,0},{2,1},{3,2},{4,3},{5,4},{6,5},{7,6},{9,8},{10,9},{11,10},{12... | collective-permute-start | bytes 786440 | tf_op jit(solution)/shard_map/ppermute | solution.py:537
  84.4 1.0 %copy-start.1 = (bf16[256,512]{1,0:T(8,128)(2,1)S(1)}, bf16[256,512]{1,0:T(8,128)(2,1)}, u32[]{:S(2)}) copy-start(bf16[256,512]{1,0:T(8,128)(2,1)} %get-tuple-element.25.band_hbm) | copy-start | bytes 786436
  85.3 0.9 %copy-start.2 = (bf16[128,1024]{1,0:T(8,128)(2,1)S(1)}, bf16[128,1024]{1,0:T(8,128)(2,1)}, u32[]{:S(2)}) copy-start(bf16[128,1024]{1,0:T(8,128)(2,1)} %get-tuple-element.24.top_hbm) | copy-start | bytes 786436
  86.3 0.9 %copy-start.3 = (bf16[128,1024]{1,0:T(8,128)(2,1)S(1)}, bf16[128,1024]{1,0:T(8,128)(2,1)}, u32[]{:S(2)}) copy-start(bf16[128,1024]{1,0:T(8,128)(2,1)} %get-tuple-element.23.bottom_hbm) | copy-start | bytes 786436

commit v4 on v3

--- a/solution.py
+++ b/solution.py
@@ -438,35 +438,55 @@
     )(*arrays)
 
 
-def finish_kernel(left_hbm, top_hbm, bottom_hbm, right_hbm, band_hbm, weight_hbm, out_ref, wide, band, weight, sems):
-    sources = (left_hbm, top_hbm, bottom_hbm, right_hbm)
+def own_part_kernel(
+    top_hbm, bottom_hbm, band_hbm, part_ref, first_ref, last_ref, acts, band, sems
+):
     copies = [
-        pltpu.make_async_copy(a, wide.at[pl.ds(i * TILE, TILE), :], sems.at[i])
-        for i, a in enumerate(sources)
+        pltpu.make_async_copy(top_hbm, acts.at[pl.ds(0, TILE), :], sems.at[0]),
+        pltpu.make_async_copy(bottom_hbm, acts.at[pl.ds(TILE, TILE), :], sems.at[1]),
+        pltpu.make_async_copy(band_hbm, band, sems.at[2]),
     ]
-    copies.append(pltpu.make_async_copy(band_hbm, band, sems.at[4]))
-    copies.append(pltpu.make_async_copy(weight_hbm, weight, sems.at[5]))
     for copy in copies:
         copy.start()
-    for copy in copies[:5]:
+    for copy in copies:
         copy.wait()
-    mixed = dot(band[...], wide[...]).astype(bf16)
-    copies[5].wait()
-    out_ref[...] = dot(mixed, weight[...]).astype(bf16)
+    part_ref[...] = dot(band[:, TILE : TILE + SLOTS], acts[...])
+    first_ref[...] = band[:, :TILE]
+    last_ref[...] = band[:, TILE + SLOTS :]
+
+
+def own_part(*arrays):
+    return pl.pallas_call(
+        own_part_kernel,
+        out_shape=(
+            jax.ShapeDtypeStruct((SLOTS, D), f32),
+            jax.ShapeDtypeStruct((SLOTS, TILE), bf16),
+            jax.ShapeDtypeStruct((SLOTS, TILE), bf16),
+        ),
+        in_specs=[ANY] * 3,
+        out_specs=(VMEM,) * 3,
+        scratch_shapes=[
+            pltpu.VMEM((SLOTS, D), bf16),
+            pltpu.VMEM((SLOTS, 2 * SLOTS), bf16),
+            pltpu.SemaphoreType.DMA((3,)),
+        ],
+        compiler_params=params(16),
+        cost_estimate=cost(2 * 10**8, 3 * 2**20),
+        name="own_part",
+    )(*arrays)
+
+
+def finish_kernel(part_ref, first_ref, last_ref, left_ref, right_ref, weight_ref, out_ref):
+    mixed = part_ref[...] + dot(first_ref[...], left_ref[...]) + dot(last_ref[...], right_ref[...])
+    out_ref[...] = dot(mixed.astype(bf16), weight_ref[...]).astype(bf16)
 
 
 def finish(*arrays):
     return pl.pallas_call(
         finish_kernel,
         out_shape=jax.ShapeDtypeStruct((SLOTS, D), bf16),
-        in_specs=[ANY] * 6,
+        in_specs=[VMEM] * 6,
         out_specs=VMEM,
-        scratch_shapes=[
-            pltpu.VMEM((2 * SLOTS, D), bf16),
-            pltpu.VMEM((SLOTS, 2 * SLOTS), bf16),
-            pltpu.VMEM((D, D), bf16),
-            pltpu.SemaphoreType.DMA((6,)),
-        ],
         compiler_params=params(16),
         cost_estimate=cost(10**9, 5 * 2**20),
         name="finish",
@@ -535,7 +555,8 @@
     returned = swap(grads)
     left = lax.ppermute(bottom, "dom", rightward)
     right = lax.ppermute(top, "dom", leftward)
-    graph_output = finish(left, top, bottom, right, band, second_weight)
+    part, first, last = own_part(top, bottom, band)
+    graph_output = finish(part, first, last, left, right, second_weight)
     return (graph_output, gather(target, returned))
 
 

time: 91.4 us -> 89.6 us (0.980)
  waiting for transfers between devices: 14.6 us -> 12.8 us
    ppermute x1, waiting for transfers between devices: 8.52 us -> 0.01 us  [local(): left = lax.ppermute(bottom, 'dom', rightward)]
    ppermute x1, waiting for transfers between devices: 2.01 us -> 7.16 us  [local(): right = lax.ppermute(top, 'dom', leftward)]
    all_to_all x2, waiting for transfers between devices: 2.56 us -> 4.12 us  [swap(): lax.all_to_all(rows.reshape(PEERS, 8, HALF), ('enc', 'dom'), split_axis=0...]
    ppermute x1, starting transfers between devices: 1.92 us -> 2.98 us  [local(): right = lax.ppermute(top, 'dom', leftward)]
    ppermute x1, starting transfers between devices: 3.54 us -> 2.59 us  [local(): left = lax.ppermute(bottom, 'dom', rightward)]
where the time goes in v4:
time: 89.6 us; the launch traced here: 89.1 us
  Pallas kernels  43.4 us (48%)
  starting transfers between devices  29.4 us (33%)
  waiting for transfers between devices  12.8 us (14%)
  local copies, waits for them, and re-layouts  2.85 us (3%)
    pallas_call x1, Pallas kernels, encode(): pl.pallas_call(encode_kernel, out_shape=(jax.ShapeDtypeStruct((ROWS, HALF...  24.9 us
    all_to_all x2, starting transfers between devices, swap(): lax.all_to_all(rows.reshape(PEERS, 8, HALF), ('enc', 'dom'), split_axis=0...  18.2 us
    ppermute x1, waiting for transfers between devices, local(): right = lax.ppermute(top, 'dom', leftward)  7.16 us
    pallas_call x1, Pallas kernels, middle(): pl.pallas_call(middle_kernel, out_shape=(jax.ShapeDtypeStruct((TILE, D),...  5.58 us
    pallas_call x1, Pallas kernels, prepare(): pl.pallas_call(prepare_kernel, out_shape=(jax.ShapeDtypeStruct((2 * SLOTS...  4.69 us
    pallas_call x1, Pallas kernels, spread(): pl.pallas_call(spread_kernel, out_shape=(jax.ShapeDtypeStruct((TILE, D),...  4.56 us
    all_to_all x2, waiting for transfers between devices, swap(): lax.all_to_all(rows.reshape(PEERS, 8, HALF), ('enc', 'dom'), split_axis=0...  4.12 us
    ppermute x1, starting transfers between devices, local(): from_left = lax.ppermute(high, 'dom', rightward)  3.55 us
  transfers between devices with their start and end apart: 6, of which 4 were waited for; matrix products, arithmetic and copies ran while one was open for 0% of the time, Pallas kernels for 13%

profile of v4, /device:TPU:1, one launch (start us, length us, event | category | flops | bytes accessed | tf_op | source)
XLA Modules:
  0.0 89.1 jit_solution(14245392953429172101)
XLA Ops:
  0.6 24.9 %encode.1 = (bf16[1024,512]{1,0:T(8,128)(2,1)}, s32[8,256]{1,0:T(8,128)}) custom-call(s32[1]{0:T(128)} %bitcast.upper_ref, s32[1,192]{1,0:T(1,128)} %bitcast.9, s32[1,1024]{1,0:T(1,128)} %node_ref.1, bf16[1024,1024]{1,0:T(8,128)(2,1)} %states_hbm.1, bf16[1024,4096]{1,0:T(8,128)(2,1)} %expand_hbm.1, bf16[4096,1024]{1,0:T(8,128)(2,1)} %contract_hbm.1), custom_call_target="tpu_custom_call" | custom-call | flops 17179869184 | bytes 20971520 | tf_op jit(solution)/shard_map/encode/pallas_call | solution.py:218
  25.6 12.0 %all-to-all-start = ((bf16[128,8,512]{2,1,0:T(8,128)(2,1)}), bf16[128,8,512]{2,1,0:T(8,128)(2,1)}, u32[]{:S(2)}, u32[]{:S(2)}) async-start(bf16[128,8,512]{2,1,0:T(8,128)(2,1)} %bitcast.8), calls=%async_computation | async-start | bytes 2097152 | tf_op jit(solution)/shard_map/all_to_all | solution.py:523
  37.6 4.6 %spread.1 = (bf16[128,1024]{1,0:T(8,128)(2,1)}, bf16[128,1024]{1,0:T(8,128)(2,1)}, f32[256,1024]{1,0:T(8,128)}) custom-call(s32[1,2,3]{2,1,0:T(2,128)} %columns_ref.3, s32[1,2]{1,0:T(1,128)} %count_ref.3, bf16[1,2,3,128,128]{4,3,2,1,0:T(8,128)(2,1)} %values_ref.3, bf16[256,1024]{1,0:T(8,128)(2,1)} %cotangent_ref, bf16[1024,1024]{1,0:T(8,128)(2,1)} %weight_ref.3), custom_call_target="tpu_custom_call" | custom-call | flops 1000000000 | bytes 5242880 | tf_op jit(solution)/shard_map/spread/pallas_call | solution.py:278
  42.1 3.6 %collective-permute-start = (bf16[128,1024]{1,0:T(8,128)(2,1)}, bf16[128,1024]{1,0:T(8,128)(2,1)}, u32[]{:S(2)}, u32[]{:S(2)}) collective-permute-start(bf16[128,1024]{1,0:T(8,128)(2,1)} %get-tuple-element.23), channel_id=1, source_target_pairs={{0,1},{1,2},{2,3},{3,4},{4,5},{5,6},{6,7},{8,9},{9,10},{10,11},{11... | collective-permute-start | bytes 786440 | tf_op jit(solution)/shard_map/ppermute | solution.py:553
  45.7 2.1 %collective-permute-start.1 = (bf16[128,1024]{1,0:T(8,128)(2,1)}, bf16[128,1024]{1,0:T(8,128)(2,1)}, u32[]{:S(2)}, u32[]{:S(2)}) collective-permute-start(bf16[128,1024]{1,0:T(8,128)(2,1)} %get-tuple-element.24), channel_id=1, source_target_pairs={{1,0},{2,1},{3,2},{4,3},{5,4},{6,5},{7,6},{9,8},{10,9},{11,10},{12... | collective-permute-start | bytes 786440 | tf_op jit(solution)/shard_map/ppermute | solution.py:552
  47.8 4.7 %prepare.1 = (bf16[512,1024]{1,0:T(8,128)(2,1)}, bf16[1024,512]{1,0:T(8,128)(2,1)}, bf16[256,512]{1,0:T(8,128)(2,1)}) custom-call(s32[1,2,3]{2,1,0:T(2,128)} %columns_ref.3, s32[1,2]{1,0:T(1,128)} %count_ref.3, bf16[1,2,3,128,128]{4,3,2,1,0:T(8,128)(2,1)} %values_ref.3, f32[256,1024]{1,0:T(8,128)} %get-tuple-element.21.order_ref.inner_hbm), custom_call_target="tpu_custom_call" | custom-call | flops 1000000000 | bytes 4194304 | tf_op jit(solution)/shard_map/prepare/pallas_call | solution.py:337
  52.5 0.0 collective-permute-done.left_hbm
  52.5 1.5 %collective-permute-done.1.right_hbm = bf16[128,1024]{1,0:T(8,128)(2,1)} collective-permute-done((bf16[128,1024]{1,0:T(8,128)(2,1)}, bf16[128,1024]{1,0:T(8,128)(2,1)}, u32[]{:S(2)}, u32[]{:S(2)}) %collective-permute-start.1) | collective-permute-done | bytes 262176 | tf_op jit(solution)/shard_map/ppermute | solution.py:552
  54.0 2.6 %all-to-all-done = bf16[128,8,512]{2,1,0:T(8,128)(2,1)} async-done(((bf16[128,8,512]{2,1,0:T(8,128)(2,1)}), bf16[128,8,512]{2,1,0:T(8,128)(2,1)}, u32[]{:S(2)}, u32[]{:S(2)}) %all-to-all-start) | async-done | bytes 1048608 | tf_op jit(solution)/shard_map/all_to_all | solution.py:523
  56.5 5.6 %middle.1 = (bf16[128,1024]{1,0:T(8,128)(2,1)}, bf16[128,1024]{1,0:T(8,128)(2,1)}, bf16[1024,512]{1,0:T(8,128)(2,1)}) custom-call(bf16[1024,512]{1,0:T(8,128)(2,1)} %bitcast.3.rows_hbm, bf16[512,1024]{1,0:T(8,128)(2,1)} %get-tuple-element.22.mix_hbm, bf16[1024,1024]{1,0:T(8,128)(2,1)} %weight_hbm.1, f32[256,1024]{1,0:T(8,128)} %get-tuple-element.21.order_ref.inner_hbm, ...), custom_call_target="tpu_custom_call" | custom-call | flops 3000000000 | bytes 8388608 | tf_op jit(solution)/shard_map/middle/pallas_call | solution.py:423
  62.1 0.0 copy-start
  62.1 6.2 %all-to-all-start.1 = ((bf16[128,8,512]{2,1,0:T(8,128)(2,1)}), bf16[128,8,512]{2,1,0:T(8,128)(2,1)S(1)}, u32[]{:S(2)}, u32[]{:S(2)}) async-start(bf16[128,8,512]{2,1,0:T(8,128)(2,1)} %bitcast.7), calls=%async_computation.1 | async-start | bytes 2097152 | tf_op jit(solution)/shard_map/all_to_all | solution.py:523
  68.3 3.0 %collective-permute-start.3 = (bf16[128,1024]{1,0:T(8,128)(2,1)}, bf16[128,1024]{1,0:T(8,128)(2,1)S(1)}, u32[]{:S(2)}, u32[]{:S(2)}) collective-permute-start(bf16[128,1024]{1,0:T(8,128)(2,1)} %get-tuple-element.26.top_hbm), channel_id=1, source_target_pairs={{1,0},{2,1},{3,2},{4,3},{5,4},{6,5},{7,6},{9,8},{10,9},{11,10},{12... | collective-permute-start | bytes 786440 | tf_op jit(solution)/shard_map/ppermute | solution.py:557
  71.3 2.6 %collective-permute-start.2 = (bf16[128,1024]{1,0:T(8,128)(2,1)}, bf16[128,1024]{1,0:T(8,128)(2,1)S(1)}, u32[]{:S(2)}, u32[]{:S(2)}) collective-permute-start(bf16[128,1024]{1,0:T(8,128)(2,1)} %get-tuple-element.27.bottom_hbm), channel_id=1, source_target_pairs={{0,1},{1,2},{2,3},{3,4},{4,5},{5,6},{6,7},{8,9},{9,10},{10,11},{11... | collective-permute-start | bytes 786440 | tf_op jit(solution)/shard_map/ppermute | solution.py:556
  73.9 0.9 %copy-done.1 = bf16[256,512]{1,0:T(8,128)(2,1)S(1)} copy-done((bf16[256,512]{1,0:T(8,128)(2,1)S(1)}, bf16[256,512]{1,0:T(8,128)(2,1)}, u32[]{:S(2)}) %copy-start.1) | copy-done | bytes 262168
  74.9 0.9 %copy-done.2 = bf16[128,1024]{1,0:T(8,128)(2,1)S(1)} copy-done((bf16[128,1024]{1,0:T(8,128)(2,1)S(1)}, bf16[128,1024]{1,0:T(8,128)(2,1)}, u32[]{:S(2)}) %copy-start.2) | copy-done | bytes 262168
  75.8 0.9 %copy-done.3 = bf16[128,1024]{1,0:T(8,128)(2,1)S(1)} copy-done((bf16[128,1024]{1,0:T(8,128)(2,1)S(1)}, bf16[128,1024]{1,0:T(8,128)(2,1)}, u32[]{:S(2)}) %copy-start.3) | copy-done | bytes 262168
  76.8 0.4 own_part.1
  77.2 7.2 %collective-permute-done.3.right_ref = bf16[128,1024]{1,0:T(8,128)(2,1)S(1)} collective-permute-done((bf16[128,1024]{1,0:T(8,128)(2,1)}, bf16[128,1024]{1,0:T(8,128)(2,1)S(1)}, u32[]{:S(2)}, u32[]{:S(2)}) %collective-permute-start.3) | collective-permute-done | bytes 262176 | tf_op jit(solution)/shard_map/ppermute | solution.py:557
  84.4 0.0 collective-permute-done.2.left_ref
  84.4 1.8 %finish.1 = bf16[256,1024]{1,0:T(8,128)(2,1)} custom-call(f32[256,1024]{1,0:T(8,128)S(1)} %get-tuple-element.29.part_ref, bf16[256,128]{1,0:T(8,128)(2,1)S(1)} %get-tuple-element.30.first_ref, bf16[256,128]{1,0:T(8,128)(2,1)S(1)} %get-tuple-element.31.last_ref, bf16[128,1024]{1,0:T(8,128)(2,1)S(1)} %collective-permute-done.2.left_ref, ...), custom_call_target="tpu_custom_call" | custom-call | flops 1000000000 | bytes 5242880 | tf_op jit(solution)/shard_map/finish/pallas_call | solution.py:485
  86.1 1.6 %all-to-all-done.1 = bf16[128,8,512]{2,1,0:T(8,128)(2,1)S(1)} async-done(((bf16[128,8,512]{2,1,0:T(8,128)(2,1)}), bf16[128,8,512]{2,1,0:T(8,128)(2,1)S(1)}, u32[]{:S(2)}, u32[]{:S(2)}) %all-to-all-start.1) | async-done | bytes 1048608 | tf_op jit(solution)/shard_map/all_to_all | solution.py:523
  87.7 0.0 copy-done.4
  87.7 1.4 %gather.1 = bf16[192,1024]{1,0:T(8,128)(2,1)} custom-call(s32[8,256]{1,0:T(8,128)S(1)} %copy-done.4, bf16[1024,512]{1,0:T(8,128)(2,1)S(1)} %bitcast.6), custom_call_target="tpu_custom_call" | custom-call | flops 400000000 | bytes 2097152 | tf_op jit(solution)/shard_map/gather/pallas_call | solution.py:510
  (5 shorter events, 0.0 us)
Async XLA Ops:
  25.6 31.0 %all-to-all-start = ((bf16[128,8,512]{2,1,0:T(8,128)(2,1)}), bf16[128,8,512]{2,1,0:T(8,128)(2,1)}, u32[]{:S(2)}, u32[]{:S(2)}) async-start(bf16[128,8,512]{2,1,0:T(8,128)(2,1)} %bitcast.8), calls=%async_computation | async-start | bytes 2097152 | tf_op jit(solution)/shard_map/all_to_all | solution.py:523
  42.1 10.4 %collective-permute-start = (bf16[128,1024]{1,0:T(8,128)(2,1)}, bf16[128,1024]{1,0:T(8,128)(2,1)}, u32[]{:S(2)}, u32[]{:S(2)}) collective-permute-start(bf16[128,1024]{1,0:T(8,128)(2,1)} %get-tuple-element.23), channel_id=1, source_target_pairs={{0,1},{1,2},{2,3},{3,4},{4,5},{5,6},{6,7},{8,9},{9,10},{10,11},{11... | collective-permute-start | bytes 786440 | tf_op jit(solution)/shard_map/ppermute | solution.py:553
  45.7 8.3 %collective-permute-start.1 = (bf16[128,1024]{1,0:T(8,128)(2,1)}, bf16[128,1024]{1,0:T(8,128)(2,1)}, u32[]{:S(2)}, u32[]{:S(2)}) collective-permute-start(bf16[128,1024]{1,0:T(8,128)(2,1)} %get-tuple-element.24), channel_id=1, source_target_pairs={{1,0},{2,1},{3,2},{4,3},{5,4},{6,5},{7,6},{9,8},{10,9},{11,10},{12... | collective-permute-start | bytes 786440 | tf_op jit(solution)/shard_map/ppermute | solution.py:552
  62.1 22.2 %copy-start = (bf16[1024,1024]{1,0:T(8,128)(2,1)S(1)}, bf16[1024,1024]{1,0:T(8,128)(2,1)}, u32[]{:S(2)}) copy-start(bf16[1024,1024]{1,0:T(8,128)(2,1)} %weight_ref.3) | copy-start | bytes 6291460
  62.1 25.5 %all-to-all-start.1 = ((bf16[128,8,512]{2,1,0:T(8,128)(2,1)}), bf16[128,8,512]{2,1,0:T(8,128)(2,1)S(1)}, u32[]{:S(2)}, u32[]{:S(2)}) async-start(bf16[128,8,512]{2,1,0:T(8,128)(2,1)} %bitcast.7), calls=%async_computation.1 | async-start | bytes 2097152 | tf_op jit(solution)/shard_map/all_to_all | solution.py:523
  68.3 16.0 %collective-permute-start.3 = (bf16[128,1024]{1,0:T(8,128)(2,1)}, bf16[128,1024]{1,0:T(8,128)(2,1)S(1)}, u32[]{:S(2)}, u32[]{:S(2)}) collective-permute-start(bf16[128,1024]{1,0:T(8,128)(2,1)} %get-tuple-element.26.top_hbm), channel_id=1, source_target_pairs={{1,0},{2,1},{3,2},{4,3},{5,4},{6,5},{7,6},{9,8},{10,9},{11,10},{12... | collective-permute-start | bytes 786440 | tf_op jit(solution)/shard_map/ppermute | solution.py:557
  71.3 13.0 %collective-permute-start.2 = (bf16[128,1024]{1,0:T(8,128)(2,1)}, bf16[128,1024]{1,0:T(8,128)(2,1)S(1)}, u32[]{:S(2)}, u32[]{:S(2)}) collective-permute-start(bf16[128,1024]{1,0:T(8,128)(2,1)} %get-tuple-element.27.bottom_hbm), channel_id=1, source_target_pairs={{0,1},{1,2},{2,3},{3,4},{4,5},{5,6},{6,7},{8,9},{9,10},{10,11},{11... | collective-permute-start | bytes 786440 | tf_op jit(solution)/shard_map/ppermute | solution.py:556
  73.9 1.0 %copy-start.1 = (bf16[256,512]{1,0:T(8,128)(2,1)S(1)}, bf16[256,512]{1,0:T(8,128)(2,1)}, u32[]{:S(2)}) copy-start(bf16[256,512]{1,0:T(8,128)(2,1)} %get-tuple-element.28.band_hbm) | copy-start | bytes 786436
  74.9 0.9 %copy-start.2 = (bf16[128,1024]{1,0:T(8,128)(2,1)S(1)}, bf16[128,1024]{1,0:T(8,128)(2,1)}, u32[]{:S(2)}) copy-start(bf16[128,1024]{1,0:T(8,128)(2,1)} %get-tuple-element.27.bottom_hbm) | copy-start | bytes 786436
  75.8 0.9 %copy-start.3 = (bf16[128,1024]{1,0:T(8,128)(2,1)S(1)}, bf16[128,1024]{1,0:T(8,128)(2,1)}, u32[]{:S(2)}) copy-start(bf16[128,1024]{1,0:T(8,128)(2,1)} %get-tuple-element.26.top_hbm) | copy-start | bytes 786436
  84.4 3.3 %copy-start.4 = (s32[8,256]{1,0:T(8,128)S(1)}, s32[8,256]{1,0:T(8,128)}, u32[]{:S(2)}) copy-start(s32[8,256]{1,0:T(8,128)} %get-tuple-element.32.target_ref) | copy-start | bytes 24580

commit v5 on v4

--- a/solution.py
+++ b/solution.py
@@ -22,6 +22,9 @@
 BLOCK = 512
 BLOCKS = TOKENS // BLOCK
 AHEAD = 2
+OPEN = (512, 512)
+USUAL = (512, 512)
+CLOSE = (256, 256, 256, 256)
 PIECES = 4
 
 bf16 = jnp.bfloat16
@@ -156,45 +159,46 @@
     member[...] = mask.astype(bf16)
     counts = jnp.maximum(jnp.sum(mask, axis=1, keepdims=True), 1.0)
 
-
-    def first(c, m):
-        return dot(states[block_of(m), :], expand[c])
-
-    def second(c, m, values, opening):
+    def first(c, r, n):
+        return dot(states[pl.ds(r, n), :], expand[c])
+
+    def second(c, r, n, values, opening):
         acted = 0.5 * values * (1.0 + lax.erf(values * ROOT_HALF))
         product = dot(acted.astype(bf16), contract[c])
-        total[block_of(m), :] = product if opening else total[block_of(m), :] + product
+        rows = pl.ds(r, n)
+        total[rows, :] = product if opening else total[rows, :] + product
 
     buffers = (hidden_a, hidden_b)
 
-    def step(c, opening=False, closing=False):
-        for m in range(BLOCKS):
-            now, later = buffers[m % 2], buffers[(m + 1) % 2]
-            if m + 1 < BLOCKS:
-                later[...] = first(c, m + 1)
+    def step(c, sizes, following, opening=False, closing=False):
+        starts = [sum(sizes[:k]) for k in range(len(sizes))]
+        for k, (r, n) in enumerate(zip(starts, sizes)):
+            now, later = buffers[k % 2], buffers[(k + 1) % 2]
+            if k + 1 < len(sizes):
+                later[: sizes[k + 1], :] = first(c, starts[k + 1], sizes[k + 1])
             elif not closing:
                 if opening:
                     start(2)
                     wait(1)
-                later[...] = first(c + 1, 0)
-            second(c, m, now[...], opening)
+                later[:following, :] = first(c + 1, 0, following)
+            second(c, r, n, now[:n, :], opening)
             if closing:
-                settle(m)
-
-    def settle(m):
-        mixed = total[block_of(m), :] + states[block_of(m), :].astype(f32)
+                settle(pl.ds(r, n))
+
+    def settle(rows):
+        mixed = total[rows, :] + states[rows, :].astype(f32)
         centred = mixed - jnp.mean(mixed, axis=1, keepdims=True)
         variance = jnp.mean(centred * centred, axis=1, keepdims=True)
-        normed[block_of(m), :] = (centred * lax.rsqrt(variance + EPS)).astype(bf16)
+        normed[rows, :] = (centred * lax.rsqrt(variance + EPS)).astype(bf16)
 
     state_copy(0).wait()
     wait_expand(0)
     start(1)
-    hidden_a[...] = first(0, 0)
+    hidden_a[:OPEN[0], :] = first(0, 0, OPEN[0])
     for m in range(1, BLOCKS):
         state_copy(m).wait()
     wait(0)
-    step(0, opening=True)
+    step(0, OPEN, USUAL[0], opening=True)
 
     def middle_step(c, carry):
         @pl.when(c + AHEAD < CHUNKS)
@@ -202,11 +206,13 @@
             start(c + AHEAD)
 
         wait(c + 1)
-        step(c)
+        step(c, USUAL, USUAL[0])
         return carry
 
-    lax.fori_loop(1, CHUNKS - 1, middle_step, 0)
-    step(CHUNKS - 1, closing=True)
+    lax.fori_loop(1, CHUNKS - 2, middle_step, 0)
+    wait(CHUNKS - 1)
+    step(CHUNKS - 2, USUAL, CLOSE[0])
+    step(CHUNKS - 1, CLOSE, None, closing=True)
     summed = dot(member[...], normed[...])
     embeds = (summed / counts).astype(bf16)
     stacked = jnp.concatenate([embeds[:, :HALF], embeds[:, HALF:]], axis=0)
@@ -311,18 +317,16 @@
     fill_band(columns_ref, count_ref, values_ref, band_ref, False)
     fill_band(columns_ref, count_ref, values_ref, band_t, True)
 
-    def place(column, u):
+    def place(column):
         peer, slot = column >> 3, column & 3
         halo = jnp.where(peer < PEERS // 2, 2 * SLOTS - TILE, -PEERS) + 2 * peer + slot - 2
-        source = jnp.where(slot < 2, TILE + 2 * peer + slot, halo)
-        return jnp.where(((column >> 2) & 1) == u, source, -1)
+        return jnp.where(slot < 2, TILE + 2 * peer + slot, halo)
 
     shape = (2 * SLOTS, ROWS)
-    for u in range(2):
-        moved = jnp.where(iota(shape, 0) == place(iota((1, ROWS), 1), u), 1.0, 0.0)
-        mix[u * SLOTS : (u + 1) * SLOTS, :] = dot(band_ref[...], moved.astype(bf16)).astype(bf16)
-        back = jnp.where(iota(shape[::-1], 1) == place(iota((ROWS, 1), 0), u), 1.0, 0.0)
-        mix_t[:, u * SLOTS : (u + 1) * SLOTS] = dot(back.astype(bf16), band_t[...]).astype(bf16)
+    moved = jnp.where(iota(shape, 0) == place(iota((1, ROWS), 1)), 1.0, 0.0)
+    mix[...] = dot(band_ref[...], moved.astype(bf16)).astype(bf16)
+    back = jnp.where(iota(shape[::-1], 1) == place(iota((ROWS, 1), 0)), 1.0, 0.0)
+    mix_t[...] = dot(back.astype(bf16), band_t[...]).astype(bf16)
     copies = [
         pltpu.make_async_copy(mix, mix_hbm, sems.at[0]),
         pltpu.make_async_copy(mix_t, mix_t_hbm, sems.at[1]),
@@ -337,16 +341,16 @@
     return pl.pallas_call(
         prepare_kernel,
         out_shape=(
-            jax.ShapeDtypeStruct((2 * SLOTS, ROWS), bf16),
-            jax.ShapeDtypeStruct((ROWS, 2 * SLOTS), bf16),
+            jax.ShapeDtypeStruct((SLOTS, ROWS), bf16),
+            jax.ShapeDtypeStruct((ROWS, SLOTS), bf16),
             jax.ShapeDtypeStruct((SLOTS, 2 * SLOTS), bf16),
         ),
         in_specs=[SMEM, SMEM, VMEM, ANY],
         out_specs=(ANY, ANY, VMEM),
         scratch_shapes=[
             pltpu.VMEM((2 * SLOTS, SLOTS), bf16),
-            pltpu.VMEM((2 * SLOTS, ROWS), bf16),
-            pltpu.VMEM((ROWS, 2 * SLOTS), bf16),
+            pltpu.VMEM((SLOTS, ROWS), bf16),
+            pltpu.VMEM((ROWS, SLOTS), bf16),
             pltpu.SemaphoreType.DMA((2,)),
         ],
         compiler_params=params(63.9),
@@ -375,6 +379,7 @@
     left,
     right,
     mix_t,
+    back,
     sems,
     act_sems,
     out_sems,
@@ -393,7 +398,10 @@
         copy.start()
     copies[0].wait()
     copies[1].wait()
-    halves = dot(mix[...], rows[...]).astype(bf16)
+    lane_half = ((iota((1, ROWS), 1) >> 2) & 1).astype(f32).astype(bf16)
+    upper_mix = mix[...] * lane_half
+    both = jnp.concatenate([mix[...] - upper_mix, upper_mix], axis=0)
+    halves = dot(both, rows[...]).astype(bf16)
     mixed = jnp.concatenate([halves[:SLOTS], halves[SLOTS:]], axis=1)
     copies[2].wait()
     before = dot(mixed, weight[...])
@@ -414,7 +422,11 @@
     grad_mix = dot_t(grad_before, weight[...]).astype(bf16)
     stacked = jnp.concatenate([grad_mix[:, :HALF], grad_mix[:, HALF:]], axis=0)
     copies[6].wait()
-    send_rows(lambda r: dot(mix_t[r, :], stacked), out, out_hbm, out_sems)
+    row_half = ((iota((ROWS, 1), 0) >> 2) & 1).astype(f32).astype(bf16)
+    upper_t = mix_t[...] * row_half
+    both_t = jnp.concatenate([mix_t[...] - upper_t, upper_t], axis=1)
+    back[...] = both_t
+    send_rows(lambda r: dot(back[r, :], stacked), out, out_hbm, out_sems)
     for copy in act_copies:
         copy.wait()
 
@@ -431,6 +443,7 @@
         out_specs=(ANY,) * 3,
         scratch_shapes=[pltpu.VMEM((SLOTS, D), bf16), pltpu.VMEM((ROWS, HALF), bf16)]
         + [pltpu.VMEM(a.shape, a.dtype) for a in arrays]
+        + [pltpu.VMEM((ROWS, 2 * SLOTS), bf16)]
         + [pltpu.SemaphoreType.DMA((n,)) for n in (7, 2, PIECES)],
         compiler_params=params(63.9),
         cost_estimate=cost(3 * 10**9, 8 * 2**20),
@@ -499,11 +512,11 @@
     halo_row = jnp.sum(jnp.where(diagonal, target_ref[1:2, :], 0), axis=1, keepdims=True)
     lanes = iota((NODES, ROWS), 1)
     for u in range(2):
-        hit = (lanes - 4 * u == own_row) | (lanes - 4 * u == halo_row)
+        hit = (lanes == own_row + 4 * u) | (lanes == halo_row + 4 * u)
         pick[u * NODES : (u + 1) * NODES, :] = jnp.where(hit, 1.0, 0.0).astype(bf16)
-    for u in range(2):
-        picked = dot(pick[u * NODES : (u + 1) * NODES, :], rows_ref[...])
-        out_ref[:, u * HALF : (u + 1) * HALF] = picked.astype(bf16)
+    picked = dot(pick[...], rows_ref[...]).astype(bf16)
+    out_ref[:, :HALF] = picked[:NODES]
+    out_ref[:, HALF:] = picked[NODES:]
 
 
 def gather(target, rows):

time: 89.6 us -> 89.1 us (level)
  Pallas kernels: 43.4 us -> 41.7 us
  waiting for transfers between devices: 12.8 us -> 14 us
    pallas_call x1, Pallas kernels: 4.69 us -> 3.46 us  [prepare(): pl.pallas_call(prepare_kernel, out_shape=(jax.ShapeDtypeStruct((SLOTS, RO...]
    ppermute x1, waiting for transfers between devices: 1.49 us -> 2.71 us  [local(): from_right = lax.ppermute(low, 'dom', leftward)]
  transfers between devices with their start and end apart: 6 -> 6, of which waited for: 4 -> 4; matrix products, arithmetic and copies ran while one was open for 0% -> 0% of each run, Pallas kernels for 13% -> 12%
where the time goes in v5:
time: 89.1 us; the launch traced here: 88.6 us
  Pallas kernels  41.7 us (47%)
  starting transfers between devices  29.4 us (33%)
  waiting for transfers between devices  14 us (16%)
  local copies, waits for them, and re-layouts  2.85 us (3%)
    pallas_call x1, Pallas kernels, encode(): pl.pallas_call(encode_kernel, out_shape=(jax.ShapeDtypeStruct((ROWS, HALF...  24.6 us
    all_to_all x2, starting transfers between devices, swap(): lax.all_to_all(rows.reshape(PEERS, 8, HALF), ('enc', 'dom'), split_axis=0...  18.1 us
    ppermute x1, waiting for transfers between devices, local(): right = lax.ppermute(top, 'dom', leftward)  7.16 us
    pallas_call x1, Pallas kernels, middle(): pl.pallas_call(middle_kernel, out_shape=(jax.ShapeDtypeStruct((TILE, D),...  5.44 us
    pallas_call x1, Pallas kernels, spread(): pl.pallas_call(spread_kernel, out_shape=(jax.ShapeDtypeStruct((TILE, D),...  4.56 us
    all_to_all x2, waiting for transfers between devices, swap(): lax.all_to_all(rows.reshape(PEERS, 8, HALF), ('enc', 'dom'), split_axis=0...  4.12 us
    ppermute x1, starting transfers between devices, local(): from_left = lax.ppermute(high, 'dom', rightward)  3.55 us
    pallas_call x1, Pallas kernels, prepare(): pl.pallas_call(prepare_kernel, out_shape=(jax.ShapeDtypeStruct((SLOTS, RO...  3.46 us
  transfers between devices with their start and end apart: 6, of which 4 were waited for; matrix products, arithmetic and copies ran while one was open for 0% of the time, Pallas kernels for 12%

profile of v5, /device:TPU:1, one launch (start us, length us, event | category | flops | bytes accessed | tf_op | source)
XLA Modules:
  0.0 88.6 jit_solution(16624096929102559834)
XLA Ops:
  0.6 24.6 %encode.1 = (bf16[1024,512]{1,0:T(8,128)(2,1)}, s32[8,256]{1,0:T(8,128)}) custom-call(s32[1]{0:T(128)} %bitcast.upper_ref, s32[1,192]{1,0:T(1,128)} %bitcast.9, s32[1,1024]{1,0:T(1,128)} %node_ref.1, bf16[1024,1024]{1,0:T(8,128)(2,1)} %states_hbm.1, bf16[1024,4096]{1,0:T(8,128)(2,1)} %expand_hbm.1, bf16[4096,1024]{1,0:T(8,128)(2,1)} %contract_hbm.1), custom_call_target="tpu_custom_call" | custom-call | flops 17179869184 | bytes 20971520 | tf_op jit(solution)/shard_map/encode/pallas_call | solution.py:224
  25.3 12.0 %all-to-all-start = ((bf16[128,8,512]{2,1,0:T(8,128)(2,1)}), bf16[128,8,512]{2,1,0:T(8,128)(2,1)}, u32[]{:S(2)}, u32[]{:S(2)}) async-start(bf16[128,8,512]{2,1,0:T(8,128)(2,1)} %bitcast.8), calls=%async_computation | async-start | bytes 2097152 | tf_op jit(solution)/shard_map/all_to_all | solution.py:536
  37.2 4.6 %spread.1 = (bf16[128,1024]{1,0:T(8,128)(2,1)}, bf16[128,1024]{1,0:T(8,128)(2,1)}, f32[256,1024]{1,0:T(8,128)}) custom-call(s32[1,2,3]{2,1,0:T(2,128)} %columns_ref.3, s32[1,2]{1,0:T(1,128)} %count_ref.3, bf16[1,2,3,128,128]{4,3,2,1,0:T(8,128)(2,1)} %values_ref.3, bf16[256,1024]{1,0:T(8,128)(2,1)} %cotangent_ref, bf16[1024,1024]{1,0:T(8,128)(2,1)} %weight_ref.3), custom_call_target="tpu_custom_call" | custom-call | flops 1000000000 | bytes 5242880 | tf_op jit(solution)/shard_map/spread/pallas_call | solution.py:284
  41.8 3.6 %collective-permute-start = (bf16[128,1024]{1,0:T(8,128)(2,1)}, bf16[128,1024]{1,0:T(8,128)(2,1)}, u32[]{:S(2)}, u32[]{:S(2)}) collective-permute-start(bf16[128,1024]{1,0:T(8,128)(2,1)} %get-tuple-element.23), channel_id=1, source_target_pairs={{0,1},{1,2},{2,3},{3,4},{4,5},{5,6},{6,7},{8,9},{9,10},{10,11},{11... | collective-permute-start | bytes 786440 | tf_op jit(solution)/shard_map/ppermute | solution.py:566
  45.3 2.1 %collective-permute-start.1 = (bf16[128,1024]{1,0:T(8,128)(2,1)}, bf16[128,1024]{1,0:T(8,128)(2,1)}, u32[]{:S(2)}, u32[]{:S(2)}) collective-permute-start(bf16[128,1024]{1,0:T(8,128)(2,1)} %get-tuple-element.24), channel_id=1, source_target_pairs={{1,0},{2,1},{3,2},{4,3},{5,4},{6,5},{7,6},{9,8},{10,9},{11,10},{12... | collective-permute-start | bytes 786440 | tf_op jit(solution)/shard_map/ppermute | solution.py:565
  47.5 3.5 %prepare.1 = (bf16[256,1024]{1,0:T(8,128)(2,1)}, bf16[1024,256]{1,0:T(8,128)(2,1)}, bf16[256,512]{1,0:T(8,128)(2,1)}) custom-call(s32[1,2,3]{2,1,0:T(2,128)} %columns_ref.3, s32[1,2]{1,0:T(1,128)} %count_ref.3, bf16[1,2,3,128,128]{4,3,2,1,0:T(8,128)(2,1)} %values_ref.3, f32[256,1024]{1,0:T(8,128)} %get-tuple-element.21.order_ref.inner_hbm), custom_call_target="tpu_custom_call" | custom-call | flops 1000000000 | bytes 4194304 | tf_op jit(solution)/shard_map/prepare/pallas_call | solution.py:341
  50.9 0.0 collective-permute-done.left_hbm
  50.9 2.7 %collective-permute-done.1.right_hbm = bf16[128,1024]{1,0:T(8,128)(2,1)} collective-permute-done((bf16[128,1024]{1,0:T(8,128)(2,1)}, bf16[128,1024]{1,0:T(8,128)(2,1)}, u32[]{:S(2)}, u32[]{:S(2)}) %collective-permute-start.1) | collective-permute-done | bytes 262176 | tf_op jit(solution)/shard_map/ppermute | solution.py:565
  53.7 2.6 %all-to-all-done = bf16[128,8,512]{2,1,0:T(8,128)(2,1)} async-done(((bf16[128,8,512]{2,1,0:T(8,128)(2,1)}), bf16[128,8,512]{2,1,0:T(8,128)(2,1)}, u32[]{:S(2)}, u32[]{:S(2)}) %all-to-all-start) | async-done | bytes 1048608 | tf_op jit(solution)/shard_map/all_to_all | solution.py:536
  56.2 5.4 %middle.1 = (bf16[128,1024]{1,0:T(8,128)(2,1)}, bf16[128,1024]{1,0:T(8,128)(2,1)}, bf16[1024,512]{1,0:T(8,128)(2,1)}) custom-call(bf16[1024,512]{1,0:T(8,128)(2,1)} %bitcast.3.rows_hbm, bf16[256,1024]{1,0:T(8,128)(2,1)} %get-tuple-element.22.mix_hbm, bf16[1024,1024]{1,0:T(8,128)(2,1)} %weight_hbm.1, f32[256,1024]{1,0:T(8,128)} %get-tuple-element.21.order_ref.inner_hbm, ...), custom_call_target="tpu_custom_call" | custom-call | flops 3000000000 | bytes 8388608 | tf_op jit(solution)/shard_map/middle/pallas_call | solution.py:435
  61.7 0.0 copy-start
  61.7 6.2 %all-to-all-start.1 = ((bf16[128,8,512]{2,1,0:T(8,128)(2,1)}), bf16[128,8,512]{2,1,0:T(8,128)(2,1)S(1)}, u32[]{:S(2)}, u32[]{:S(2)}) async-start(bf16[128,8,512]{2,1,0:T(8,128)(2,1)} %bitcast.7), calls=%async_computation.1 | async-start | bytes 2097152 | tf_op jit(solution)/shard_map/all_to_all | solution.py:536
  67.9 3.0 %collective-permute-start.3 = (bf16[128,1024]{1,0:T(8,128)(2,1)}, bf16[128,1024]{1,0:T(8,128)(2,1)S(1)}, u32[]{:S(2)}, u32[]{:S(2)}) collective-permute-start(bf16[128,1024]{1,0:T(8,128)(2,1)} %get-tuple-element.26.top_hbm), channel_id=1, source_target_pairs={{1,0},{2,1},{3,2},{4,3},{5,4},{6,5},{7,6},{9,8},{10,9},{11,10},{12... | collective-permute-start | bytes 786440 | tf_op jit(solution)/shard_map/ppermute | solution.py:570
  70.8 2.6 %collective-permute-start.2 = (bf16[128,1024]{1,0:T(8,128)(2,1)}, bf16[128,1024]{1,0:T(8,128)(2,1)S(1)}, u32[]{:S(2)}, u32[]{:S(2)}) collective-permute-start(bf16[128,1024]{1,0:T(8,128)(2,1)} %get-tuple-element.27.bottom_hbm), channel_id=1, source_target_pairs={{0,1},{1,2},{2,3},{3,4},{4,5},{5,6},{6,7},{8,9},{9,10},{10,11},{11... | collective-permute-start | bytes 786440 | tf_op jit(solution)/shard_map/ppermute | solution.py:569
  73.4 0.0 copy-start.1
  73.5 0.9 %copy-done.1 = bf16[256,512]{1,0:T(8,128)(2,1)S(1)} copy-done((bf16[256,512]{1,0:T(8,128)(2,1)S(1)}, bf16[256,512]{1,0:T(8,128)(2,1)}, u32[]{:S(2)}) %copy-start.1) | copy-done | bytes 262168
  74.4 0.9 %copy-done.2 = bf16[128,1024]{1,0:T(8,128)(2,1)S(1)} copy-done((bf16[128,1024]{1,0:T(8,128)(2,1)S(1)}, bf16[128,1024]{1,0:T(8,128)(2,1)}, u32[]{:S(2)}) %copy-start.2) | copy-done | bytes 262168
  75.3 0.9 %copy-done.3 = bf16[128,1024]{1,0:T(8,128)(2,1)S(1)} copy-done((bf16[128,1024]{1,0:T(8,128)(2,1)S(1)}, bf16[128,1024]{1,0:T(8,128)(2,1)}, u32[]{:S(2)}) %copy-start.3) | copy-done | bytes 262168
  76.3 0.4 own_part.1
  76.7 7.2 %collective-permute-done.3.right_ref = bf16[128,1024]{1,0:T(8,128)(2,1)S(1)} collective-permute-done((bf16[128,1024]{1,0:T(8,128)(2,1)}, bf16[128,1024]{1,0:T(8,128)(2,1)S(1)}, u32[]{:S(2)}, u32[]{:S(2)}) %collective-permute-start.3) | collective-permute-done | bytes 262176 | tf_op jit(solution)/shard_map/ppermute | solution.py:570
  83.9 0.0 collective-permute-done.2.left_ref
  83.9 1.8 %finish.1 = bf16[256,1024]{1,0:T(8,128)(2,1)} custom-call(f32[256,1024]{1,0:T(8,128)S(1)} %get-tuple-element.29.part_ref, bf16[256,128]{1,0:T(8,128)(2,1)S(1)} %get-tuple-element.30.first_ref, bf16[256,128]{1,0:T(8,128)(2,1)S(1)} %get-tuple-element.31.last_ref, bf16[128,1024]{1,0:T(8,128)(2,1)S(1)} %collective-permute-done.2.left_ref, ...), custom_call_target="tpu_custom_call" | custom-call | flops 1000000000 | bytes 5242880 | tf_op jit(solution)/shard_map/finish/pallas_call | solution.py:498
  85.6 1.6 %all-to-all-done.1 = bf16[128,8,512]{2,1,0:T(8,128)(2,1)S(1)} async-done(((bf16[128,8,512]{2,1,0:T(8,128)(2,1)}), bf16[128,8,512]{2,1,0:T(8,128)(2,1)S(1)}, u32[]{:S(2)}, u32[]{:S(2)}) %all-to-all-start.1) | async-done | bytes 1048608 | tf_op jit(solution)/shard_map/all_to_all | solution.py:536
  87.2 1.4 %gather.1 = bf16[192,1024]{1,0:T(8,128)(2,1)} custom-call(s32[8,256]{1,0:T(8,128)S(1)} %copy-done.4, bf16[1024,512]{1,0:T(8,128)(2,1)S(1)} %bitcast.6), custom_call_target="tpu_custom_call" | custom-call | flops 400000000 | bytes 2097152 | tf_op jit(solution)/shard_map/gather/pallas_call | solution.py:523
  (5 shorter events, 0.0 us)
Async XLA Ops:
  25.3 31.0 %all-to-all-start = ((bf16[128,8,512]{2,1,0:T(8,128)(2,1)}), bf16[128,8,512]{2,1,0:T(8,128)(2,1)}, u32[]{:S(2)}, u32[]{:S(2)}) async-start(bf16[128,8,512]{2,1,0:T(8,128)(2,1)} %bitcast.8), calls=%async_computation | async-start | bytes 2097152 | tf_op jit(solution)/shard_map/all_to_all | solution.py:536
  41.8 9.1 %collective-permute-start = (bf16[128,1024]{1,0:T(8,128)(2,1)}, bf16[128,1024]{1,0:T(8,128)(2,1)}, u32[]{:S(2)}, u32[]{:S(2)}) collective-permute-start(bf16[128,1024]{1,0:T(8,128)(2,1)} %get-tuple-element.23), channel_id=1, source_target_pairs={{0,1},{1,2},{2,3},{3,4},{4,5},{5,6},{6,7},{8,9},{9,10},{10,11},{11... | collective-permute-start | bytes 786440 | tf_op jit(solution)/shard_map/ppermute | solution.py:566
  45.3 8.3 %collective-permute-start.1 = (bf16[128,1024]{1,0:T(8,128)(2,1)}, bf16[128,1024]{1,0:T(8,128)(2,1)}, u32[]{:S(2)}, u32[]{:S(2)}) collective-permute-start(bf16[128,1024]{1,0:T(8,128)(2,1)} %get-tuple-element.24), channel_id=1, source_target_pairs={{1,0},{2,1},{3,2},{4,3},{5,4},{6,5},{7,6},{9,8},{10,9},{11,10},{12... | collective-permute-start | bytes 786440 | tf_op jit(solution)/shard_map/ppermute | solution.py:565
  61.7 22.2 %copy-start = (bf16[1024,1024]{1,0:T(8,128)(2,1)S(1)}, bf16[1024,1024]{1,0:T(8,128)(2,1)}, u32[]{:S(2)}) copy-start(bf16[1024,1024]{1,0:T(8,128)(2,1)} %weight_ref.3) | copy-start | bytes 6291460
  61.7 25.5 %all-to-all-start.1 = ((bf16[128,8,512]{2,1,0:T(8,128)(2,1)}), bf16[128,8,512]{2,1,0:T(8,128)(2,1)S(1)}, u32[]{:S(2)}, u32[]{:S(2)}) async-start(bf16[128,8,512]{2,1,0:T(8,128)(2,1)} %bitcast.7), calls=%async_computation.1 | async-start | bytes 2097152 | tf_op jit(solution)/shard_map/all_to_all | solution.py:536
  67.9 16.0 %collective-permute-start.3 = (bf16[128,1024]{1,0:T(8,128)(2,1)}, bf16[128,1024]{1,0:T(8,128)(2,1)S(1)}, u32[]{:S(2)}, u32[]{:S(2)}) collective-permute-start(bf16[128,1024]{1,0:T(8,128)(2,1)} %get-tuple-element.26.top_hbm), channel_id=1, source_target_pairs={{1,0},{2,1},{3,2},{4,3},{5,4},{6,5},{7,6},{9,8},{10,9},{11,10},{12... | collective-permute-start | bytes 786440 | tf_op jit(solution)/shard_map/ppermute | solution.py:570
  70.8 13.0 %collective-permute-start.2 = (bf16[128,1024]{1,0:T(8,128)(2,1)}, bf16[128,1024]{1,0:T(8,128)(2,1)S(1)}, u32[]{:S(2)}, u32[]{:S(2)}) collective-permute-start(bf16[128,1024]{1,0:T(8,128)(2,1)} %get-tuple-element.27.bottom_hbm), channel_id=1, source_target_pairs={{0,1},{1,2},{2,3},{3,4},{4,5},{5,6},{6,7},{8,9},{9,10},{10,11},{11... | collective-permute-start | bytes 786440 | tf_op jit(solution)/shard_map/ppermute | solution.py:569
  73.4 1.0 %copy-start.1 = (bf16[256,512]{1,0:T(8,128)(2,1)S(1)}, bf16[256,512]{1,0:T(8,128)(2,1)}, u32[]{:S(2)}) copy-start(bf16[256,512]{1,0:T(8,128)(2,1)} %get-tuple-element.28.band_hbm) | copy-start | bytes 786436
  74.4 0.9 %copy-start.2 = (bf16[128,1024]{1,0:T(8,128)(2,1)S(1)}, bf16[128,1024]{1,0:T(8,128)(2,1)}, u32[]{:S(2)}) copy-start(bf16[128,1024]{1,0:T(8,128)(2,1)} %get-tuple-element.27.bottom_hbm) | copy-start | bytes 786436
  75.3 0.9 %copy-start.3 = (bf16[128,1024]{1,0:T(8,128)(2,1)S(1)}, bf16[128,1024]{1,0:T(8,128)(2,1)}, u32[]{:S(2)}) copy-start(bf16[128,1024]{1,0:T(8,128)(2,1)} %get-tuple-element.26.top_hbm) | copy-start | bytes 786436
  83.9 3.3 %copy-start.4 = (s32[8,256]{1,0:T(8,128)S(1)}, s32[8,256]{1,0:T(8,128)}, u32[]{:S(2)}) copy-start(s32[8,256]{1,0:T(8,128)} %get-tuple-element.32.target_ref) | copy-start | bytes 24580

commit v6 on v5

--- a/solution.py
+++ b/solution.py
@@ -58,12 +58,21 @@
     return pl.CostEstimate(flops=flops, bytes_accessed=moved, transcendentals=0)
 
 
+def interleave(low, high):
+    count = low.shape[0] // 8
+    low, high = low.reshape(count, 8, HALF), high.reshape(count, 8, HALF)
+    upper_rows = iota(low.shape, 1) >= 4
+    even = jnp.where(upper_rows, pltpu.roll(high, 4, 1), low)
+    odd = jnp.where(upper_rows, high, pltpu.roll(low, 4, 1))
+    return jnp.stack([even, odd], axis=1).reshape(count * 16, HALF)
+
+
 def send_rows(rows_of, out, out_hbm, sem):
     size = ROWS // PIECES
     copies = []
     for i in range(PIECES):
         rows = pl.ds(i * size, size)
-        out[rows, :] = rows_of(rows).astype(bf16)
+        out[rows, :] = rows_of(pl.ds(i * size // 2, size // 2)).astype(bf16)
         copies.append(pltpu.make_async_copy(out.at[rows, :], out_hbm.at[rows, :], sem.at[i]))
         copies[-1].start()
     for copy in copies:
@@ -150,11 +159,9 @@
     has_beside = (owner & (GROUP - 1)) != edge
     halo_row = jnp.where(has_beside, beside * 8 + 2 + rank, -4096)
     target_ref[...] = jnp.where(iota((8, NPAD), 0) == 0, own_row, halo_row)
-    rows = iota((ROWS, NPAD), 0)
-    for u in range(2):
-        shifted = rows - 4 * u
-        hit = (shifted == own_row) | (shifted == halo_row)
-        route[:, u * NPAD : (u + 1) * NPAD] = jnp.where(hit, 1.0, 0.0).astype(bf16)
+    rows = iota((ROWS // 2, NPAD), 0)
+    hit = (rows == owner * 4 + rank) | (rows == jnp.where(has_beside, beside * 4 + 2 + rank, -4096))
+    route[...] = jnp.where(hit, 1.0, 0.0).astype(bf16)
     mask = jnp.where(iota((NPAD, TOKENS), 0) == node_ref[...], 1.0, 0.0)
     member[...] = mask.astype(bf16)
     counts = jnp.maximum(jnp.sum(mask, axis=1, keepdims=True), 1.0)
@@ -215,8 +222,12 @@
     step(CHUNKS - 1, CLOSE, None, closing=True)
     summed = dot(member[...], normed[...])
     embeds = (summed / counts).astype(bf16)
-    stacked = jnp.concatenate([embeds[:, :HALF], embeds[:, HALF:]], axis=0)
-    send_rows(lambda r: dot(route[r, :], stacked), out, out_hbm, out_sem)
+    send_rows(
+        lambda r: interleave(dot(route[r, :], embeds[:, :HALF]), dot(route[r, :], embeds[:, HALF:])),
+        out,
+        out_hbm,
+        out_sem,
+    )
 
 
 def encode(upper, owner, node_ids, states, expand_weight, contract_weight):
@@ -238,7 +249,7 @@
             pltpu.VMEM((BLOCK, CHUNK), f32),
             pltpu.VMEM((BLOCK, CHUNK), f32),
             pltpu.VMEM((8, NPAD), jnp.int32),
-            pltpu.VMEM((ROWS, 2 * NPAD), bf16),
+            pltpu.VMEM((ROWS // 2, NPAD), bf16),
             pltpu.VMEM((NPAD, TOKENS), bf16),
             pltpu.VMEM((TOKENS, D), bf16),
             dma((BLOCKS,)),
@@ -325,7 +336,9 @@
     shape = (2 * SLOTS, ROWS)
     moved = jnp.where(iota(shape, 0) == place(iota((1, ROWS), 1)), 1.0, 0.0)
     mix[...] = dot(band_ref[...], moved.astype(bf16)).astype(bf16)
-    back = jnp.where(iota(shape[::-1], 1) == place(iota((ROWS, 1), 0)), 1.0, 0.0)
+    pair = iota((ROWS // 2, 1), 0)
+    source = place((pair >> 2) * 8 + (pair & 3))
+    back = jnp.where(iota((ROWS // 2, 2 * SLOTS), 1) == source, 1.0, 0.0)
     mix_t[...] = dot(back.astype(bf16), band_t[...]).astype(bf16)
     copies = [
         pltpu.make_async_copy(mix, mix_hbm, sems.at[0]),
@@ -342,7 +355,7 @@
         prepare_kernel,
         out_shape=(
             jax.ShapeDtypeStruct((SLOTS, ROWS), bf16),
-            jax.ShapeDtypeStruct((ROWS, SLOTS), bf16),
+            jax.ShapeDtypeStruct((ROWS // 2, SLOTS), bf16),
             jax.ShapeDtypeStruct((SLOTS, 2 * SLOTS), bf16),
         ),
         in_specs=[SMEM, SMEM, VMEM, ANY],
@@ -350,7 +363,7 @@
         scratch_shapes=[
             pltpu.VMEM((2 * SLOTS, SLOTS), bf16),
             pltpu.VMEM((SLOTS, ROWS), bf16),
-            pltpu.VMEM((ROWS, SLOTS), bf16),
+            pltpu.VMEM((ROWS // 2, SLOTS), bf16),
             pltpu.SemaphoreType.DMA((2,)),
         ],
         compiler_params=params(63.9),
@@ -379,7 +392,6 @@
     left,
     right,
     mix_t,
-    back,
     sems,
     act_sems,
     out_sems,
@@ -420,13 +432,13 @@
     rims = jnp.concatenate([left[...], right[...]], axis=0).astype(f32)
     grad_before = ((inner[...] + rims) * slope).astype(bf16)
     grad_mix = dot_t(grad_before, weight[...]).astype(bf16)
-    stacked = jnp.concatenate([grad_mix[:, :HALF], grad_mix[:, HALF:]], axis=0)
     copies[6].wait()
-    row_half = ((iota((ROWS, 1), 0) >> 2) & 1).astype(f32).astype(bf16)
-    upper_t = mix_t[...] * row_half
-    both_t = jnp.concatenate([mix_t[...] - upper_t, upper_t], axis=1)
-    back[...] = both_t
-    send_rows(lambda r: dot(back[r, :], stacked), out, out_hbm, out_sems)
+    send_rows(
+        lambda r: interleave(dot(mix_t[r, :], grad_mix[:, :HALF]), dot(mix_t[r, :], grad_mix[:, HALF:])),
+        out,
+        out_hbm,
+        out_sems,
+    )
     for copy in act_copies:
         copy.wait()
 
@@ -443,7 +455,6 @@
         out_specs=(ANY,) * 3,
         scratch_shapes=[pltpu.VMEM((SLOTS, D), bf16), pltpu.VMEM((ROWS, HALF), bf16)]
         + [pltpu.VMEM(a.shape, a.dtype) for a in arrays]
-        + [pltpu.VMEM((ROWS, 2 * SLOTS), bf16)]
         + [pltpu.SemaphoreType.DMA((n,)) for n in (7, 2, PIECES)],
         compiler_params=params(63.9),
         cost_estimate=cost(3 * 10**9, 8 * 2**20),

time: 89.1 us -> 88.7 us (level)
  transfers between devices with their start and end apart: 6 -> 6, of which waited for: 4 -> 5; matrix products, arithmetic and copies ran while one was open for 0% -> 0% of each run, Pallas kernels for 12% -> 11%
where the time goes in v6:
time: 88.7 us; the launch traced here: 88.3 us
  Pallas kernels  41 us (46%)
  starting transfers between devices  29.4 us (33%)
  waiting for transfers between devices  14.3 us (16%)
  local copies, waits for them, and re-layouts  2.85 us (3%)
    pallas_call x1, Pallas kernels, encode(): pl.pallas_call(encode_kernel, out_shape=(jax.ShapeDtypeStruct((ROWS, HALF...  24.4 us
    all_to_all x2, starting transfers between devices, swap(): lax.all_to_all(rows.reshape(PEERS, 8, HALF), ('enc', 'dom'), split_axis=0...  18.2 us
    ppermute x1, waiting for transfers between devices, local(): right = lax.ppermute(top, 'dom', leftward)  7.16 us
    pallas_call x1, Pallas kernels, middle(): pl.pallas_call(middle_kernel, out_shape=(jax.ShapeDtypeStruct((TILE, D),...  5.24 us
    pallas_call x1, Pallas kernels, spread(): pl.pallas_call(spread_kernel, out_shape=(jax.ShapeDtypeStruct((TILE, D),...  4.57 us
    all_to_all x2, waiting for transfers between devices, swap(): lax.all_to_all(rows.reshape(PEERS, 8, HALF), ('enc', 'dom'), split_axis=0...  4.13 us
    ppermute x1, starting transfers between devices, local(): from_left = lax.ppermute(high, 'dom', rightward)  3.54 us
    pallas_call x1, Pallas kernels, prepare(): pl.pallas_call(prepare_kernel, out_shape=(jax.ShapeDtypeStruct((SLOTS, RO...  3.21 us
  transfers between devices with their start and end apart: 6, of which 5 were waited for; matrix products, arithmetic and copies ran while one was open for 0% of the time, Pallas kernels for 11%

profile of v6, /device:TPU:1, one launch (start us, length us, event | category | flops | bytes accessed | tf_op | source)
XLA Modules:
  0.0 88.3 jit_solution(17543044120417263162)
XLA Ops:
  0.6 24.4 %encode.1 = (bf16[1024,512]{1,0:T(8,128)(2,1)}, s32[8,256]{1,0:T(8,128)}) custom-call(s32[1]{0:T(128)} %bitcast.upper_ref, s32[1,192]{1,0:T(1,128)} %bitcast.9, s32[1,1024]{1,0:T(1,128)} %node_ref.1, bf16[1024,1024]{1,0:T(8,128)(2,1)} %states_hbm.1, bf16[1024,4096]{1,0:T(8,128)(2,1)} %expand_hbm.1, bf16[4096,1024]{1,0:T(8,128)(2,1)} %contract_hbm.1), custom_call_target="tpu_custom_call" | custom-call | flops 17179869184 | bytes 20971520 | tf_op jit(solution)/shard_map/encode/pallas_call | solution.py:235
  25.1 12.0 %all-to-all-start = ((bf16[128,8,512]{2,1,0:T(8,128)(2,1)}), bf16[128,8,512]{2,1,0:T(8,128)(2,1)}, u32[]{:S(2)}, u32[]{:S(2)}) async-start(bf16[128,8,512]{2,1,0:T(8,128)(2,1)} %bitcast.8), calls=%async_computation | async-start | bytes 2097152 | tf_op jit(solution)/shard_map/all_to_all | solution.py:547
  37.0 4.6 %spread.1 = (bf16[128,1024]{1,0:T(8,128)(2,1)}, bf16[128,1024]{1,0:T(8,128)(2,1)}, f32[256,1024]{1,0:T(8,128)}) custom-call(s32[1,2,3]{2,1,0:T(2,128)} %columns_ref.3, s32[1,2]{1,0:T(1,128)} %count_ref.3, bf16[1,2,3,128,128]{4,3,2,1,0:T(8,128)(2,1)} %values_ref.3, bf16[256,1024]{1,0:T(8,128)(2,1)} %cotangent_ref, bf16[1024,1024]{1,0:T(8,128)(2,1)} %weight_ref.3), custom_call_target="tpu_custom_call" | custom-call | flops 1000000000 | bytes 5242880 | tf_op jit(solution)/shard_map/spread/pallas_call | solution.py:295
  41.6 3.5 %collective-permute-start = (bf16[128,1024]{1,0:T(8,128)(2,1)}, bf16[128,1024]{1,0:T(8,128)(2,1)}, u32[]{:S(2)}, u32[]{:S(2)}) collective-permute-start(bf16[128,1024]{1,0:T(8,128)(2,1)} %get-tuple-element.23), channel_id=1, source_target_pairs={{0,1},{1,2},{2,3},{3,4},{4,5},{5,6},{6,7},{8,9},{9,10},{10,11},{11... | collective-permute-start | bytes 786440 | tf_op jit(solution)/shard_map/ppermute | solution.py:577
  45.1 2.1 %collective-permute-start.1 = (bf16[128,1024]{1,0:T(8,128)(2,1)}, bf16[128,1024]{1,0:T(8,128)(2,1)}, u32[]{:S(2)}, u32[]{:S(2)}) collective-permute-start(bf16[128,1024]{1,0:T(8,128)(2,1)} %get-tuple-element.24), channel_id=1, source_target_pairs={{1,0},{2,1},{3,2},{4,3},{5,4},{6,5},{7,6},{9,8},{10,9},{11,10},{12... | collective-permute-start | bytes 786440 | tf_op jit(solution)/shard_map/ppermute | solution.py:576
  47.3 3.2 %prepare.1 = (bf16[256,1024]{1,0:T(8,128)(2,1)}, bf16[512,256]{1,0:T(8,128)(2,1)}, bf16[256,512]{1,0:T(8,128)(2,1)}) custom-call(s32[1,2,3]{2,1,0:T(2,128)} %columns_ref.3, s32[1,2]{1,0:T(1,128)} %count_ref.3, bf16[1,2,3,128,128]{4,3,2,1,0:T(8,128)(2,1)} %values_ref.3, f32[256,1024]{1,0:T(8,128)} %get-tuple-element.21.order_ref.inner_hbm), custom_call_target="tpu_custom_call" | custom-call | flops 1000000000 | bytes 4194304 | tf_op jit(solution)/shard_map/prepare/pallas_call | solution.py:354
  50.5 0.1 collective-permute-done.left_hbm
  50.6 2.9 %collective-permute-done.1.right_hbm = bf16[128,1024]{1,0:T(8,128)(2,1)} collective-permute-done((bf16[128,1024]{1,0:T(8,128)(2,1)}, bf16[128,1024]{1,0:T(8,128)(2,1)}, u32[]{:S(2)}, u32[]{:S(2)}) %collective-permute-start.1) | collective-permute-done | bytes 262176 | tf_op jit(solution)/shard_map/ppermute | solution.py:576
  53.4 2.6 %all-to-all-done = bf16[128,8,512]{2,1,0:T(8,128)(2,1)} async-done(((bf16[128,8,512]{2,1,0:T(8,128)(2,1)}), bf16[128,8,512]{2,1,0:T(8,128)(2,1)}, u32[]{:S(2)}, u32[]{:S(2)}) %all-to-all-start) | async-done | bytes 1048608 | tf_op jit(solution)/shard_map/all_to_all | solution.py:547
  56.0 5.2 %middle.1 = (bf16[128,1024]{1,0:T(8,128)(2,1)}, bf16[128,1024]{1,0:T(8,128)(2,1)}, bf16[1024,512]{1,0:T(8,128)(2,1)}) custom-call(bf16[1024,512]{1,0:T(8,128)(2,1)} %bitcast.3.rows_hbm, bf16[256,1024]{1,0:T(8,128)(2,1)} %get-tuple-element.22.mix_hbm, bf16[1024,1024]{1,0:T(8,128)(2,1)} %weight_hbm.1, f32[256,1024]{1,0:T(8,128)} %get-tuple-element.21.order_ref.inner_hbm, ...), custom_call_target="tpu_custom_call" | custom-call | flops 3000000000 | bytes 8388608 | tf_op jit(solution)/shard_map/middle/pallas_call | solution.py:447
  61.3 0.0 copy-start
  61.3 6.2 %all-to-all-start.1 = ((bf16[128,8,512]{2,1,0:T(8,128)(2,1)}), bf16[128,8,512]{2,1,0:T(8,128)(2,1)S(1)}, u32[]{:S(2)}, u32[]{:S(2)}) async-start(bf16[128,8,512]{2,1,0:T(8,128)(2,1)} %bitcast.7), calls=%async_computation.1 | async-start | bytes 2097152 | tf_op jit(solution)/shard_map/all_to_all | solution.py:547
  67.5 3.0 %collective-permute-start.3 = (bf16[128,1024]{1,0:T(8,128)(2,1)}, bf16[128,1024]{1,0:T(8,128)(2,1)S(1)}, u32[]{:S(2)}, u32[]{:S(2)}) collective-permute-start(bf16[128,1024]{1,0:T(8,128)(2,1)} %get-tuple-element.26.top_hbm), channel_id=1, source_target_pairs={{1,0},{2,1},{3,2},{4,3},{5,4},{6,5},{7,6},{9,8},{10,9},{11,10},{12... | collective-permute-start | bytes 786440 | tf_op jit(solution)/shard_map/ppermute | solution.py:581
  70.5 2.6 %collective-permute-start.2 = (bf16[128,1024]{1,0:T(8,128)(2,1)}, bf16[128,1024]{1,0:T(8,128)(2,1)S(1)}, u32[]{:S(2)}, u32[]{:S(2)}) collective-permute-start(bf16[128,1024]{1,0:T(8,128)(2,1)} %get-tuple-element.27.bottom_hbm), channel_id=1, source_target_pairs={{0,1},{1,2},{2,3},{3,4},{4,5},{5,6},{6,7},{8,9},{9,10},{10,11},{11... | collective-permute-start | bytes 786440 | tf_op jit(solution)/shard_map/ppermute | solution.py:580
  73.1 0.9 %copy-done.1 = bf16[256,512]{1,0:T(8,128)(2,1)S(1)} copy-done((bf16[256,512]{1,0:T(8,128)(2,1)S(1)}, bf16[256,512]{1,0:T(8,128)(2,1)}, u32[]{:S(2)}) %copy-start.1) | copy-done | bytes 262168
  74.0 0.9 %copy-done.2 = bf16[128,1024]{1,0:T(8,128)(2,1)S(1)} copy-done((bf16[128,1024]{1,0:T(8,128)(2,1)S(1)}, bf16[128,1024]{1,0:T(8,128)(2,1)}, u32[]{:S(2)}) %copy-start.2) | copy-done | bytes 262168
  75.0 0.9 %copy-done.3 = bf16[128,1024]{1,0:T(8,128)(2,1)S(1)} copy-done((bf16[128,1024]{1,0:T(8,128)(2,1)S(1)}, bf16[128,1024]{1,0:T(8,128)(2,1)}, u32[]{:S(2)}) %copy-start.3) | copy-done | bytes 262168
  75.9 0.4 own_part.1
  76.3 7.2 %collective-permute-done.3.right_ref = bf16[128,1024]{1,0:T(8,128)(2,1)S(1)} collective-permute-done((bf16[128,1024]{1,0:T(8,128)(2,1)}, bf16[128,1024]{1,0:T(8,128)(2,1)S(1)}, u32[]{:S(2)}, u32[]{:S(2)}) %collective-permute-start.3) | collective-permute-done | bytes 262176 | tf_op jit(solution)/shard_map/ppermute | solution.py:581
  83.5 0.0 collective-permute-done.2.left_ref
  83.5 1.8 %finish.1 = bf16[256,1024]{1,0:T(8,128)(2,1)} custom-call(f32[256,1024]{1,0:T(8,128)S(1)} %get-tuple-element.29.part_ref, bf16[256,128]{1,0:T(8,128)(2,1)S(1)} %get-tuple-element.30.first_ref, bf16[256,128]{1,0:T(8,128)(2,1)S(1)} %get-tuple-element.31.last_ref, bf16[128,1024]{1,0:T(8,128)(2,1)S(1)} %collective-permute-done.2.left_ref, ...), custom_call_target="tpu_custom_call" | custom-call | flops 1000000000 | bytes 5242880 | tf_op jit(solution)/shard_map/finish/pallas_call | solution.py:509
  85.3 1.6 %all-to-all-done.1 = bf16[128,8,512]{2,1,0:T(8,128)(2,1)S(1)} async-done(((bf16[128,8,512]{2,1,0:T(8,128)(2,1)}), bf16[128,8,512]{2,1,0:T(8,128)(2,1)S(1)}, u32[]{:S(2)}, u32[]{:S(2)}) %all-to-all-start.1) | async-done | bytes 1048608 | tf_op jit(solution)/shard_map/all_to_all | solution.py:547
  86.8 0.0 copy-done.4
  86.8 1.4 %gather.1 = bf16[192,1024]{1,0:T(8,128)(2,1)} custom-call(s32[8,256]{1,0:T(8,128)S(1)} %copy-done.4, bf16[1024,512]{1,0:T(8,128)(2,1)S(1)} %bitcast.6), custom_call_target="tpu_custom_call" | custom-call | flops 400000000 | bytes 2097152 | tf_op jit(solution)/shard_map/gather/pallas_call | solution.py:534
  (5 shorter events, 0.0 us)
Async XLA Ops:
  25.1 31.0 %all-to-all-start = ((bf16[128,8,512]{2,1,0:T(8,128)(2,1)}), bf16[128,8,512]{2,1,0:T(8,128)(2,1)}, u32[]{:S(2)}, u32[]{:S(2)}) async-start(bf16[128,8,512]{2,1,0:T(8,128)(2,1)} %bitcast.8), calls=%async_computation | async-start | bytes 2097152 | tf_op jit(solution)/shard_map/all_to_all | solution.py:547
  41.6 9.0 %collective-permute-start = (bf16[128,1024]{1,0:T(8,128)(2,1)}, bf16[128,1024]{1,0:T(8,128)(2,1)}, u32[]{:S(2)}, u32[]{:S(2)}) collective-permute-start(bf16[128,1024]{1,0:T(8,128)(2,1)} %get-tuple-element.23), channel_id=1, source_target_pairs={{0,1},{1,2},{2,3},{3,4},{4,5},{5,6},{6,7},{8,9},{9,10},{10,11},{11... | collective-permute-start | bytes 786440 | tf_op jit(solution)/shard_map/ppermute | solution.py:577
  45.1 8.3 %collective-permute-start.1 = (bf16[128,1024]{1,0:T(8,128)(2,1)}, bf16[128,1024]{1,0:T(8,128)(2,1)}, u32[]{:S(2)}, u32[]{:S(2)}) collective-permute-start(bf16[128,1024]{1,0:T(8,128)(2,1)} %get-tuple-element.24), channel_id=1, source_target_pairs={{1,0},{2,1},{3,2},{4,3},{5,4},{6,5},{7,6},{9,8},{10,9},{11,10},{12... | collective-permute-start | bytes 786440 | tf_op jit(solution)/shard_map/ppermute | solution.py:576
  61.3 22.2 %copy-start = (bf16[1024,1024]{1,0:T(8,128)(2,1)S(1)}, bf16[1024,1024]{1,0:T(8,128)(2,1)}, u32[]{:S(2)}) copy-start(bf16[1024,1024]{1,0:T(8,128)(2,1)} %weight_ref.3) | copy-start | bytes 6291460
  61.3 25.6 %all-to-all-start.1 = ((bf16[128,8,512]{2,1,0:T(8,128)(2,1)}), bf16[128,8,512]{2,1,0:T(8,128)(2,1)S(1)}, u32[]{:S(2)}, u32[]{:S(2)}) async-start(bf16[128,8,512]{2,1,0:T(8,128)(2,1)} %bitcast.7), calls=%async_computation.1 | async-start | bytes 2097152 | tf_op jit(solution)/shard_map/all_to_all | solution.py:547
  67.5 16.0 %collective-permute-start.3 = (bf16[128,1024]{1,0:T(8,128)(2,1)}, bf16[128,1024]{1,0:T(8,128)(2,1)S(1)}, u32[]{:S(2)}, u32[]{:S(2)}) collective-permute-start(bf16[128,1024]{1,0:T(8,128)(2,1)} %get-tuple-element.26.top_hbm), channel_id=1, source_target_pairs={{1,0},{2,1},{3,2},{4,3},{5,4},{6,5},{7,6},{9,8},{10,9},{11,10},{12... | collective-permute-start | bytes 786440 | tf_op jit(solution)/shard_map/ppermute | solution.py:581
  70.5 13.0 %collective-permute-start.2 = (bf16[128,1024]{1,0:T(8,128)(2,1)}, bf16[128,1024]{1,0:T(8,128)(2,1)S(1)}, u32[]{:S(2)}, u32[]{:S(2)}) collective-permute-start(bf16[128,1024]{1,0:T(8,128)(2,1)} %get-tuple-element.27.bottom_hbm), channel_id=1, source_target_pairs={{0,1},{1,2},{2,3},{3,4},{4,5},{5,6},{6,7},{8,9},{9,10},{10,11},{11... | collective-permute-start | bytes 786440 | tf_op jit(solution)/shard_map/ppermute | solution.py:580
  73.1 1.0 %copy-start.1 = (bf16[256,512]{1,0:T(8,128)(2,1)S(1)}, bf16[256,512]{1,0:T(8,128)(2,1)}, u32[]{:S(2)}) copy-start(bf16[256,512]{1,0:T(8,128)(2,1)} %get-tuple-element.28.band_hbm) | copy-start | bytes 786436
  74.0 0.9 %copy-start.2 = (bf16[128,1024]{1,0:T(8,128)(2,1)S(1)}, bf16[128,1024]{1,0:T(8,128)(2,1)}, u32[]{:S(2)}) copy-start(bf16[128,1024]{1,0:T(8,128)(2,1)} %get-tuple-element.27.bottom_hbm) | copy-start | bytes 786436
  75.0 0.9 %copy-start.3 = (bf16[128,1024]{1,0:T(8,128)(2,1)S(1)}, bf16[128,1024]{1,0:T(8,128)(2,1)}, u32[]{:S(2)}) copy-start(bf16[128,1024]{1,0:T(8,128)(2,1)} %get-tuple-element.26.top_hbm) | copy-start | bytes 786436
  83.5 3.3 %copy-start.4 = (s32[8,256]{1,0:T(8,128)S(1)}, s32[8,256]{1,0:T(8,128)}, u32[]{:S(2)}) copy-start(s32[8,256]{1,0:T(8,128)} %get-tuple-element.32.target_ref) | copy-start | bytes 24580

commit v7 on v6

--- a/solution.py
+++ b/solution.py
@@ -25,7 +25,7 @@
 OPEN = (512, 512)
 USUAL = (512, 512)
 CLOSE = (256, 256, 256, 256)
-PIECES = 4
+PIECES = 2
 
 bf16 = jnp.bfloat16
 f32 = jnp.float32

time: 88.7 us -> 88.8 us (level)
  no operation moved by 1% of the time
where the time goes in v7:
time: 88.8 us; the launch traced here: 88.3 us
  Pallas kernels  41.1 us (46%)
  starting transfers between devices  29.3 us (33%)
  waiting for transfers between devices  14.3 us (16%)
  local copies, waits for them, and re-layouts  2.85 us (3%)
    pallas_call x1, Pallas kernels, encode(): pl.pallas_call(encode_kernel, out_shape=(jax.ShapeDtypeStruct((ROWS, HALF...  24.4 us
    all_to_all x2, starting transfers between devices, swap(): lax.all_to_all(rows.reshape(PEERS, 8, HALF), ('enc', 'dom'), split_axis=0...  18.1 us
    ppermute x1, waiting for transfers between devices, local(): right = lax.ppermute(top, 'dom', leftward)  7.16 us
    pallas_call x1, Pallas kernels, middle(): pl.pallas_call(middle_kernel, out_shape=(jax.ShapeDtypeStruct((TILE, D),...  5.3 us
    pallas_call x1, Pallas kernels, spread(): pl.pallas_call(spread_kernel, out_shape=(jax.ShapeDtypeStruct((TILE, D),...  4.58 us
    all_to_all x2, waiting for transfers between devices, swap(): lax.all_to_all(rows.reshape(PEERS, 8, HALF), ('enc', 'dom'), split_axis=0...  4.13 us
    ppermute x1, starting transfers between devices, local(): from_left = lax.ppermute(high, 'dom', rightward)  3.53 us
    pallas_call x1, Pallas kernels, prepare(): pl.pallas_call(prepare_kernel, out_shape=(jax.ShapeDtypeStruct((SLOTS, RO...  3.2 us
  transfers between devices with their start and end apart: 6, of which 5 were waited for; matrix products, arithmetic and copies ran while one was open for 0% of the time, Pallas kernels for 11%

profile of v7, /device:TPU:1, one launch (start us, length us, event | category | flops | bytes accessed | tf_op | source)
XLA Modules:
  0.0 88.3 jit_solution(3384122392477680050)
XLA Ops:
  0.6 24.4 %encode.1 = (bf16[1024,512]{1,0:T(8,128)(2,1)}, s32[8,256]{1,0:T(8,128)}) custom-call(s32[1]{0:T(128)} %bitcast.upper_ref, s32[1,192]{1,0:T(1,128)} %bitcast.9, s32[1,1024]{1,0:T(1,128)} %node_ref.1, bf16[1024,1024]{1,0:T(8,128)(2,1)} %states_hbm.1, bf16[1024,4096]{1,0:T(8,128)(2,1)} %expand_hbm.1, bf16[4096,1024]{1,0:T(8,128)(2,1)} %contract_hbm.1), custom_call_target="tpu_custom_call" | custom-call | flops 17179869184 | bytes 20971520 | tf_op jit(solution)/shard_map/encode/pallas_call | solution.py:235
  25.1 12.0 %all-to-all-start = ((bf16[128,8,512]{2,1,0:T(8,128)(2,1)}), bf16[128,8,512]{2,1,0:T(8,128)(2,1)}, u32[]{:S(2)}, u32[]{:S(2)}) async-start(bf16[128,8,512]{2,1,0:T(8,128)(2,1)} %bitcast.8), calls=%async_computation | async-start | bytes 2097152 | tf_op jit(solution)/shard_map/all_to_all | solution.py:547
  37.0 4.6 %spread.1 = (bf16[128,1024]{1,0:T(8,128)(2,1)}, bf16[128,1024]{1,0:T(8,128)(2,1)}, f32[256,1024]{1,0:T(8,128)}) custom-call(s32[1,2,3]{2,1,0:T(2,128)} %columns_ref.3, s32[1,2]{1,0:T(1,128)} %count_ref.3, bf16[1,2,3,128,128]{4,3,2,1,0:T(8,128)(2,1)} %values_ref.3, bf16[256,1024]{1,0:T(8,128)(2,1)} %cotangent_ref, bf16[1024,1024]{1,0:T(8,128)(2,1)} %weight_ref.3), custom_call_target="tpu_custom_call" | custom-call | flops 1000000000 | bytes 5242880 | tf_op jit(solution)/shard_map/spread/pallas_call | solution.py:295
  41.6 3.5 %collective-permute-start = (bf16[128,1024]{1,0:T(8,128)(2,1)}, bf16[128,1024]{1,0:T(8,128)(2,1)}, u32[]{:S(2)}, u32[]{:S(2)}) collective-permute-start(bf16[128,1024]{1,0:T(8,128)(2,1)} %get-tuple-element.23), channel_id=1, source_target_pairs={{0,1},{1,2},{2,3},{3,4},{4,5},{5,6},{6,7},{8,9},{9,10},{10,11},{11... | collective-permute-start | bytes 786440 | tf_op jit(solution)/shard_map/ppermute | solution.py:577
  45.2 2.1 %collective-permute-start.1 = (bf16[128,1024]{1,0:T(8,128)(2,1)}, bf16[128,1024]{1,0:T(8,128)(2,1)}, u32[]{:S(2)}, u32[]{:S(2)}) collective-permute-start(bf16[128,1024]{1,0:T(8,128)(2,1)} %get-tuple-element.24), channel_id=1, source_target_pairs={{1,0},{2,1},{3,2},{4,3},{5,4},{6,5},{7,6},{9,8},{10,9},{11,10},{12... | collective-permute-start | bytes 786440 | tf_op jit(solution)/shard_map/ppermute | solution.py:576
  47.3 3.2 %prepare.1 = (bf16[256,1024]{1,0:T(8,128)(2,1)}, bf16[512,256]{1,0:T(8,128)(2,1)}, bf16[256,512]{1,0:T(8,128)(2,1)}) custom-call(s32[1,2,3]{2,1,0:T(2,128)} %columns_ref.3, s32[1,2]{1,0:T(1,128)} %count_ref.3, bf16[1,2,3,128,128]{4,3,2,1,0:T(8,128)(2,1)} %values_ref.3, f32[256,1024]{1,0:T(8,128)} %get-tuple-element.21.order_ref.inner_hbm), custom_call_target="tpu_custom_call" | custom-call | flops 1000000000 | bytes 4194304 | tf_op jit(solution)/shard_map/prepare/pallas_call | solution.py:354
  50.5 0.1 collective-permute-done.left_hbm
  50.6 2.9 %collective-permute-done.1.right_hbm = bf16[128,1024]{1,0:T(8,128)(2,1)} collective-permute-done((bf16[128,1024]{1,0:T(8,128)(2,1)}, bf16[128,1024]{1,0:T(8,128)(2,1)}, u32[]{:S(2)}, u32[]{:S(2)}) %collective-permute-start.1) | collective-permute-done | bytes 262176 | tf_op jit(solution)/shard_map/ppermute | solution.py:576
  53.5 2.6 %all-to-all-done = bf16[128,8,512]{2,1,0:T(8,128)(2,1)} async-done(((bf16[128,8,512]{2,1,0:T(8,128)(2,1)}), bf16[128,8,512]{2,1,0:T(8,128)(2,1)}, u32[]{:S(2)}, u32[]{:S(2)}) %all-to-all-start) | async-done | bytes 1048608 | tf_op jit(solution)/shard_map/all_to_all | solution.py:547
  56.0 5.3 %middle.1 = (bf16[128,1024]{1,0:T(8,128)(2,1)}, bf16[128,1024]{1,0:T(8,128)(2,1)}, bf16[1024,512]{1,0:T(8,128)(2,1)}) custom-call(bf16[1024,512]{1,0:T(8,128)(2,1)} %bitcast.3.rows_hbm, bf16[256,1024]{1,0:T(8,128)(2,1)} %get-tuple-element.22.mix_hbm, bf16[1024,1024]{1,0:T(8,128)(2,1)} %weight_hbm.1, f32[256,1024]{1,0:T(8,128)} %get-tuple-element.21.order_ref.inner_hbm, ...), custom_call_target="tpu_custom_call" | custom-call | flops 3000000000 | bytes 8388608 | tf_op jit(solution)/shard_map/middle/pallas_call | solution.py:447
  61.3 0.0 copy-start
  61.3 6.2 %all-to-all-start.1 = ((bf16[128,8,512]{2,1,0:T(8,128)(2,1)}), bf16[128,8,512]{2,1,0:T(8,128)(2,1)S(1)}, u32[]{:S(2)}, u32[]{:S(2)}) async-start(bf16[128,8,512]{2,1,0:T(8,128)(2,1)} %bitcast.7), calls=%async_computation.1 | async-start | bytes 2097152 | tf_op jit(solution)/shard_map/all_to_all | solution.py:547
  67.5 3.0 %collective-permute-start.3 = (bf16[128,1024]{1,0:T(8,128)(2,1)}, bf16[128,1024]{1,0:T(8,128)(2,1)S(1)}, u32[]{:S(2)}, u32[]{:S(2)}) collective-permute-start(bf16[128,1024]{1,0:T(8,128)(2,1)} %get-tuple-element.26.top_hbm), channel_id=1, source_target_pairs={{1,0},{2,1},{3,2},{4,3},{5,4},{6,5},{7,6},{9,8},{10,9},{11,10},{12... | collective-permute-start | bytes 786440 | tf_op jit(solution)/shard_map/ppermute | solution.py:581
  70.5 2.6 %collective-permute-start.2 = (bf16[128,1024]{1,0:T(8,128)(2,1)}, bf16[128,1024]{1,0:T(8,128)(2,1)S(1)}, u32[]{:S(2)}, u32[]{:S(2)}) collective-permute-start(bf16[128,1024]{1,0:T(8,128)(2,1)} %get-tuple-element.27.bottom_hbm), channel_id=1, source_target_pairs={{0,1},{1,2},{2,3},{3,4},{4,5},{5,6},{6,7},{8,9},{9,10},{10,11},{11... | collective-permute-start | bytes 786440 | tf_op jit(solution)/shard_map/ppermute | solution.py:580
  73.1 0.0 copy-start.1
  73.1 0.9 %copy-done.1 = bf16[256,512]{1,0:T(8,128)(2,1)S(1)} copy-done((bf16[256,512]{1,0:T(8,128)(2,1)S(1)}, bf16[256,512]{1,0:T(8,128)(2,1)}, u32[]{:S(2)}) %copy-start.1) | copy-done | bytes 262168
  74.1 0.9 %copy-done.2 = bf16[128,1024]{1,0:T(8,128)(2,1)S(1)} copy-done((bf16[128,1024]{1,0:T(8,128)(2,1)S(1)}, bf16[128,1024]{1,0:T(8,128)(2,1)}, u32[]{:S(2)}) %copy-start.2) | copy-done | bytes 262168
  75.0 0.9 %copy-done.3 = bf16[128,1024]{1,0:T(8,128)(2,1)S(1)} copy-done((bf16[128,1024]{1,0:T(8,128)(2,1)S(1)}, bf16[128,1024]{1,0:T(8,128)(2,1)}, u32[]{:S(2)}) %copy-start.3) | copy-done | bytes 262168
  76.0 0.4 own_part.1
  76.4 7.2 %collective-permute-done.3.right_ref = bf16[128,1024]{1,0:T(8,128)(2,1)S(1)} collective-permute-done((bf16[128,1024]{1,0:T(8,128)(2,1)}, bf16[128,1024]{1,0:T(8,128)(2,1)S(1)}, u32[]{:S(2)}, u32[]{:S(2)}) %collective-permute-start.3) | collective-permute-done | bytes 262176 | tf_op jit(solution)/shard_map/ppermute | solution.py:581
  83.5 0.0 collective-permute-done.2.left_ref
  83.6 1.8 %finish.1 = bf16[256,1024]{1,0:T(8,128)(2,1)} custom-call(f32[256,1024]{1,0:T(8,128)S(1)} %get-tuple-element.29.part_ref, bf16[256,128]{1,0:T(8,128)(2,1)S(1)} %get-tuple-element.30.first_ref, bf16[256,128]{1,0:T(8,128)(2,1)S(1)} %get-tuple-element.31.last_ref, bf16[128,1024]{1,0:T(8,128)(2,1)S(1)} %collective-permute-done.2.left_ref, ...), custom_call_target="tpu_custom_call" | custom-call | flops 1000000000 | bytes 5242880 | tf_op jit(solution)/shard_map/finish/pallas_call | solution.py:509
  85.3 1.6 %all-to-all-done.1 = bf16[128,8,512]{2,1,0:T(8,128)(2,1)S(1)} async-done(((bf16[128,8,512]{2,1,0:T(8,128)(2,1)}), bf16[128,8,512]{2,1,0:T(8,128)(2,1)S(1)}, u32[]{:S(2)}, u32[]{:S(2)}) %all-to-all-start.1) | async-done | bytes 1048608 | tf_op jit(solution)/shard_map/all_to_all | solution.py:547
  86.9 1.4 %gather.1 = bf16[192,1024]{1,0:T(8,128)(2,1)} custom-call(s32[8,256]{1,0:T(8,128)S(1)} %copy-done.4, bf16[1024,512]{1,0:T(8,128)(2,1)S(1)} %bitcast.6), custom_call_target="tpu_custom_call" | custom-call | flops 400000000 | bytes 2097152 | tf_op jit(solution)/shard_map/gather/pallas_call | solution.py:534
  (5 shorter events, 0.0 us)
Async XLA Ops:
  25.1 31.0 %all-to-all-start = ((bf16[128,8,512]{2,1,0:T(8,128)(2,1)}), bf16[128,8,512]{2,1,0:T(8,128)(2,1)}, u32[]{:S(2)}, u32[]{:S(2)}) async-start(bf16[128,8,512]{2,1,0:T(8,128)(2,1)} %bitcast.8), calls=%async_computation | async-start | bytes 2097152 | tf_op jit(solution)/shard_map/all_to_all | solution.py:547
  41.6 9.0 %collective-permute-start = (bf16[128,1024]{1,0:T(8,128)(2,1)}, bf16[128,1024]{1,0:T(8,128)(2,1)}, u32[]{:S(2)}, u32[]{:S(2)}) collective-permute-start(bf16[128,1024]{1,0:T(8,128)(2,1)} %get-tuple-element.23), channel_id=1, source_target_pairs={{0,1},{1,2},{2,3},{3,4},{4,5},{5,6},{6,7},{8,9},{9,10},{10,11},{11... | collective-permute-start | bytes 786440 | tf_op jit(solution)/shard_map/ppermute | solution.py:577
  45.2 8.3 %collective-permute-start.1 = (bf16[128,1024]{1,0:T(8,128)(2,1)}, bf16[128,1024]{1,0:T(8,128)(2,1)}, u32[]{:S(2)}, u32[]{:S(2)}) collective-permute-start(bf16[128,1024]{1,0:T(8,128)(2,1)} %get-tuple-element.24), channel_id=1, source_target_pairs={{1,0},{2,1},{3,2},{4,3},{5,4},{6,5},{7,6},{9,8},{10,9},{11,10},{12... | collective-permute-start | bytes 786440 | tf_op jit(solution)/shard_map/ppermute | solution.py:576
  61.3 22.2 %copy-start = (bf16[1024,1024]{1,0:T(8,128)(2,1)S(1)}, bf16[1024,1024]{1,0:T(8,128)(2,1)}, u32[]{:S(2)}) copy-start(bf16[1024,1024]{1,0:T(8,128)(2,1)} %weight_ref.3) | copy-start | bytes 6291460
  61.3 25.5 %all-to-all-start.1 = ((bf16[128,8,512]{2,1,0:T(8,128)(2,1)}), bf16[128,8,512]{2,1,0:T(8,128)(2,1)S(1)}, u32[]{:S(2)}, u32[]{:S(2)}) async-start(bf16[128,8,512]{2,1,0:T(8,128)(2,1)} %bitcast.7), calls=%async_computation.1 | async-start | bytes 2097152 | tf_op jit(solution)/shard_map/all_to_all | solution.py:547
  67.5 16.0 %collective-permute-start.3 = (bf16[128,1024]{1,0:T(8,128)(2,1)}, bf16[128,1024]{1,0:T(8,128)(2,1)S(1)}, u32[]{:S(2)}, u32[]{:S(2)}) collective-permute-start(bf16[128,1024]{1,0:T(8,128)(2,1)} %get-tuple-element.26.top_hbm), channel_id=1, source_target_pairs={{1,0},{2,1},{3,2},{4,3},{5,4},{6,5},{7,6},{9,8},{10,9},{11,10},{12... | collective-permute-start | bytes 786440 | tf_op jit(solution)/shard_map/ppermute | solution.py:581
  70.5 13.0 %collective-permute-start.2 = (bf16[128,1024]{1,0:T(8,128)(2,1)}, bf16[128,1024]{1,0:T(8,128)(2,1)S(1)}, u32[]{:S(2)}, u32[]{:S(2)}) collective-permute-start(bf16[128,1024]{1,0:T(8,128)(2,1)} %get-tuple-element.27.bottom_hbm), channel_id=1, source_target_pairs={{0,1},{1,2},{2,3},{3,4},{4,5},{5,6},{6,7},{8,9},{9,10},{10,11},{11... | collective-permute-start | bytes 786440 | tf_op jit(solution)/shard_map/ppermute | solution.py:580
  73.1 1.0 %copy-start.1 = (bf16[256,512]{1,0:T(8,128)(2,1)S(1)}, bf16[256,512]{1,0:T(8,128)(2,1)}, u32[]{:S(2)}) copy-start(bf16[256,512]{1,0:T(8,128)(2,1)} %get-tuple-element.28.band_hbm) | copy-start | bytes 786436
  74.1 0.9 %copy-start.2 = (bf16[128,1024]{1,0:T(8,128)(2,1)S(1)}, bf16[128,1024]{1,0:T(8,128)(2,1)}, u32[]{:S(2)}) copy-start(bf16[128,1024]{1,0:T(8,128)(2,1)} %get-tuple-element.27.bottom_hbm) | copy-start | bytes 786436
  75.0 0.9 %copy-start.3 = (bf16[128,1024]{1,0:T(8,128)(2,1)S(1)}, bf16[128,1024]{1,0:T(8,128)(2,1)}, u32[]{:S(2)}) copy-start(bf16[128,1024]{1,0:T(8,128)(2,1)} %get-tuple-element.26.top_hbm) | copy-start | bytes 786436
  83.6 3.3 %copy-start.4 = (s32[8,256]{1,0:T(8,128)S(1)}, s32[8,256]{1,0:T(8,128)}, u32[]{:S(2)}) copy-start(s32[8,256]{1,0:T(8,128)} %get-tuple-element.32.target_ref) | copy-start | bytes 24580
